TPU v7x, 512 devices: a whole 4x4x16 slice. The times are simulated.
512 devices in a mesh: gx: 32 (over y, x, z_hi), gy: 16 (over z_lo, core).
Axes of the slice: x: 4, y: 4, z: 16 (z_hi: 2, z_lo: 8; z = z_hi * 8 + z_lo), core: 2. Of those that a mesh axis runs over, the one named last changes fastest.
Arguments:
- points: bfloat16 [131072, 2048], P(('gx', 'gy')), may hold values from -8 to 8
- residual: float32 [131072, 1000], P(('gx', 'gy')), may hold values from -6 to 6
- block_ids: int32 [512], replicated, may hold values from 0 to 131071, as said below
Outputs:
- updated: float32 [131072, 1000], P(('gx', 'gy'))
- block_step: float32 [512, 1000], P('gy')
Inputs may be any that keep to these rules, and one draw needn't show every extreme that they name: `block_ids`: the 512 indices are distinct. The 256 consecutive indices of one device hold at most 2 of them, and some device holds exactly 2. The 16 devices of one gx index, 4096 consecutive indices, hold at most 24, and some such group holds exactly 24.
All inputs are finite; a program needn't handle non-finite values.
Results may differ from a plain program's by a relative error of at most 0.0003.
Values may be sent and summed in bfloat16 or wider, within the bound.
No kernel may reach another device: no remote copies, remote signals or barrier semaphores. Data moves between devices by JAX's collectives and lax.ppermute only.
A program may use at most 64 MiB of HBM per device.

v0:
```python
import jax
import jax.numpy as jnp
from jax import lax
from jax.sharding import PartitionSpec as P

GAMMA = 0.125
RIDGE = 0.5


def kernel(left, right):
    left_sq = jnp.sum(jnp.square(left.astype(jnp.float32)), axis=1)
    right_sq = jnp.sum(jnp.square(right.astype(jnp.float32)), axis=1)
    cross = lax.dot_general(
        left, right, (((1,), (1,)), ((), ())), preferred_element_type=jnp.float32
    )
    return jnp.exp(-GAMMA * (left_sq[:, None] + right_sq[None, :] - 2.0 * cross))


def earlier_count(labels, before):
    same_label = labels[:, None] == labels[None, :]
    return jnp.sum(jnp.where(same_label & before, 1, 0), axis=0).astype(jnp.int32)


def on_device(points, residual, block_ids):
    point_count = points.shape[0]
    width_gx = lax.axis_size("gx")
    width_gy = lax.axis_size("gy")
    devices = width_gx * width_gy
    block_len = block_ids.shape[0]
    capacity = 2 * block_len // devices
    my_flat = lax.axis_index("gx") * width_gy + lax.axis_index("gy")
    owner_dev = block_ids // point_count
    local_row = block_ids - owner_dev * point_count
    positions = jnp.arange(block_len, dtype=jnp.int32)
    before = positions[:, None] < positions[None, :]
    slot_rank = earlier_count(owner_dev, before)
    mine = owner_dev == my_flat
    slot_numbers = jnp.arange(capacity, dtype=jnp.int32)
    chosen = mine[None, :] & (slot_rank[None, :] == slot_numbers[:, None])
    filled = jnp.any(chosen, axis=1)
    source_row = jnp.sum(jnp.where(chosen, local_row[None, :], 0), axis=1)
    packed_points = jnp.where(
        filled[:, None], jnp.take(points, source_row, axis=0), jnp.zeros((), jnp.bfloat16)
    )
    packed_resid = jnp.where(
        filled[:, None], jnp.take(residual, source_row, axis=0), jnp.zeros((), jnp.float32)
    )
    all_points = lax.all_gather(packed_points, ("gx", "gy"), axis=0, tiled=True)
    all_resid = lax.all_gather(packed_resid, ("gx", "gy"), axis=0, tiled=True)
    gather_index = owner_dev * capacity + slot_rank
    block_points = jnp.take(all_points, gather_index, axis=0)
    block_resid = jnp.take(all_resid, gather_index, axis=0)
    gram = kernel(block_points, block_points) + RIDGE * jnp.eye(block_len, dtype=jnp.float32)
    factor = jnp.linalg.cholesky(gram)
    block_step = jax.scipy.linalg.cho_solve((factor, True), block_resid)
    updated = residual - jnp.dot(
        kernel(points, block_points), block_step, precision=lax.Precision.HIGHEST
    )
    target_row = jnp.where(mine, local_row, point_count)
    updated = updated.at[target_row].add(-RIDGE * block_step, mode="drop")
    share = block_len // width_gy
    step_share = lax.dynamic_slice_in_dim(block_step, lax.axis_index("gy") * share, share, 0)
    return (updated, step_share)


def solution(mesh):
    return jax.shard_map(
        on_device,
        mesh=mesh,
        in_specs=(P(("gx", "gy"), None), P(("gx", "gy"), None), P()),
        out_specs=(P(("gx", "gy"), None), P("gy", None)),
        check_vma=False,
    )
```

profile of v0, /device:TPU:1, one launch (start us, length us, event | category | flops | bytes accessed | tf_op | source)
XLA Modules:
  0.0 620.4 jit_solution(7608415455256286226)
XLA Ops:
  13.0 203.8 %all-gather.7.cloned.1.call-done = f32[512,2,1000]{2,1,0:T(2,128)} async-done(((f32[1,2,1000]{2,1,0:T(2,128)}), f32[512,2,1000]{2,1,0:T(2,128)}) %all-gather.7.cloned.1.call-update) | async-done | bytes 4096016 | tf_op jit(solution)/shard_map/all_gather | solution.py:49
  216.7 6.1 reshape.152
  222.8 5.0 gather_fusion.3
  227.9 1.9 copy.31
  229.7 3.2 broadcast_select_fusion.1
  232.9 182.4 %all-gather.5.cloned.1.call-done = bf16[512,2,2048]{2,1,0:T(2,128)(2,1)} async-done(((bf16[1,2,2048]{2,1,0:T(2,128)(2,1)}), bf16[512,2,2048]{2,1,0:T(2,128)(2,1)}) %all-gather.5.cloned.1.call-update) | async-done | bytes 4194320 | tf_op jit(solution)/shard_map/all_gather | solution.py:48
  415.3 7.2 %reshape.150 = bf16[1024,2048]{1,0:T(8,128)(2,1)} reshape(bf16[512,2,2048]{2,1,0:T(2,128)(2,1)} %all-gather.5.cloned.1.call-done) | data formatting | bytes 8388608
  422.5 7.3 %gather_fusion.1 = bf16[512,2048]{1,0:T(8,128)(2,1)S(1)} fusion(bf16[1024,2048]{1,0:T(8,128)(2,1)} %reshape.150, s32[1024]{0:T(1024)S(1)} %pad_clamp_fusion), kind=kCustom, calls=%fused_computation.1 | custom fusion | bytes 4196352 | tf_op jit(solution)/shard_map/jit(_take)/gather | solution.py:51
  430.5 3.0 fusion.36
  433.5 1.6 fusion.15
  435.1 1.6 copy.28
  437.1 1.6 fusion.26
  439.7 11.7 %cholesky.103 = f32[128,128]{1,0:T(8,128)S(1)} custom-call(f32[128,128]{1,0:T(8,128)S(1)} %cholesky.263), custom_call_target="Cholesky" | custom-call | tf_op jit(solution)/shard_map/jit(cholesky)/cholesky | solution.py:54
  451.5 9.8 %custom-call.34 = f32[1,128,128]{1,2,0:T(8,128)S(1)} custom-call(f32[1,128,128]{2,1,0:T(8,128)S(1)} %get-tuple-element.45), custom_call_target="InvertDiagBlocksLowerTriangular" | custom-call | tf_op jit(solution)/shard_map/jit(cholesky)/cholesky | solution.py:54
  463.9 12.1 %cholesky.215 = f32[128,128]{1,0:T(8,128)S(1)} custom-call(f32[128,128]{1,0:T(8,128)S(1)} %cholesky.267), custom_call_target="Cholesky" | custom-call | tf_op jit(solution)/shard_map/jit(cholesky)/cholesky | solution.py:54
  476.1 9.8 %custom-call.35 = f32[1,128,128]{1,2,0:T(8,128)S(1)} custom-call(f32[1,128,128]{2,1,0:T(8,128)S(1)} %get-tuple-element.42), custom_call_target="InvertDiagBlocksLowerTriangular" | custom-call | tf_op jit(solution)/shard_map/jit(cholesky)/cholesky | solution.py:54
  487.5 11.7 %cholesky.236 = f32[128,128]{1,0:T(8,128)S(1)} custom-call(f32[128,128]{1,0:T(8,128)S(1)} %cholesky.272), custom_call_target="Cholesky" | custom-call | tf_op jit(solution)/shard_map/jit(cholesky)/cholesky | solution.py:54
  499.9 9.8 %custom-call.36 = f32[1,128,128]{1,2,0:T(8,128)S(1)} custom-call(f32[1,128,128]{2,1,0:T(8,128)S(1)} %get-tuple-element.39), custom_call_target="InvertDiagBlocksLowerTriangular" | custom-call | tf_op jit(solution)/shard_map/jit(cholesky)/cholesky | solution.py:54
  511.1 11.9 %cholesky.253 = f32[128,128]{1,0:T(8,128)S(1)} custom-call(f32[128,128]{1,0:T(8,128)S(1)} %convolution_subtract_fusion.7), custom_call_target="Cholesky" | custom-call | tf_op jit(solution)/shard_map/jit(cholesky)/cholesky | solution.py:54
  528.1 13.9 %while.1 = (s32[]{:T(128)}, f32[512,512]{1,0:T(8,128)}, s32[4,2]{0,1:T(2,128)S(1)}, f32[4,128,128]{2,1,0:T(8,128)}, s32[]{:T(128)}) while((s32[]{:T(128)}, f32[512,512]{1,0:T(8,128)}, s32[4,2]{0,1:T(2,128)S(1)}, f32[4,128,128]{2,1,0:T(8,128)}, s32[]{:T(128)}) %tuple.42), condition=%wide.while_cond, body=%wide.while_body.sunk | while | flops 2 | bytes 132205 | solution.py:55
  528.7 2.9 bitcast_dynamic-update-slice_fusion.2
  532.2 2.9 bitcast_dynamic-update-slice_fusion.2
  535.7 2.9 bitcast_dynamic-update-slice_fusion.2
  539.2 2.8 bitcast_dynamic-update-slice_fusion.2
  542.0 40.2 %custom-call.37 = f32[4,128,128]{1,2,0:T(8,128)S(1)} custom-call(f32[4,128,128]{2,1,0:T(8,128)} %get-tuple-element.9), custom_call_target="InvertDiagBlocksLowerTriangular" | custom-call | tf_op jit(solution)/shard_map/jit(_cho_solve)/triangular_solve | solution.py:55
  583.2 1.8 convolution_subtract_fusion.4
  587.9 1.8 fusion.19
  595.8 1.8 fusion.16
  598.6 2.2 pad_maximum_fusion
  600.8 1.9 convolution_subtract_fusion
  605.1 1.9 copy.33
  607.0 5.1 scatter_fusion
  (79 shorter events, 33.6 us)
Async XLA Ops:
  7.2 4.2 copy-start.4
  7.2 209.6 %all-gather.7.cloned.1.call-start = ((), (), s32[]{:S(2)}) async-start(), calls=%async_computation.1 | async-start | bytes 4202496 | tf_op jit(solution)/shard_map/all_gather | solution.py:49
  11.3 404.0 %all-gather.5.cloned.1.call-start = ((), (), s32[]{:S(2)}) async-start(), calls=%async_computation | async-start | bytes 4202496 | tf_op jit(solution)/shard_map/all_gather | solution.py:48
  435.1 1.7 copy-start.5
  438.7 1.0 copy-start.3
  487.5 94.8 %copy-start = (f32[512,1000]{0,1:T(8,128)S(1)}, f32[512,1000]{0,1:T(8,128)}, u32[]{:S(2)}) copy-start(f32[512,1000]{0,1:T(8,128)} %broadcast_select_fusion.1) | copy-start | bytes 6144004
  542.0 44.0 %copy-start.1 = (f32[512,512]{1,0:T(8,128)S(1)}, f32[512,512]{1,0:T(8,128)}, u32[]{:S(2)}) copy-start(f32[512,512]{1,0:T(8,128)} %get-tuple-element.99) | copy-start | bytes 3145732
  598.6 2.2 copy-start.2
  598.6 2.2 copy-start.6
Sparse Core Ops, SparseCore 0:
  13.2 203.5 all-gather.6
  221.9 193.3 all-gather.4
where the time goes:
time: 626 us; the launch traced here: 620 us
  waiting for transfers between devices  386 us (62%)
  other arithmetic  136 us (22%)
  local copies, waits for them, and re-layouts  52.8 us (8%)
  matrix products  28.1 us (4%)
  between operations  17.2 us (3%)
    all_gather x1, waiting for transfers between devices, on_device(): all_resid = lax.all_gather(packed_resid, ('gx', 'gy'), axis=0, tiled=True)  204 us
    all_gather x1, waiting for transfers between devices, on_device(): all_points = lax.all_gather(packed_points, ('gx', 'gy'), axis=0, tiled=True)  182 us
    another operation x14, other arithmetic, on_device(): factor = jnp.linalg.cholesky(gram)  79 us
    another operation x4, other arithmetic, on_device(): block_step = jax.scipy.linalg.cho_solve((factor, True), block_resid)  43.5 us
    unnamed x19, local copies, waits for them, and re-layouts  18 us
    another operation x14, matrix products, on_device(): block_step = jax.scipy.linalg.cho_solve((factor, True), block_resid)  16.2 us
    another operation x12, local copies, waits for them, and re-layouts  13.9 us
  transfers between devices with their start and end apart: 2, of which 2 were waited for; matrix products, arithmetic and copies ran while one was open for 3% of the time, Pallas kernels for 0%

commit v1 on v0

v1 whole, which is shorter than its diff:
```python
import functools

import jax
import jax.numpy as jnp
from jax import lax
from jax.experimental import pallas as pl
from jax.experimental.pallas import tpu as pltpu
from jax.sharding import Mesh
from jax.sharding import PartitionSpec as P

F32=jnp.float32; BF=jnp.bfloat16
NN=(((1,),(0,)),((),())); NT=(((1,),(1,)),((),()))
def dot(a,b,dn=NN,prec=None):
    return lax.dot_general(a,b,dn,preferred_element_type=F32,precision=prec)
def split(v):
    hi=v.astype(BF); return hi,(v-hi.astype(F32)).astype(BF)
def mm3(a,b):
    ah,al=a; bh,bl=b
    return dot(ah,bh)+(dot(ah,bl)+dot(al,bh))
HI=lax.Precision.HIGHEST
def factor_body(info, idrow, own_ref, oth_ref, pts_ref, w_ref, g_ref, gh_ref, gl_ref, x_ref, m_ref, *, half, share):
    n=own_ref.shape[0]; rows=pts_ref.shape[0]
    core=info[0]; first=info[1]; share0=info[2]
    own=own_ref[...]; oth=oth_ref[...]
    cross=dot(own,own,NT)+dot(oth,oth,NT)
    ri=lax.broadcasted_iota(jnp.int32,(n,n),0); ci=lax.broadcasted_iota(jnp.int32,(n,n),1)
    eye=ri==ci
    diag=jnp.where(eye,cross,0.0)
    sq_row=jnp.sum(diag,axis=0,keepdims=True); sq_col=jnp.sum(diag,axis=1,keepdims=True)
    gram=jnp.exp(-0.125*(sq_col+sq_row-2.0*cross))+jnp.where(eye,0.5,0.0)
    g_ref[...]=gram
    gh,gl=split(gram); gh_ref[...]=gh; gl_ref[...]=gl
    p_own=pts_ref[:,pl.ds(pl.multiple_of(core*half,half),half)]
    p_oth=pts_ref[:,pl.ds(pl.multiple_of((1-core)*half,half),half)]
    pf=pts_ref[...].astype(F32)
    psq=jnp.sum(pf*pf,axis=1,keepdims=True)
    pc=dot(p_own,own,NT)+dot(p_oth,oth,NT)
    pk=jnp.exp(-0.125*(psq+sq_row-2.0*pc))
    pid=first+lax.broadcasted_iota(jnp.int32,(rows,n),0)
    m_ref[pl.ds(0,rows),:]=pk+jnp.where(pid==idrow[...],0.5,0.0)
    sid=share0+lax.broadcasted_iota(jnp.int32,(share,n),0)
    m_ref[pl.ds(rows,share),:]=jnp.where(sid==lax.broadcasted_iota(jnp.int32,(share,n),1),1.0,0.0)
    lo=0.499; hi=jnp.max(jnp.sum(gram,axis=0,keepdims=True))*1.001
    s=2.0/(lo+hi)
    x_ref[...]=jnp.where(eye,2.0*s,0.0)-(s*s)*gram
    d=(hi-lo)/(hi+lo)
    def cond(resid): return resid>1e-4
    def body(resid):
        s=2.0/(2.0-resid)
        x=x_ref[...]*s
        xs=split(x)
        t=mm3((gh_ref[...],gl_ref[...]),xs)
        r=jnp.where(eye,1.0,0.0)-t
        x_ref[...]=x+mm3(xs,split(r))
        dn=resid/(2.0-resid)
        return dn*dn
    lax.while_loop(cond,body,d*d)
    m=m_ref[...]
    xs=split(x_ref[...])
    w=mm3(split(m),xs)
    e=m-dot(w,g_ref[...],NN,HI)
    w_ref[...]=w+mm3(split(e),xs)
def factor(info,ids,own,oth,pts,share):
    n=own.shape[0]; rows=pts.shape[0]
    V=pl.BlockSpec(memory_space=pltpu.VMEM)
    return pl.pallas_call(functools.partial(factor_body,half=own.shape[1],share=share),
        out_shape=jax.ShapeDtypeStruct((rows+share,n),F32),
        in_specs=[pl.BlockSpec(memory_space=pltpu.SMEM),V,V,V,V],out_specs=V,
        scratch_shapes=[pltpu.VMEM((n,n),F32),pltpu.VMEM((n,n),BF),pltpu.VMEM((n,n),BF),pltpu.VMEM((n,n),F32),pltpu.VMEM((rows+share,n),F32)],
        compiler_params=pltpu.CompilerParams(vmem_limit_bytes=48*1024*1024),
    )(info,ids.reshape(1,n),own,oth,pts)


PLANE = ("y", "x")
COLUMN = ("zh", "zl", "c")
EVERY = PLANE + COLUMN
CAP = 2
COL_CAP = 48
CLASS_PAD = 1024


def three_parts(value):
    hi = lax.reduce_precision(value, 8, 7)
    mid = lax.reduce_precision(value - hi, 8, 7)
    low = lax.reduce_precision((value - hi) - mid, 8, 7)
    return hi.astype(BF), mid.astype(BF), low.astype(BF)


def on_device(points, residual, block_ids):
    rows, feats = points.shape
    classes = residual.shape[1]
    block = block_ids.shape[0]
    n_plane = lax.axis_size(PLANE)
    n_col = lax.axis_size(COLUMN)
    plane = lax.axis_index(PLANE)
    place = lax.axis_index(COLUMN)
    core = lax.axis_index("c")
    me = plane * n_col + place
    half = feats // 2
    chalf = CLASS_PAD // 2

    owner = block_ids // rows
    column = block_ids // (rows * n_col)
    less = block_ids[:, None] > block_ids[None, :]
    slot = jnp.sum(jnp.where(less & (owner[:, None] == owner[None, :]), 1, 0), axis=1).astype(jnp.int32)
    rank = jnp.sum(jnp.where(less & (column[:, None] == column[None, :]), 1, 0), axis=1).astype(jnp.int32)
    mine = owner == me
    picked_points, picked_resid = [], []
    for k in range(CAP):
        row = jnp.sum(jnp.where(mine & (slot == k), block_ids - me * rows, 0)).astype(jnp.int32)
        picked_points.append(lax.dynamic_slice(points, (row, 0), (1, feats)))
        picked_resid.append(lax.dynamic_slice(residual, (row, 0), (1, classes)))
    my_points = jnp.concatenate(picked_points, axis=0)
    my_resid = jnp.pad(jnp.concatenate(picked_resid, axis=0), ((0, 0), (0, CLASS_PAD - classes)))
    hi, mid, low = three_parts(my_resid)
    parts = [my_points.reshape(CAP, 2, half)] + [v.reshape(CAP, 2, chalf) for v in (hi, mid, low)]
    packed = jnp.concatenate(parts, axis=2).transpose(1, 0, 2)
    width = packed.shape[2]
    packed = jnp.broadcast_to(packed[None], (n_col // 2, 2, CAP, width)).reshape(n_col, CAP, width)
    column_rows = lax.all_to_all(packed, COLUMN, 0, 0, tiled=True).reshape(n_col * CAP, width)

    in_column = column == plane
    sel_rank = in_column[None, :] & (rank[None, :] == jnp.arange(COL_CAP, dtype=jnp.int32)[:, None])
    col_slot = (owner % n_col) * CAP + slot
    sel_slot = col_slot[:, None] == jnp.arange(n_col * CAP, dtype=jnp.int32)[None, :]
    pick = dot(sel_rank.astype(BF), sel_slot.astype(BF)).astype(BF)
    compact = dot(pick, column_rows).astype(BF)
    col_points = compact[:, :half]
    r_hi, r_mid, r_low = [compact[:, half + k * chalf : half + (k + 1) * chalf].astype(F32) for k in range(3)]
    col_resid = (r_hi + r_mid) + r_low

    resid_own = lax.all_gather(col_resid, PLANE, axis=0, tiled=True)
    spread = jnp.broadcast_to(col_points[None], (n_plane, COL_CAP, half))
    plane_rows = lax.all_to_all(spread, PLANE, 0, 0, tiled=True).reshape(n_plane * COL_CAP, half)
    place_of = (column * COL_CAP + rank)[:, None] == jnp.arange(n_plane * COL_CAP, dtype=jnp.int32)[None, :]
    place_of = place_of.astype(BF)
    own = dot(place_of, plane_rows).astype(BF)
    other = lax.ppermute(own, "c", [(0, 1), (1, 0)])

    share = block // (lax.axis_size("zl") * lax.axis_size("c"))
    share_at = (place % (lax.axis_size("zl") * lax.axis_size("c"))) * share
    info = jnp.stack([core, me * rows, share_at]).astype(jnp.int32)
    weights = factor(info, block_ids, own, other, points, share)
    w_hi, w_mid, w_low = three_parts(weights)
    spread_w = (dot(w_hi, place_of) + dot(w_mid, place_of)) + dot(w_low, place_of)

    resid_other = lax.ppermute(resid_own, "c", [(0, 1), (1, 0)])
    first = core == 0
    resid = jnp.concatenate([jnp.where(first, resid_own, resid_other), jnp.where(first, resid_other, resid_own)], axis=1)
    change = dot(spread_w, resid[:, :classes], prec=HI)
    return (residual - change[:rows], change[rows:])


def solution(mesh):
    fine = Mesh(mesh.devices.reshape(4, 4, 2, 8, 2), EVERY)
    return jax.shard_map(
        on_device,
        mesh=fine,
        in_specs=(P(EVERY, None), P(EVERY, None), P()),
        out_specs=(P(EVERY, None), P(("zl", "c"), None)),
        check_vma=False,
    )
```

time: 626 us -> 154 us (0.25)
  waiting for transfers between devices: 386 us -> 40.2 us
  other arithmetic: 136 us -> 6.23 us
  local copies, waits for them, and re-layouts: 52.8 us -> 7.98 us
  blocking collectives: 0 us -> 41.6 us
  matrix products: 28.1 us -> 7.94 us
  Pallas kernels: 0 us -> 17 us
  starting transfers between devices: 0.08 us -> 14.1 us
    all_gather x2 -> x1, waiting for transfers between devices: 386 us -> 14.9 us  [on_device(): resid_own = lax.all_gather(col_resid, PLANE, axis=0, tiled=True)]
    another operation x18 -> x1, other arithmetic: 123 us -> 0.08 us  [on_device(): info = jnp.stack([core, me * rows, share_at]).astype(jnp.int32)]
    all_to_all x0 -> x1, blocking collectives: none -> 41.6 us  [on_device(): lax.all_to_all(packed, COLUMN, 0, 0, tiled=True).reshape(n_col * CAP, width)]
    all_to_all x0 -> x1, waiting for transfers between devices: none -> 25.2 us  [on_device(): lax.all_to_all(spread, PLANE, 0, 0, tiled=True)]
    another operation x20 -> x0, matrix products: 21.7 us -> none  [the longest x14 16.2 us: on_device(): block_step = jax.scipy.linalg.cho_solve((factor, True), block_resid)]
    pallas_call x0 -> x1, Pallas kernels: none -> 17 us  [factor(): pl.pallas_call(functools.partial(factor_body, half=own.shape[1], share=sh...]
    gather x5 -> x0, local copies, waits for them, and re-layouts: 15.3 us -> none  [the longest x1 7.31 us: on_device(): block_points = jnp.take(all_points, gather_index, axis=0)]
    another operation x17 -> x0, local copies, waits for them, and re-layouts: 14 us -> none
  transfers between devices with their start and end apart: 2 -> 4, of which waited for: 2 -> 2; matrix products, arithmetic and copies ran while one was open for 3% -> 4% of each run, Pallas kernels for 0% -> 11%
where the time goes in v1:
time: 154 us; the launch traced here: 153 us
  blocking collectives  41.6 us (27%)
  waiting for transfers between devices  40.2 us (26%)
  between operations  18.1 us (12%)
  Pallas kernels  17 us (11%)
  starting transfers between devices  14.1 us (9%)
  local copies, waits for them, and re-layouts  7.98 us (5%)
  matrix products  7.94 us (5%)
  other arithmetic  6.23 us (4%)
    all_to_all x1, blocking collectives, on_device(): lax.all_to_all(packed, COLUMN, 0, 0, tiled=True).reshape(n_col * CAP, width)  41.6 us
    all_to_all x1, waiting for transfers between devices, on_device(): lax.all_to_all(spread, PLANE, 0, 0, tiled=True)  25.2 us
    pallas_call x1, Pallas kernels, factor(): pl.pallas_call(functools.partial(factor_body, half=own.shape[1], share=sh...  17 us
    all_gather x1, waiting for transfers between devices, on_device(): resid_own = lax.all_gather(col_resid, PLANE, axis=0, tiled=True)  14.9 us
    dot_general x6, matrix products, dot(): return lax.dot_general(a, b, dn, preferred_element_type=F32, precision=prec)  7.94 us
    all_to_all x1, starting transfers between devices, on_device(): lax.all_to_all(spread, PLANE, 0, 0, tiled=True)  6.69 us
    unnamed x14, local copies, waits for them, and re-layouts  4.79 us
    ppermute x1, starting transfers between devices, on_device(): other = lax.ppermute(own, 'c', [(0, 1), (1, 0)])  3.74 us
  transfers between devices with their start and end apart: 4, of which 2 were waited for; matrix products, arithmetic and copies ran while one was open for 4% of the time, Pallas kernels for 11%

profile of v1, /device:TPU:1, one launch (start us, length us, event | category | flops | bytes accessed | tf_op | source)
XLA Modules:
  0.0 153.2 jit_solution(364749898319634948)
XLA Ops:
  7.2 0.0 all-gather.2.cloned.1.call-start
  7.2 0.7 broadcast_compare_fusion.1
  7.9 1.4 select_reduce_fusion
  9.4 1.4 select_reduce_fusion.3
  14.6 0.8 constant_dynamic-slice_fusion.3
  15.4 1.5 %copy.19 = f32[256,1000]{1,0:T(8,128)S(1)} copy(f32[256,1000]{0,1:T(8,128)} %param.4) | data formatting | bytes 2048000 | tf_op args[1]
  17.1 0.2 broadcast_in_dim.19
  17.3 41.6 %all_to_all.10 = bf16[32,2,2560]{2,1,0:T(2,128)(2,1)S(1)} all-to-all(bf16[32,2,2560]{2,1,0:T(2,128)(2,1)S(1)} %bitcast.13), channel_id=1, replica_groups=mesh['y'=4,'x'=4,'zh'=2,'zl'=8,'c'=2] {'zh','zl','c'}, dimensions={0} | all-to-all | bytes 655360 | tf_op jit(solution)/shard_map/all_to_all | solution.py:120
  59.0 0.1 reshape.46
  59.1 0.4 convolution_convert_fusion
  59.5 0.7 convert_add_fusion
  60.2 0.0 all-gather.2.cloned.1.call-update
  60.2 1.3 broadcast_in_dim.20
  61.6 6.7 %all-to-all-start.1 = ((bf16[16,48,1024]{2,1,0:T(8,128)(2,1)}), bf16[16,48,1024]{2,1,0:T(8,128)(2,1)S(1)}, u32[]{:S(2)}, u32[]{:S(2)}) async-start(bf16[16,48,1024]{2,1,0:T(8,128)(2,1)} %broadcast_in_dim.20), calls=%async_computation.1 | async-start | bytes 3145728 | tf_op jit(solution)/shard_map/all_to_all | solution.py:134
  68.3 25.2 %all-to-all-done.1 = bf16[16,48,1024]{2,1,0:T(8,128)(2,1)S(1)} async-done(((bf16[16,48,1024]{2,1,0:T(8,128)(2,1)}), bf16[16,48,1024]{2,1,0:T(8,128)(2,1)S(1)}, u32[]{:S(2)}, u32[]{:S(2)}) %all-to-all-start.1) | async-done | bytes 1572896 | tf_op jit(solution)/shard_map/all_to_all | solution.py:134
  93.5 1.1 copy-done.4
  94.7 2.5 %fusion.6.own_ref = bf16[512,1024]{1,0:T(8,128)(2,1)S(1)} fusion(bf16[768,1024]{1,0:T(8,128)(2,1)} %bitcast.12, s32[512]{0:T(512)S(1)} %multiply_add_fusion), kind=kOutput, calls=%fused_computation.9 | convolution fusion | flops 806223872 | bytes 2623488 | tf_op jit(solution)/shard_map/dot_general | solution.py:14
  97.2 3.7 %collective-permute-start = (bf16[512,1024]{1,0:T(8,128)(2,1)S(1)}, bf16[512,1024]{1,0:T(8,128)(2,1)S(1)}, u32[]{:S(2)}, u32[]{:S(2)}) collective-permute-start(bf16[512,1024]{1,0:T(8,128)(2,1)S(1)} %fusion.6.own_ref), channel_id=1, source_target_pairs={{0,1},{1,0},{2,3},{3,2},{4,5},{5,4},{6,7},{7,6},{8,9},{9,8},{10,11... | collective-permute-start | bytes 3145736 | tf_op jit(solution)/shard_map/ppermute | solution.py:138
  101.0 14.9 %all-gather.2.cloned.1.call-done = f32[768,512]{1,0:T(8,128)} async-done(((f32[48,512]{1,0:T(8,128)}), f32[768,512]{1,0:T(8,128)}) %all-gather.2.cloned.1.call-update) | async-done | bytes 1572880 | tf_op jit(solution)/shard_map/all_gather | solution.py:132
  115.9 3.6 %collective-permute-start.1 = (f32[768,512]{1,0:T(8,128)}, f32[768,512]{1,0:T(8,128)}, u32[]{:S(2)}, u32[]{:S(2)}) collective-permute-start(f32[768,512]{1,0:T(8,128)} %all-gather.2.cloned.1.call-done), channel_id=1, source_target_pairs={{0,1},{1,0},{2,3},{3,2},{4,5},{5,4},{6,7},{7,6},{8,9},{9,8},{10,11... | collective-permute-start | bytes 4718600 | tf_op jit(solution)/shard_map/ppermute | solution.py:147
  119.5 0.1 pad_add_fusion.info
  119.6 17.0 %shard_map.50 = f32[288,512]{1,0:T(8,128)S(1)} custom-call(s32[3]{0:T(128)S(1)} %pad_add_fusion.info, s32[1,512]{1,0:T(1,128)S(1)} %bitcast.11, bf16[512,1024]{1,0:T(8,128)(2,1)S(1)} %fusion.6.own_ref, bf16[512,1024]{1,0:T(8,128)(2,1)S(1)} %collective-permute-done.oth_ref, bf16[256,2048]{1,0:T(8,128)(2,1)S(1)} %copy-done), custom_call_target="tpu_custom_call" | custom-call | tf_op jit(solution)/shard_map/pallas_call | solution.py:66
  136.6 0.6 fusion.3
  137.2 0.6 fusion.2
  137.9 0.6 fusion.8
  138.5 0.0 collective-permute-done.1
  138.5 0.8 copy-done.5
  139.3 1.8 %broadcast_select_fusion.1 = (f32[768,512]{1,0:T(8,128)S(1)}, f32[768,512]{1,0:T(8,128)S(1)}) fusion(f32[768,512]{1,0:T(8,128)S(1)} %copy-done.5, f32[768,512]{1,0:T(8,128)} %collective-permute-done.1, pred[]{:T(512)S(6)} %eq.113), kind=kLoop, calls=%fused_computation.27 | loop fusion | flops 786432 | bytes 6291457 | tf_op jit(solution)/shard_map/jit(_where)/select_n | solution.py:149
  141.1 3.1 %fusion = f32[288,1000]{1,0:T(8,128)S(1)} fusion(f32[288,768]{1,0:T(8,128)S(1)} %fusion.8, f32[768,512]{1,0:T(8,128)S(1)} %get-tuple-element.19, f32[768,512]{1,0:T(8,128)S(1)} %get-tuple-element.18), kind=kOutput, calls=%fused_computation.2 | convolution fusion | flops 2654976000 | bytes 5182464 | tf_op jit(solution)/shard_map/dot_general | solution.py:14
  144.2 0.1 slice_subtract_fusion
  144.4 0.7 slice.33
  145.0 1.3 copy.20
  (23 shorter events, 0.2 us)
Async XLA Ops:
  7.2 108.7 %all-gather.2.cloned.1.call-start = ((), (), s32[]{:S(2)}) async-start(), calls=%async_computation.2 | async-start | bytes 1671168 | tf_op jit(solution)/shard_map/all_gather | solution.py:132
  17.0 44.6 %copy-start.2 = (f32[256,1000]{1,0:T(8,128)}, f32[256,1000]{1,0:T(8,128)S(1)}, u32[]{:S(2)}) copy-start(f32[256,1000]{1,0:T(8,128)S(1)} %copy.19) | copy-start | bytes 3072004
  61.6 32.0 %all-to-all-start.1 = ((bf16[16,48,1024]{2,1,0:T(8,128)(2,1)}), bf16[16,48,1024]{2,1,0:T(8,128)(2,1)S(1)}, u32[]{:S(2)}, u32[]{:S(2)}) async-start(bf16[16,48,1024]{2,1,0:T(8,128)(2,1)} %broadcast_in_dim.20), calls=%async_computation.1 | async-start | bytes 3145728 | tf_op jit(solution)/shard_map/all_to_all | solution.py:134
  93.5 1.1 copy-start.4
  94.7 24.9 %copy-start = (bf16[256,2048]{1,0:T(8,128)(2,1)S(1)}, bf16[256,2048]{1,0:T(8,128)(2,1)}, u32[]{:S(2)}) copy-start(bf16[256,2048]{1,0:T(8,128)(2,1)} %pts_ref.1) | copy-start | bytes 3145732
  94.7 24.9 %copy-start.1 = (s32[512]{0:T(512)S(1)}, s32[512]{0:T(512)}, u32[]{:S(2)}) copy-start(s32[512]{0:T(512)} %param.5) | copy-start | bytes 6148
  97.2 22.4 %collective-permute-start = (bf16[512,1024]{1,0:T(8,128)(2,1)S(1)}, bf16[512,1024]{1,0:T(8,128)(2,1)S(1)}, u32[]{:S(2)}, u32[]{:S(2)}) collective-permute-start(bf16[512,1024]{1,0:T(8,128)(2,1)S(1)} %fusion.6.own_ref), channel_id=1, source_target_pairs={{0,1},{1,0},{2,3},{3,2},{4,5},{5,4},{6,7},{7,6},{8,9},{9,8},{10,11... | collective-permute-start | bytes 3145736 | tf_op jit(solution)/shard_map/ppermute | solution.py:138
  115.9 22.6 %collective-permute-start.1 = (f32[768,512]{1,0:T(8,128)}, f32[768,512]{1,0:T(8,128)}, u32[]{:S(2)}, u32[]{:S(2)}) collective-permute-start(f32[768,512]{1,0:T(8,128)} %all-gather.2.cloned.1.call-done), channel_id=1, source_target_pairs={{0,1},{1,0},{2,3},{3,2},{4,5},{5,4},{6,7},{7,6},{8,9},{9,8},{10,11... | collective-permute-start | bytes 4718600 | tf_op jit(solution)/shard_map/ppermute | solution.py:147
  137.9 1.4 copy-start.5
  141.1 3.1 %copy-start.3 = (f32[256,1000]{1,0:T(8,128)S(1)}, f32[256,1000]{1,0:T(8,128)}, u32[]{:S(2)}) copy-start(f32[256,1000]{1,0:T(8,128)} %copy-done.2) | copy-start | bytes 3072004
Sparse Core Ops, SparseCore 0:
  60.4 55.5 all-gather.1

commit v2 on v0

v2 whole, which is shorter than its diff:
```python
import functools

import jax
import jax.numpy as jnp
from jax import lax
from jax.experimental import pallas as pl
from jax.experimental.pallas import tpu as pltpu
from jax.sharding import Mesh
from jax.sharding import PartitionSpec as P

F32 = jnp.float32
BF = jnp.bfloat16
I32 = jnp.int32
HI = lax.Precision.HIGHEST
NN = (((1,), (0,)), ((), ()))
NT = (((1,), (1,)), ((), ()))
TN = (((0,), (0,)), ((), ()))

GAMMA = 0.125
RIDGE = 0.5
PLANE = ("y", "x")
COLUMN = ("zh", "zl", "c")
EVERY = PLANE + COLUMN
CAP = 2
COL_CAP = 48
CLASS_PAD = 1024
SPLIT = 4
MIB = 1024 * 1024


def dot(a, b, dn=NN, prec=None):
    return lax.dot_general(a, b, dn, preferred_element_type=F32, precision=prec)


def iota(shape, axis):
    return lax.broadcasted_iota(I32, shape, axis)


def two_parts(v):
    hi = v.astype(BF)
    return hi, (v - hi.astype(F32)).astype(BF)


def mm3(a, b):
    ah, al = a
    bh, bl = b
    return dot(ah, bh) + (dot(ah, bl) + dot(al, bh))


def vmem():
    return pl.BlockSpec(memory_space=pltpu.VMEM)


def smem():
    return pl.BlockSpec(memory_space=pltpu.SMEM)


def params(mib):
    return pltpu.CompilerParams(vmem_limit_bytes=mib * MIB)


def pack_body(info, ids_ref, pts_ref, res_ref, out_ref, rank_ref, slot_ref, *, n_col):
    me = info[2]
    rows = pts_ref.shape[0]
    ids = ids_ref[...]
    n = ids.shape[1]
    eye = iota((n, n), 0) == iota((n, n), 1)
    ids_col = jnp.sum(jnp.where(eye, jnp.broadcast_to(ids, (n, n)), 0), axis=1, keepdims=True)
    owner = ids // rows
    column = ids // (rows * n_col)
    less = jnp.broadcast_to(ids_col, (n, n)) < ids
    rank = jnp.sum(jnp.where(less & (ids_col >= column * (rows * n_col)), 1, 0), axis=0, keepdims=True)
    slot = jnp.sum(jnp.where(less & (ids_col >= owner * rows), 1, 0), axis=0, keepdims=True)
    rank_ref[...] = rank
    slot_ref[...] = slot
    mine = owner == me
    lane = iota((8, rows), 1)
    sub = iota((8, rows), 0)
    take = jnp.zeros((8, rows), F32)
    for k in range(CAP):
        at = jnp.max(jnp.where(mine & (slot == k), ids - me * rows, -1), axis=1, keepdims=True)
        take = jnp.where((sub == k) & (lane == at), 1.0, take)
    take = take.astype(BF)
    picked = dot(take, pts_ref[...]).astype(BF)
    res = res_ref[...]
    hi = res.astype(BF)
    rest = res - hi.astype(F32)
    mid = rest.astype(BF)
    low = (rest - mid.astype(F32)).astype(BF)
    classes = res.shape[0]
    pad = jnp.zeros((8, CLASS_PAD - classes), F32)
    parts = [jnp.concatenate([dot(take, v, NT), pad], axis=1).astype(BF) for v in (hi, mid, low)]
    half = pts_ref.shape[1] // 2
    chalf = CLASS_PAD // 2
    for core in range(2):
        row = [picked[:CAP, core * half : (core + 1) * half]]
        row += [v[:CAP, core * chalf : (core + 1) * chalf] for v in parts]
        row = jnp.concatenate(row, axis=1).astype(F32)
        w = row.shape[1] // SPLIT
        block = jnp.concatenate([row[:, q * w : (q + 1) * w] for q in range(SPLIT)], axis=0).astype(BF)
        for z in range(n_col // 2):
            out_ref[2 * z + core] = block


def pack(info, ids, points, res_t, n_col):
    width = points.shape[1] // 2 + 3 * CLASS_PAD // 2
    n = ids.shape[1]
    return pl.pallas_call(
        functools.partial(pack_body, n_col=n_col),
        out_shape=(
            jax.ShapeDtypeStruct((n_col, CAP * SPLIT, width // SPLIT), BF),
            jax.ShapeDtypeStruct((1, n), I32),
            jax.ShapeDtypeStruct((1, n), I32),
        ),
        in_specs=[smem(), vmem(), vmem(), vmem()],
        out_specs=(vmem(), vmem(), vmem()),
        compiler_params=params(32),
    )(info, ids, points, res_t)


def compact_body(info, ids_ref, rank_ref, slot_ref, in_ref, pts_ref, res_ref, *, rows, n_col):
    plane = info[1]
    ids = ids_ref[...]
    n = ids.shape[1]
    owner = ids // rows
    column = ids // (rows * n_col)
    wide = in_ref.shape[0]
    sel_rank = (iota((COL_CAP, n), 0) == rank_ref[...]) & (column == plane)
    at = iota((wide, n), 0)
    group = CAP * SPLIT
    sel_slot = (at // group == owner - column * n_col) & (at % CAP == slot_ref[...])
    pick = dot(sel_rank.astype(F32).astype(BF), sel_slot.astype(F32).astype(BF), NT)
    part = (iota((COL_CAP, wide), 1) // CAP) % SPLIT
    data = in_ref[...]
    whole = [dot(jnp.where(part == q, pick, 0.0).astype(BF), data) for q in range(SPLIT)]
    whole = jnp.concatenate(whole, axis=1)
    half = pts_ref.shape[2]
    chalf = CLASS_PAD // 2
    pts = whole[:, :half].astype(BF)
    res = whole[:, half : half + chalf] + whole[:, half + chalf : half + 2 * chalf]
    res = res + whole[:, half + 2 * chalf :]
    for p in range(pts_ref.shape[0]):
        pts_ref[p] = pts
        res_ref[p] = res


def compact(info, ids, rank, slot, data, rows, half, n_plane, n_col):
    return pl.pallas_call(
        functools.partial(compact_body, rows=rows, n_col=n_col),
        out_shape=(
            jax.ShapeDtypeStruct((n_plane, COL_CAP, half), BF),
            jax.ShapeDtypeStruct((n_plane, COL_CAP, CLASS_PAD // 2), F32),
        ),
        in_specs=[smem(), vmem(), vmem(), vmem(), vmem()],
        out_specs=(vmem(), vmem()),
        compiler_params=params(32),
    )(info, ids, rank, slot, data)


def place_matrix(ids, rank, wide, span):
    return (iota((wide, ids.shape[1]), 0) == (ids // span) * COL_CAP + rank).astype(F32).astype(BF)


def order_body(ids_ref, rank_ref, in_ref, out_ref, *, span):
    place = place_matrix(ids_ref[...], rank_ref[...], in_ref.shape[0], span)
    out_ref[...] = dot(place, in_ref[...], TN).astype(BF)


def order(ids, rank, data, span):
    return pl.pallas_call(
        functools.partial(order_body, span=span),
        out_shape=jax.ShapeDtypeStruct((ids.shape[1], data.shape[1]), BF),
        in_specs=[vmem(), vmem(), vmem()],
        out_specs=vmem(),
        compiler_params=params(32),
    )(ids, rank, data)


def weights_body(info, ids_ref, rank_ref, own_ref, oth_ref, pts_ref, hi_ref, lo_ref, g_ref, gh_ref, gl_ref, x_ref, m_ref, *, half, share, span):
    n = own_ref.shape[0]
    rows = pts_ref.shape[0]
    core, me, share_at = info[0], info[2], info[3]
    own = own_ref[...]
    oth = oth_ref[...]
    cross = dot(own, own, NT) + dot(oth, oth, NT)
    eye = iota((n, n), 0) == iota((n, n), 1)
    diag = jnp.where(eye, cross, 0.0)
    sq_row = jnp.sum(diag, axis=0, keepdims=True)
    sq_col = jnp.sum(diag, axis=1, keepdims=True)
    gram = jnp.exp(-GAMMA * (sq_col + sq_row - 2.0 * cross)) + jnp.where(eye, RIDGE, 0.0)
    g_ref[...] = gram
    gh, gl = two_parts(gram)
    gh_ref[...] = gh
    gl_ref[...] = gl
    p_own = pts_ref[:, pl.ds(pl.multiple_of(core * half, half), half)]
    p_oth = pts_ref[:, pl.ds(pl.multiple_of((1 - core) * half, half), half)]
    pf = pts_ref[...].astype(F32)
    psq = jnp.sum(pf * pf, axis=1, keepdims=True)
    p_cross = dot(p_own, own, NT) + dot(p_oth, oth, NT)
    p_kern = jnp.exp(-GAMMA * (psq + sq_row - 2.0 * p_cross))
    point_id = me * rows + iota((rows, n), 0)
    m_ref[pl.ds(0, rows), :] = p_kern + jnp.where(point_id == ids_ref[...], RIDGE, 0.0)
    m_ref[pl.ds(rows, share), :] = jnp.where(share_at + iota((share, n), 0) == iota((share, n), 1), 1.0, 0.0)
    lo = 0.499
    hi = jnp.max(jnp.sum(gram, axis=0, keepdims=True)) * 1.001
    s = 2.0 / (lo + hi)
    x_ref[...] = jnp.where(eye, 2.0 * s, 0.0) - (s * s) * gram
    d = (hi - lo) / (hi + lo)

    def refine(resid):
        x = x_ref[...] * (2.0 / (2.0 - resid))
        xs = two_parts(x)
        r = jnp.where(eye, 1.0, 0.0) - mm3((gh_ref[...], gl_ref[...]), xs)
        x_ref[...] = x + mm3(xs, two_parts(r))
        after = resid / (2.0 - resid)
        return after * after

    lax.while_loop(lambda resid: resid > 1e-4, refine, d * d)
    m = m_ref[...]
    xs = two_parts(x_ref[...])
    w = mm3(two_parts(m), xs)
    e = m - dot(w, g_ref[...], NN, HI)
    w = w + mm3(two_parts(e), xs)
    place = place_matrix(ids_ref[...], rank_ref[...], hi_ref.shape[1], span)
    wh, wl = two_parts(w)
    hi_ref[...] = dot(wh, place, NT).astype(BF)
    lo_ref[...] = dot(wl, place, NT).astype(BF)


def weights(info, ids, rank, own, oth, points, share, wide, span):
    n = own.shape[0]
    rows = points.shape[0]
    out = jax.ShapeDtypeStruct((rows + share, wide), BF)
    return pl.pallas_call(
        functools.partial(weights_body, half=own.shape[1], share=share, span=span),
        out_shape=(out, out),
        in_specs=[smem()] + [vmem()] * 5,
        out_specs=(vmem(), vmem()),
        scratch_shapes=[
            pltpu.VMEM((n, n), F32),
            pltpu.VMEM((n, n), BF),
            pltpu.VMEM((n, n), BF),
            pltpu.VMEM((n, n), F32),
            pltpu.VMEM((rows + share, n), F32),
        ],
        compiler_params=params(48),
        cost_estimate=pl.CostEstimate(flops=10**10, bytes_accessed=6 * 10**6, transcendentals=4 * 10**5),
    )(info, ids, rank, own, oth, points)


def update_body(info, hi_ref, lo_ref, own_ref, oth_ref, res_ref, out_ref, share_ref, ch_ref):
    core = info[0]
    rows = res_ref.shape[1]
    classes = res_ref.shape[0]
    chalf = own_ref.shape[1]
    w = hi_ref[...], lo_ref[...]
    ch_ref[:, pl.ds(pl.multiple_of(core * chalf, chalf), chalf)] = mm3(w, two_parts(own_ref[...]))
    ch_ref[:, pl.ds(pl.multiple_of((1 - core) * chalf, chalf), chalf)] = mm3(w, two_parts(oth_ref[...]))
    share_ref[...] = ch_ref[pl.ds(rows, share_ref.shape[0]), pl.ds(0, classes)]
    out_ref[...] = res_ref[...] - ch_ref[pl.ds(0, rows), :].T[:classes]


def update(info, hi, lo, own, oth, res_t, share):
    classes, rows = res_t.shape
    return pl.pallas_call(
        update_body,
        out_shape=(jax.ShapeDtypeStruct((classes, rows), F32), jax.ShapeDtypeStruct((share, classes), F32)),
        in_specs=[smem()] + [vmem()] * 5,
        out_specs=(vmem(), vmem()),
        scratch_shapes=[pltpu.VMEM((rows + share, CLASS_PAD), F32)],
        compiler_params=params(48),
    )(info, hi, lo, own, oth, res_t)


def on_device(points, residual, block_ids):
    rows, feats = points.shape
    block = block_ids.shape[0]
    n_plane = lax.axis_size(PLANE)
    n_col = lax.axis_size(COLUMN)
    n_gy = lax.axis_size("zl") * lax.axis_size("c")
    plane = lax.axis_index(PLANE)
    place = lax.axis_index(COLUMN)
    share = block // n_gy
    half = feats // 2
    wide = n_plane * COL_CAP
    span = rows * n_col
    info = jnp.stack([lax.axis_index("c"), plane, plane * n_col + place, (place % n_gy) * share]).astype(I32)
    ids = block_ids.reshape(1, block)
    res_t = residual.T
    swap = [(0, 1), (1, 0)]

    packed, rank, slot = pack(info, ids, points, res_t, n_col)
    col_rows = lax.all_to_all(packed, COLUMN, 0, 0, tiled=True)
    col_rows = col_rows.reshape(n_col * CAP * SPLIT, col_rows.shape[2])
    pts_out, res_out = compact(info, ids, rank, slot, col_rows, rows, half, n_plane, n_col)
    all_pts = lax.all_to_all(pts_out, PLANE, 0, 0, tiled=True).reshape(wide, half)
    all_res = lax.all_to_all(res_out, PLANE, 0, 0, tiled=True).reshape(wide, CLASS_PAD // 2)
    own = order(ids, rank, all_pts, span)
    other = lax.ppermute(own, "c", swap)
    hi, lo = weights(info, ids, rank, own, other, points, share, wide, span)
    other_res = lax.ppermute(all_res, "c", swap)
    out_t, step_share = update(info, hi, lo, all_res, other_res, res_t, share)
    return (out_t.T, step_share)


def solution(mesh):
    fine = Mesh(mesh.devices.reshape(4, 4, 2, 8, 2), EVERY)
    return jax.shard_map(
        on_device,
        mesh=fine,
        in_specs=(P(EVERY, None), P(EVERY, None), P()),
        out_specs=(P(EVERY, None), P(("zl", "c"), None)),
        check_vma=False,
    )
```

time: 626 us -> 131 us (0.21)
  waiting for transfers between devices: 386 us -> 14.6 us
  other arithmetic: 136 us -> 0.08 us
  blocking collectives: 0 us -> 69.9 us
  local copies, waits for them, and re-layouts: 52.8 us -> 4.36 us
  matrix products: 28.1 us -> 0 us
  Pallas kernels: 0 us -> 26.8 us
  between operations: 17.2 us -> 0.75 us
  starting transfers between devices: 0.08 us -> 13.6 us
    all_gather x2 -> x0, waiting for transfers between devices: 386 us -> none  [the longest x1 204 us: on_device(): all_resid = lax.all_gather(packed_resid, ('gx', 'gy'), axis=0, tiled=True)]
    another operation x18 -> x1, other arithmetic: 123 us -> 0.08 us  [on_device(): jnp.stack([lax.axis_index('c'), plane, plane * n_col + place, place % n_g...]
    all_to_all x0 -> x2, blocking collectives: none -> 69.9 us  [the longest x1 41.6 us: on_device(): col_rows = lax.all_to_all(packed, COLUMN, 0, 0, tiled=True)]
    pallas_call x0 -> x5, Pallas kernels: none -> 26.8 us  [the longest x1 18.1 us: weights(): pl.pallas_call(functools.partial(weights_body, half=own.shape[1], share=s...]
    another operation x20 -> x0, matrix products: 21.7 us -> none  [the longest x14 16.2 us: on_device(): block_step = jax.scipy.linalg.cho_solve((factor, True), block_resid)]
    gather x5 -> x0, local copies, waits for them, and re-layouts: 15.3 us -> none  [the longest x1 7.31 us: on_device(): block_points = jnp.take(all_points, gather_index, axis=0)]
    all_to_all x0 -> x1, waiting for transfers between devices: none -> 14.6 us  [on_device(): lax.all_to_all(res_out, PLANE, 0, 0, tiled=True)]
    another operation x17 -> x0, local copies, waits for them, and re-layouts: 14 us -> none
  transfers between devices with their start and end apart: 2 -> 3, of which waited for: 2 -> 1; matrix products, arithmetic and copies ran while one was open for 3% -> 0% of each run, Pallas kernels for 0% -> 15%
where the time goes in v2:
time: 131 us; the launch traced here: 130 us
  blocking collectives  69.9 us (53%)
  Pallas kernels  26.8 us (20%)
  waiting for transfers between devices  14.6 us (11%)
  starting transfers between devices  13.6 us (10%)
  local copies, waits for them, and re-layouts  4.36 us (3%)
    all_to_all x1, blocking collectives, on_device(): col_rows = lax.all_to_all(packed, COLUMN, 0, 0, tiled=True)  41.6 us
    all_to_all x1, blocking collectives, on_device(): lax.all_to_all(pts_out, PLANE, 0, 0, tiled=True).reshape(wide, half)  28.3 us
    pallas_call x1, Pallas kernels, weights(): pl.pallas_call(functools.partial(weights_body, half=own.shape[1], share=s...  18.1 us
    all_to_all x1, waiting for transfers between devices, on_device(): lax.all_to_all(res_out, PLANE, 0, 0, tiled=True)  14.6 us
    ppermute x1, starting transfers between devices, on_device(): other_res = lax.ppermute(all_res, 'c', swap)  5.97 us
    unnamed x14, local copies, waits for them, and re-layouts  4.36 us
    ppermute x1, starting transfers between devices, on_device(): other = lax.ppermute(own, 'c', swap)  3.88 us
    all_to_all x1, starting transfers between devices, on_device(): lax.all_to_all(res_out, PLANE, 0, 0, tiled=True)  3.71 us
  transfers between devices with their start and end apart: 3, of which 1 were waited for; matrix products, arithmetic and copies ran while one was open for 0% of the time, Pallas kernels for 15%

profile of v2, /device:TPU:1, one launch (start us, length us, event | category | flops | bytes accessed | tf_op | source)
XLA Modules:
  0.0 130.1 jit_solution(14546675119828296159)
XLA Ops:
  0.6 0.0 copy-start.6
  0.7 0.1 pad_add_fusion.info
  0.7 0.0 copy-start
  0.7 1.2 copy-done
  2.0 0.0 copy-start.3
  2.0 1.2 copy-done.3
  3.2 0.0 copy-start.5
  3.2 0.7 copy-done.5
  3.9 1.9 %shard_map.50 = (bf16[32,8,640]{2,1,0:T(8,128)(2,1)S(1)}, s32[1,512]{1,0:T(1,128)S(1)}, s32[1,512]{1,0:T(1,128)S(1)}) custom-call(s32[4]{0:T(128)S(1)} %pad_add_fusion.info, s32[1,512]{1,0:T(1,128)S(1)} %bitcast.16, bf16[256,2048]{1,0:T(8,128)(2,1)S(1)} %copy-done.3, f32[1000,256]{1,0:T(8,128)S(1)} %bitcast.13), custom_call_target="tpu_custom_call" | custom-call | tf_op jit(solution)/shard_map/pallas_call | solution.py:108
  5.7 41.6 %all_to_all.15 = bf16[32,8,640]{2,1,0:T(8,128)(2,1)S(1)} all-to-all(bf16[32,8,640]{2,1,0:T(8,128)(2,1)S(1)} %get-tuple-element.13), channel_id=1, replica_groups=mesh['y'=4,'x'=4,'zh'=2,'zl'=8,'c'=2] {'zh','zl','c'}, dimensions={0} | all-to-all | bytes 655360 | tf_op jit(solution)/shard_map/all_to_all | solution.py:293
  47.3 0.0 copy-done.6
  47.3 1.4 %shard_map.51 = (bf16[16,48,1024]{2,1,0:T(8,128)(2,1)S(1)}, f32[16,48,512]{2,1,0:T(8,128)S(1)}) custom-call(s32[4]{0:T(128)S(1)} %pad_add_fusion.info, s32[1,512]{1,0:T(1,128)S(1)} %bitcast.17, s32[1,512]{1,0:T(1,128)S(1)} %get-tuple-element.11.rank_ref, s32[1,512]{1,0:T(1,128)S(1)} %get-tuple-element.12.slot_ref, bf16[256,640]{1,0:T(8,128)(2,1)S(1)} %bitcast.15), custom_call_target="tpu_custom_call" | custom-call | tf_op jit(solution)/shard_map/pallas_call | solution.py:148
  48.7 0.0 copy-start.2
  48.7 28.3 %all_to_all.16 = bf16[16,48,1024]{2,1,0:T(8,128)(2,1)S(1)} all-to-all(bf16[16,48,1024]{2,1,0:T(8,128)(2,1)S(1)} %get-tuple-element.14), channel_id=1, replica_groups=mesh['y'=4,'x'=4,'zh'=2,'zl'=8,'c'=2] {'y','x'}, dimensions={0} | all-to-all | bytes 3145728 | tf_op jit(solution)/shard_map/all_to_all | solution.py:296
  77.0 0.0 copy-done.2
  77.0 3.7 %all-to-all-start.2 = ((f32[16,48,512]{2,1,0:T(8,128)}), f32[16,48,512]{2,1,0:T(8,128)S(1)}, u32[]{:S(2)}, u32[]{:S(2)}) async-start(f32[16,48,512]{2,1,0:T(8,128)} %copy-done.2), calls=%async_computation.2 | async-start | bytes 3145728 | tf_op jit(solution)/shard_map/all_to_all | solution.py:297
  80.7 2.0 %shard_map.52.own_ref = bf16[512,1024]{1,0:T(8,128)(2,1)} custom-call(s32[1,512]{1,0:T(1,128)S(1)} %bitcast.18, s32[1,512]{1,0:T(1,128)S(1)} %get-tuple-element.11.rank_ref, bf16[768,1024]{1,0:T(8,128)(2,1)S(1)} %bitcast.10), custom_call_target="tpu_custom_call" | custom-call | tf_op jit(solution)/shard_map/pallas_call | solution.py:170
  82.7 3.9 %collective-permute-start = (bf16[512,1024]{1,0:T(8,128)(2,1)}, bf16[512,1024]{1,0:T(8,128)(2,1)S(1)}, u32[]{:S(2)}, u32[]{:S(2)}) collective-permute-start(bf16[512,1024]{1,0:T(8,128)(2,1)} %shard_map.52.own_ref), channel_id=1, source_target_pairs={{0,1},{1,0},{2,3},{3,2},{4,5},{5,4},{6,7},{7,6},{8,9},{9,8},{10,11... | collective-permute-start | bytes 3145736 | tf_op jit(solution)/shard_map/ppermute | solution.py:299
  86.6 14.6 %all-to-all-done.2 = f32[16,48,512]{2,1,0:T(8,128)S(1)} async-done(((f32[16,48,512]{2,1,0:T(8,128)}), f32[16,48,512]{2,1,0:T(8,128)S(1)}, u32[]{:S(2)}, u32[]{:S(2)}) %all-to-all-start.2) | async-done | bytes 1572896 | tf_op jit(solution)/shard_map/all_to_all | solution.py:297
  101.3 0.0 copy-start.1
  101.3 6.0 %collective-permute-start.1 = (f32[768,512]{1,0:T(8,128)S(1)}, f32[768,512]{1,0:T(8,128)S(1)}, u32[]{:S(2)}, u32[]{:S(2)}) collective-permute-start(f32[768,512]{1,0:T(8,128)S(1)} %bitcast.11), channel_id=1, source_target_pairs={{0,1},{1,0},{2,3},{3,2},{4,5},{5,4},{6,7},{7,6},{8,9},{9,8},{10,11... | collective-permute-start | bytes 4718600 | tf_op jit(solution)/shard_map/ppermute | solution.py:301
  107.2 0.0 collective-permute-done.oth_ref
  107.2 0.0 copy-start.4
  107.3 1.2 copy-done.4
  108.5 18.1 %shard_map.53 = (bf16[288,768]{1,0:T(8,128)(2,1)S(1)}, bf16[288,768]{1,0:T(8,128)(2,1)S(1)}) custom-call(s32[4]{0:T(128)S(1)} %pad_add_fusion.info, s32[1,512]{1,0:T(1,128)S(1)} %bitcast.19, s32[1,512]{1,0:T(1,128)S(1)} %get-tuple-element.11.rank_ref, bf16[512,1024]{1,0:T(8,128)(2,1)} %shard_map.52.own_ref, ...), custom_call_target="tpu_custom_call" | custom-call | flops 10000000000 | bytes 6000000 | tf_op jit(solution)/shard_map/pallas_call | solution.py:234
  126.6 0.0 collective-permute-done.1.oth_ref
  126.6 0.0 copy-done.1
  126.6 3.5 %shard_map.54 = (f32[1000,256]{1,0:T(8,128)}, f32[32,1000]{1,0:T(8,128)}) custom-call(s32[4]{0:T(128)S(1)} %pad_add_fusion.info, bf16[288,768]{1,0:T(8,128)(2,1)S(1)} %get-tuple-element.15.hi_ref, bf16[288,768]{1,0:T(8,128)(2,1)S(1)} %get-tuple-element.16.lo_ref, f32[768,512]{1,0:T(8,128)S(1)} %bitcast.12, f32[768,512]{1,0:T(8,128)S(1)} %collective-permute-done.1.oth_ref, ...), custom_call_target="tpu_custom_call" | custom-call | tf_op jit(solution)/shard_map/pallas_call | solution.py:265
Async XLA Ops:
  0.6 46.7 %copy-start.6 = (s32[512]{0:T(512)S(1)}, s32[512]{0:T(512)}, u32[]{:S(2)}) copy-start(s32[512]{0:T(512)} %param.5) | copy-start | bytes 6148
  0.7 1.2 copy-start
  2.0 1.2 copy-start.3
  3.2 0.7 copy-start.5
  48.7 28.3 %copy-start.2 = (f32[16,48,512]{2,1,0:T(8,128)}, f32[16,48,512]{2,1,0:T(8,128)S(1)}, u32[]{:S(2)}) copy-start(f32[16,48,512]{2,1,0:T(8,128)S(1)} %get-tuple-element.17) | copy-start | bytes 4718596
  77.0 24.2 %all-to-all-start.2 = ((f32[16,48,512]{2,1,0:T(8,128)}), f32[16,48,512]{2,1,0:T(8,128)S(1)}, u32[]{:S(2)}, u32[]{:S(2)}) async-start(f32[16,48,512]{2,1,0:T(8,128)} %copy-done.2), calls=%async_computation.2 | async-start | bytes 3145728 | tf_op jit(solution)/shard_map/all_to_all | solution.py:297
  82.7 24.5 %collective-permute-start = (bf16[512,1024]{1,0:T(8,128)(2,1)}, bf16[512,1024]{1,0:T(8,128)(2,1)S(1)}, u32[]{:S(2)}, u32[]{:S(2)}) collective-permute-start(bf16[512,1024]{1,0:T(8,128)(2,1)} %shard_map.52.own_ref), channel_id=1, source_target_pairs={{0,1},{1,0},{2,3},{3,2},{4,5},{5,4},{6,7},{7,6},{8,9},{9,8},{10,11... | collective-permute-start | bytes 3145736 | tf_op jit(solution)/shard_map/ppermute | solution.py:299
  101.3 25.3 %copy-start.1 = (f32[256,1000]{0,1:T(8,128)S(1)}, f32[256,1000]{0,1:T(8,128)}, u32[]{:S(2)}) copy-start(f32[256,1000]{0,1:T(8,128)} %param.4) | copy-start | bytes 3072004
  101.3 25.3 %collective-permute-start.1 = (f32[768,512]{1,0:T(8,128)S(1)}, f32[768,512]{1,0:T(8,128)S(1)}, u32[]{:S(2)}, u32[]{:S(2)}) collective-permute-start(f32[768,512]{1,0:T(8,128)S(1)} %bitcast.11), channel_id=1, source_target_pairs={{0,1},{1,0},{2,3},{3,2},{4,5},{5,4},{6,7},{7,6},{8,9},{9,8},{10,11... | collective-permute-start | bytes 4718600 | tf_op jit(solution)/shard_map/ppermute | solution.py:301
  107.2 1.2 copy-start.4

commit v3 on v2

v3 whole, which is shorter than its diff:
```python
import functools

import jax
import jax.numpy as jnp
from jax import lax
from jax.experimental import pallas as pl
from jax.experimental.pallas import tpu as pltpu
from jax.sharding import Mesh
from jax.sharding import PartitionSpec as P

F32 = jnp.float32
BF = jnp.bfloat16
I32 = jnp.int32
HI = lax.Precision.HIGHEST
NN = (((1,), (0,)), ((), ()))
NT = (((1,), (1,)), ((), ()))
TN = (((0,), (0,)), ((), ()))

GAMMA = 0.125
RIDGE = 0.5
PLANE = ("y", "x")
COLUMN = ("zh", "zl", "c")
EVERY = PLANE + COLUMN
CAP = 2
COL_CAP = 48
CLASS_PAD = 1024
SPLIT = 4
MIB = 1024 * 1024


def dot(a, b, dn=NN, prec=None):
    return lax.dot_general(a, b, dn, preferred_element_type=F32, precision=prec)


def iota(shape, axis):
    return lax.broadcasted_iota(I32, shape, axis)


def two_parts(v):
    hi = v.astype(BF)
    return hi, (v - hi.astype(F32)).astype(BF)


def mm3(a, b):
    ah, al = a
    bh, bl = b
    return dot(ah, bh) + (dot(ah, bl) + dot(al, bh))


def vmem():
    return pl.BlockSpec(memory_space=pltpu.VMEM)


def smem():
    return pl.BlockSpec(memory_space=pltpu.SMEM)


def hbm():
    return pl.BlockSpec(memory_space=pltpu.HBM)


def params(mib):
    return pltpu.CompilerParams(vmem_limit_bytes=mib * MIB)


def pack_body(info, ids_hbm, pts_hbm, res_hbm, out_ref, tab_ref, ids_ref, pts_ref, res_ref, sems, *, n_col):
    me = info[2]
    rows = pts_ref.shape[0]
    ids_in = pltpu.make_async_copy(ids_hbm, ids_ref, sems.at[0])
    pts_in = pltpu.make_async_copy(pts_hbm, pts_ref, sems.at[1])
    res_in = pltpu.make_async_copy(res_hbm, res_ref, sems.at[2])
    ids_in.start()
    pts_in.start()
    res_in.start()
    ids_in.wait()
    ids = ids_ref[...]
    n = ids.shape[1]
    eye = iota((n, n), 0) == iota((n, n), 1)
    ids_col = jnp.sum(jnp.where(eye, jnp.broadcast_to(ids, (n, n)), 0), axis=1, keepdims=True)
    owner = ids // rows
    column = ids // (rows * n_col)
    less = jnp.broadcast_to(ids_col, (n, n)) < ids
    rank = jnp.sum(jnp.where(less & (ids_col >= column * (rows * n_col)), 1, 0), axis=0, keepdims=True)
    slot = jnp.sum(jnp.where(less & (ids_col >= owner * rows), 1, 0), axis=0, keepdims=True)
    tab_ref[...] = jnp.concatenate([ids, rank, slot, jnp.zeros((5, n), I32)], axis=0)
    mine = owner == me
    lane = iota((8, rows), 1)
    sub = iota((8, rows), 0)
    take = jnp.zeros((8, rows), F32)
    for k in range(CAP):
        at = jnp.max(jnp.where(mine & (slot == k), ids - me * rows, -1), axis=1, keepdims=True)
        take = jnp.where((sub == k) & (lane == at), 1.0, take)
    take = take.astype(BF)
    pts_in.wait()
    picked = dot(take, pts_ref[...]).astype(BF)
    res_in.wait()
    res = res_ref[...]
    hi = res.astype(BF)
    rest = res - hi.astype(F32)
    mid = rest.astype(BF)
    low = (rest - mid.astype(F32)).astype(BF)
    classes = res.shape[0]
    pad = jnp.zeros((8, CLASS_PAD - classes), F32)
    parts = [jnp.concatenate([dot(take, v, NT), pad], axis=1).astype(BF) for v in (hi, mid, low)]
    half = pts_ref.shape[1] // 2
    chalf = CLASS_PAD // 2
    for core in range(2):
        row = [picked[:CAP, core * half : (core + 1) * half]]
        row += [v[:CAP, core * chalf : (core + 1) * chalf] for v in parts]
        row = jnp.concatenate(row, axis=1).astype(F32)
        w = row.shape[1] // SPLIT
        block = jnp.concatenate([row[:, q * w : (q + 1) * w] for q in range(SPLIT)], axis=0).astype(BF)
        for z in range(n_col // 2):
            out_ref[2 * z + core] = block


def pack(info, ids, points, res_t, n_col):
    width = points.shape[1] // 2 + 3 * CLASS_PAD // 2
    n = ids.shape[1]
    return pl.pallas_call(
        functools.partial(pack_body, n_col=n_col),
        out_shape=(
            jax.ShapeDtypeStruct((n_col, CAP * SPLIT, width // SPLIT), BF),
            jax.ShapeDtypeStruct((8, n), I32),
        ),
        in_specs=[smem(), hbm(), hbm(), hbm()],
        out_specs=(vmem(), vmem()),
        scratch_shapes=[
            pltpu.VMEM(ids.shape, I32),
            pltpu.VMEM(points.shape, BF),
            pltpu.VMEM(res_t.shape, F32),
            pltpu.SemaphoreType.DMA((3,)),
        ],
        compiler_params=params(60),
    )(info, ids, points, res_t)


def table(tab_ref):
    return tab_ref[0:1, :], tab_ref[1:2, :], tab_ref[2:3, :]


def compact_body(info, tab_ref, in_ref, pts_ref, res_ref, *, rows, n_col):
    plane = info[1]
    ids, rank, slot = table(tab_ref)
    n = ids.shape[1]
    owner = ids // rows
    column = ids // (rows * n_col)
    wide = in_ref.shape[0]
    sel_rank = (iota((COL_CAP, n), 0) == rank) & (column == plane)
    at = iota((wide, n), 0)
    group = CAP * SPLIT
    sel_slot = (at // group == owner - column * n_col) & (at % CAP == slot)
    pick = dot(sel_rank.astype(F32).astype(BF), sel_slot.astype(F32).astype(BF), NT)
    part = (iota((COL_CAP, wide), 1) // CAP) % SPLIT
    data = in_ref[...]
    whole = [dot(jnp.where(part == q, pick, 0.0).astype(BF), data) for q in range(SPLIT)]
    whole = jnp.concatenate(whole, axis=1)
    half = pts_ref.shape[2]
    chalf = CLASS_PAD // 2
    pts = whole[:, :half].astype(BF)
    res = whole[:, half : half + chalf] + whole[:, half + chalf : half + 2 * chalf]
    res = res + whole[:, half + 2 * chalf :]
    for p in range(pts_ref.shape[0]):
        pts_ref[p] = pts
        res_ref[p] = res


def compact(info, tab, data, rows, half, n_plane, n_col):
    return pl.pallas_call(
        functools.partial(compact_body, rows=rows, n_col=n_col),
        out_shape=(
            jax.ShapeDtypeStruct((n_plane, COL_CAP, half), BF),
            jax.ShapeDtypeStruct((n_plane, COL_CAP, CLASS_PAD // 2), F32),
        ),
        in_specs=[smem(), vmem(), vmem()],
        out_specs=(vmem(), vmem()),
        compiler_params=params(16),
    )(info, tab, data)


def place_matrix(tab_ref, wide, span):
    ids, rank, _ = table(tab_ref)
    return (iota((wide, ids.shape[1]), 0) == (ids // span) * COL_CAP + rank).astype(F32).astype(BF)


def order_body(tab_ref, in_ref, out_ref, *, span):
    out_ref[...] = dot(place_matrix(tab_ref, in_ref.shape[0], span), in_ref[...], TN).astype(BF)


def order(tab, data, span):
    return pl.pallas_call(
        functools.partial(order_body, span=span),
        out_shape=jax.ShapeDtypeStruct((tab.shape[1], data.shape[1]), BF),
        in_specs=[vmem(), vmem()],
        out_specs=vmem(),
        compiler_params=params(10),
    )(tab, data)


def first_half_body(info, pts_ref, own_ref, cross_ref, p_cross_ref, psq_ref, p_oth_ref, *, half):
    core = info[0]
    own = own_ref[...]
    cross_ref[...] = dot(own, own, NT)
    p_own = pts_ref[:, pl.ds(pl.multiple_of(core * half, half), half)]
    p_oth = pts_ref[:, pl.ds(pl.multiple_of((1 - core) * half, half), half)]
    p_cross_ref[...] = dot(p_own, own, NT)
    p_oth_ref[...] = p_oth
    a = p_own.astype(F32)
    b = p_oth.astype(F32)
    psq_ref[...] = jnp.sum(a * a, axis=1, keepdims=True) + jnp.sum(b * b, axis=1, keepdims=True)


def first_half(info, points, own):
    n, half = own.shape
    rows = points.shape[0]
    return pl.pallas_call(
        functools.partial(first_half_body, half=half),
        out_shape=(
            jax.ShapeDtypeStruct((n, n), F32),
            jax.ShapeDtypeStruct((rows, n), F32),
            jax.ShapeDtypeStruct((rows, 1), F32),
            jax.ShapeDtypeStruct((rows, half), BF),
        ),
        in_specs=[smem(), vmem(), vmem()],
        out_specs=(vmem(),) * 4,
        compiler_params=params(12),
        cost_estimate=pl.CostEstimate(flops=2 * 10**9, bytes_accessed=3 * 10**6, transcendentals=0),
    )(info, points, own)


def inverse_body(info, tab_ref, p_oth_ref, oth_ref, cross_ref, p_cross_ref, psq_ref, hi_ref, lo_ref, g_ref, m_ref, gh_ref, gl_ref, x_ref, *, share):
    n = oth_ref.shape[0]
    rows = p_cross_ref.shape[0]
    me, share_at = info[2], info[3]
    oth = oth_ref[...]
    cross = cross_ref[...] + dot(oth, oth, NT)
    eye = iota((n, n), 0) == iota((n, n), 1)
    diag = jnp.where(eye, cross, 0.0)
    sq_row = jnp.sum(diag, axis=0, keepdims=True)
    sq_col = jnp.sum(diag, axis=1, keepdims=True)
    gram = jnp.exp(-GAMMA * (sq_col + sq_row - 2.0 * cross)) + jnp.where(eye, RIDGE, 0.0)
    g_ref[...] = gram
    gh, gl = two_parts(gram)
    gh_ref[...] = gh
    gl_ref[...] = gl
    p_cross = p_cross_ref[...] + dot(p_oth_ref[...], oth, NT)
    p_kern = jnp.exp(-GAMMA * (psq_ref[...] + sq_row - 2.0 * p_cross))
    point_id = me * rows + iota((rows, n), 0)
    m_ref[pl.ds(0, rows), :] = p_kern + jnp.where(point_id == table(tab_ref)[0], RIDGE, 0.0)
    m_ref[pl.ds(rows, share), :] = jnp.where(share_at + iota((share, n), 0) == iota((share, n), 1), 1.0, 0.0)
    lo = 0.499
    gram = g_ref[...]
    v_col = jnp.sum(gram, axis=1, keepdims=True)
    v_row = jnp.sum(gram, axis=0, keepdims=True)
    hi = jnp.max(jnp.sum(gram * v_col, axis=0, keepdims=True) / v_row) * 1.001
    s = 2.0 / (lo + hi)
    x_ref[...] = jnp.where(eye, 2.0 * s, 0.0) - (s * s) * gram
    d = (hi - lo) / (hi + lo)

    def refine(resid):
        x = x_ref[...] * (2.0 / (2.0 - resid))
        xh, xl = two_parts(x)
        r = (jnp.where(eye, 1.0, 0.0) - mm3((gh_ref[...], gl_ref[...]), (xh, xl))).astype(BF)
        x_ref[...] = x + (dot(xh, r) + dot(xl, r))
        after = resid / (2.0 - resid)
        return after * after

    lax.while_loop(lambda resid: resid > 5e-4, refine, d * d)
    xs = two_parts(x_ref[...])
    m = m_ref[...]
    w = mm3(two_parts(m), xs)
    e = m - dot(w, g_ref[...], NN, HI)
    w = w + mm3(two_parts(e), xs)
    wh, wl = two_parts(w)
    hi_ref[...] = wh
    lo_ref[...] = wl


def inverse(info, tab, p_oth, oth, cross, p_cross, psq, share):
    n = oth.shape[0]
    rows = p_oth.shape[0]
    out = jax.ShapeDtypeStruct((rows + share, n), BF)
    return pl.pallas_call(
        functools.partial(inverse_body, share=share),
        out_shape=(out, out),
        in_specs=[smem()] + [vmem()] * 6,
        out_specs=(vmem(), vmem()),
        scratch_shapes=[
            pltpu.VMEM((n, n), F32),
            pltpu.VMEM((rows + share, n), F32),
            pltpu.VMEM((n, n), BF),
            pltpu.VMEM((n, n), BF),
            pltpu.VMEM((n, n), F32),
        ],
        compiler_params=params(18),
        cost_estimate=pl.CostEstimate(flops=12 * 10**9, bytes_accessed=6 * 10**6, transcendentals=4 * 10**5),
    )(info, tab, p_oth, oth, cross, p_cross, psq)


def update_own_body(tab_ref, wh_ref, wl_ref, res_ref, hi_ref, lo_ref, ch_ref, *, span):
    place = place_matrix(tab_ref, res_ref.shape[0], span)
    hi = dot(wh_ref[...], place, NT).astype(BF)
    lo = dot(wl_ref[...], place, NT).astype(BF)
    hi_ref[...] = hi
    lo_ref[...] = lo
    ch_ref[...] = mm3((hi, lo), two_parts(res_ref[...]))


def update_own(tab, wh, wl, res, span):
    m = wh.shape[0]
    wide, chalf = res.shape
    out = jax.ShapeDtypeStruct((m, wide), BF)
    return pl.pallas_call(
        functools.partial(update_own_body, span=span),
        out_shape=(out, out, jax.ShapeDtypeStruct((m, chalf), F32)),
        in_specs=[vmem()] * 4,
        out_specs=(vmem(),) * 3,
        compiler_params=params(10),
        cost_estimate=pl.CostEstimate(flops=2 * 10**9, bytes_accessed=4 * 10**6, transcendentals=0),
    )(tab, wh, wl, res)


def update_other_body(info, hi_ref, lo_ref, res_ref, ch_ref, res_t_ref, out_ref, share_ref, all_ref):
    core = info[0]
    classes, rows = res_t_ref.shape
    chalf = res_ref.shape[1]
    all_ref[:, pl.ds(pl.multiple_of(core * chalf, chalf), chalf)] = ch_ref[...]
    change = mm3((hi_ref[...], lo_ref[...]), two_parts(res_ref[...]))
    all_ref[:, pl.ds(pl.multiple_of((1 - core) * chalf, chalf), chalf)] = change
    share_ref[...] = all_ref[pl.ds(rows, share_ref.shape[0]), pl.ds(0, classes)]
    out_ref[...] = res_t_ref[...] - all_ref[pl.ds(0, rows), :].T[:classes]


def update_other(info, hi, lo, res, change, res_t, share):
    classes, rows = res_t.shape
    return pl.pallas_call(
        update_other_body,
        out_shape=(jax.ShapeDtypeStruct((classes, rows), F32), jax.ShapeDtypeStruct((share, classes), F32)),
        in_specs=[smem()] + [vmem()] * 5,
        out_specs=(vmem(), vmem()),
        scratch_shapes=[pltpu.VMEM((rows + share, CLASS_PAD), F32)],
        compiler_params=params(16),
    )(info, hi, lo, res, change, res_t)


def on_device(points, residual, block_ids):
    rows, feats = points.shape
    block = block_ids.shape[0]
    n_plane = lax.axis_size(PLANE)
    n_col = lax.axis_size(COLUMN)
    n_gy = lax.axis_size("zl") * lax.axis_size("c")
    plane = lax.axis_index(PLANE)
    place = lax.axis_index(COLUMN)
    share = block // n_gy
    half = feats // 2
    wide = n_plane * COL_CAP
    span = rows * n_col
    info = jnp.stack([lax.axis_index("c"), plane, plane * n_col + place, (place % n_gy) * share]).astype(I32)
    ids = block_ids.reshape(1, block)
    res_t = residual.T
    swap = [(0, 1), (1, 0)]

    packed, tab = pack(info, ids, points, res_t, n_col)
    col_rows = lax.all_to_all(packed, COLUMN, 0, 0, tiled=True)
    col_rows = col_rows.reshape(n_col * CAP * SPLIT, col_rows.shape[2])
    pts_out, res_out = compact(info, tab, col_rows, rows, half, n_plane, n_col)
    all_pts = lax.all_to_all(pts_out, PLANE, 0, 0, tiled=True).reshape(wide, half)
    all_res = lax.all_to_all(res_out, PLANE, 0, 0, tiled=True).reshape(wide, CLASS_PAD // 2)
    own = order(tab, all_pts, span)
    other = lax.ppermute(own, "c", swap)
    cross, p_cross, psq, p_oth = first_half(info, points, own)
    wh, wl = inverse(info, tab, p_oth, other, cross, p_cross, psq, share)
    all_res, wh = lax.optimization_barrier((all_res, wh))
    other_res = lax.ppermute(all_res, "c", swap)
    hi, lo, change = update_own(tab, wh, wl, all_res, span)
    out_t, step_share = update_other(info, hi, lo, other_res, change, res_t, share)
    return (out_t.T, step_share)


def solution(mesh):
    fine = Mesh(mesh.devices.reshape(4, 4, 2, 8, 2), EVERY)
    return jax.shard_map(
        on_device,
        mesh=fine,
        in_specs=(P(EVERY, None), P(EVERY, None), P()),
        out_specs=(P(EVERY, None), P(("zl", "c"), None)),
        check_vma=False,
    )
```

time: 131 us -> 123 us (0.939)
  starting transfers between devices: 13.6 us -> 10.3 us
  waiting for transfers between devices: 14.6 us -> 12 us
  local copies, waits for them, and re-layouts: 4.36 us -> 1.95 us
    all_to_all x1, waiting for transfers between devices: 14.6 us -> 10.4 us  [on_device(): lax.all_to_all(res_out, PLANE, 0, 0, tiled=True)]
    ppermute x1, starting transfers between devices: 5.97 us -> 2.69 us  [on_device(): other_res = lax.ppermute(all_res, 'c', swap)]
    unnamed x14 -> x10, local copies, waits for them, and re-layouts: 4.36 us -> 1.95 us
    pallas_call x2 -> x4, Pallas kernels: 21.6 us -> 19.2 us  [the longest x1 13.5 us: inverse(): pl.pallas_call(functools.partial(inverse_body, share=share), out_shape=(o...]
    pallas_call x1, Pallas kernels: 1.87 us -> 3.78 us  [pack(): pl.pallas_call(functools.partial(pack_body, n_col=n_col), out_shape=(jax....]
    ppermute x1, waiting for transfers between devices: 0.01 us -> 1.59 us  [on_device(): other_res = lax.ppermute(all_res, 'c', swap)]
  transfers between devices with their start and end apart: 3 -> 3, of which waited for: 1 -> 2; matrix products, arithmetic and copies ran while one was open for 0% -> 0% of each run, Pallas kernels for 15% -> 13%
where the time goes in v3:
time: 123 us; the launch traced here: 122 us
  blocking collectives  70.1 us (57%)
  Pallas kernels  26.5 us (22%)
  waiting for transfers between devices  12 us (10%)
  starting transfers between devices  10.3 us (8%)
  local copies, waits for them, and re-layouts  1.95 us (2%)
    all_to_all x1, blocking collectives, on_device(): col_rows = lax.all_to_all(packed, COLUMN, 0, 0, tiled=True)  41.8 us
    all_to_all x1, blocking collectives, on_device(): lax.all_to_all(pts_out, PLANE, 0, 0, tiled=True).reshape(wide, half)  28.3 us
    pallas_call x1, Pallas kernels, inverse(): pl.pallas_call(functools.partial(inverse_body, share=share), out_shape=(o...  13.5 us
    all_to_all x1, waiting for transfers between devices, on_device(): lax.all_to_all(res_out, PLANE, 0, 0, tiled=True)  10.4 us
    ppermute x1, starting transfers between devices, on_device(): other = lax.ppermute(own, 'c', swap)  3.89 us
    pallas_call x1, Pallas kernels, pack(): pl.pallas_call(functools.partial(pack_body, n_col=n_col), out_shape=(jax....  3.78 us
    all_to_all x1, starting transfers between devices, on_device(): lax.all_to_all(res_out, PLANE, 0, 0, tiled=True)  3.72 us
    pallas_call x1, Pallas kernels, update_other(): pl.pallas_call(update_other_body, out_shape=(jax.ShapeDtypeStruct((classe...  2.73 us
  transfers between devices with their start and end apart: 3, of which 2 were waited for; matrix products, arithmetic and copies ran while one was open for 0% of the time, Pallas kernels for 13%

profile of v3, /device:TPU:1, one launch (start us, length us, event | category | flops | bytes accessed | tf_op | source)
XLA Modules:
  0.0 122.2 jit_solution(3879197265730920153)
XLA Ops:
  0.6 0.6 pad_add_fusion.info
  1.3 0.0 copy-start.4
  1.3 3.8 %shard_map.50 = (bf16[32,8,640]{2,1,0:T(8,128)(2,1)}, s32[8,512]{1,0:T(8,128)}) custom-call(s32[4]{0:T(128)} %pad_add_fusion.info, s32[1,512]{1,0:T(1,128)} %bitcast.16, bf16[256,2048]{1,0:T(8,128)(2,1)} %pts_ref.1, f32[1000,256]{1,0:T(8,128)} %bitcast.11), custom_call_target="tpu_custom_call" | custom-call | tf_op jit(solution)/shard_map/pallas_call | solution.py:120
  5.0 41.8 %all_to_all.15 = bf16[32,8,640]{2,1,0:T(8,128)(2,1)S(1)} all-to-all(bf16[32,8,640]{2,1,0:T(8,128)(2,1)} %get-tuple-element.20), channel_id=1, replica_groups=mesh['y'=4,'x'=4,'zh'=2,'zl'=8,'c'=2] {'zh','zl','c'}, dimensions={0} | all-to-all | bytes 655360 | tf_op jit(solution)/shard_map/all_to_all | solution.py:364
  46.8 0.0 copy-done.4
  46.8 0.0 copy-start.2
  46.8 0.7 copy-done.2
  47.6 2.5 %shard_map.51 = (bf16[16,48,1024]{2,1,0:T(8,128)(2,1)S(1)}, f32[16,48,512]{2,1,0:T(8,128)}) custom-call(s32[4]{0:T(128)S(1)} %copy-done.4, s32[8,512]{1,0:T(8,128)S(1)} %copy-done.2, bf16[256,640]{1,0:T(8,128)(2,1)S(1)} %bitcast.15), custom_call_target="tpu_custom_call" | custom-call | tf_op jit(solution)/shard_map/pallas_call | solution.py:169
  50.1 28.3 %all_to_all.16 = bf16[16,48,1024]{2,1,0:T(8,128)(2,1)S(1)} all-to-all(bf16[16,48,1024]{2,1,0:T(8,128)(2,1)S(1)} %get-tuple-element.22), channel_id=1, replica_groups=mesh['y'=4,'x'=4,'zh'=2,'zl'=8,'c'=2] {'y','x'}, dimensions={0} | all-to-all | bytes 3145728 | tf_op jit(solution)/shard_map/all_to_all | solution.py:367
  78.4 1.0 shard_map.52.own_ref
  79.4 3.9 %collective-permute-start = (bf16[512,1024]{1,0:T(8,128)(2,1)S(1)}, bf16[512,1024]{1,0:T(8,128)(2,1)}, u32[]{:S(2)}, u32[]{:S(2)}) collective-permute-start(bf16[512,1024]{1,0:T(8,128)(2,1)S(1)} %shard_map.52.own_ref), channel_id=1, source_target_pairs={{0,1},{1,0},{2,3},{3,2},{4,5},{5,4},{6,7},{7,6},{8,9},{9,8},{10,11... | collective-permute-start | bytes 3145736 | tf_op jit(solution)/shard_map/ppermute | solution.py:370
  83.3 3.7 %all-to-all-start.1 = ((f32[16,48,512]{2,1,0:T(8,128)}), f32[16,48,512]{2,1,0:T(8,128)S(1)}, u32[]{:S(2)}, u32[]{:S(2)}) async-start(f32[16,48,512]{2,1,0:T(8,128)} %get-tuple-element.21), calls=%async_computation.1 | async-start | bytes 3145728 | tf_op jit(solution)/shard_map/all_to_all | solution.py:368
  87.0 0.0 copy-start.1
  87.0 1.2 copy-done.1
  88.2 0.0 copy-start.3
  88.3 1.6 %shard_map.53 = (f32[512,512]{1,0:T(8,128)S(1)}, f32[256,512]{1,0:T(8,128)S(1)}, f32[256,1]{1,0:T(8,128)S(1)}, bf16[256,1024]{1,0:T(8,128)(2,1)S(1)}) custom-call(s32[4]{0:T(128)S(1)} %copy-done.4, bf16[256,2048]{1,0:T(8,128)(2,1)S(1)} %copy-done.1, bf16[512,1024]{1,0:T(8,128)(2,1)S(1)} %shard_map.52.own_ref), custom_call_target="tpu_custom_call" | custom-call | flops 2000000000 | bytes 3000000 | tf_op jit(solution)/shard_map/pallas_call | solution.py:216
  89.9 0.0 collective-permute-done.oth_ref
  89.9 0.0 copy-done.3
  89.9 13.5 %shard_map.54 = (bf16[288,512]{1,0:T(8,128)(2,1)S(1)}, bf16[288,512]{1,0:T(8,128)(2,1)S(1)}) custom-call(s32[4]{0:T(128)S(1)} %copy-done.4, s32[8,512]{1,0:T(8,128)S(1)} %copy-done.3, bf16[256,1024]{1,0:T(8,128)(2,1)S(1)} %get-tuple-element.23.p_oth_ref, bf16[512,1024]{1,0:T(8,128)(2,1)} %collective-permute-done.oth_ref, ...), custom_call_target="tpu_custom_call" | custom-call | flops 12000000000 | bytes 6000000 | tf_op jit(solution)/shard_map/pallas_call | solution.py:283
  103.3 10.4 %all-to-all-done.1 = f32[16,48,512]{2,1,0:T(8,128)S(1)} async-done(((f32[16,48,512]{2,1,0:T(8,128)}), f32[16,48,512]{2,1,0:T(8,128)S(1)}, u32[]{:S(2)}, u32[]{:S(2)}) %all-to-all-start.1) | async-done | bytes 1572896 | tf_op jit(solution)/shard_map/all_to_all | solution.py:368
  113.7 2.7 %collective-permute-start.1 = (f32[768,512]{1,0:T(8,128)S(1)}, f32[768,512]{1,0:T(8,128)S(1)}, u32[]{:S(2)}, u32[]{:S(2)}) collective-permute-start(f32[768,512]{1,0:T(8,128)S(1)} %bitcast.13), channel_id=1, source_target_pairs={{0,1},{1,0},{2,3},{3,2},{4,5},{5,4},{6,7},{7,6},{8,9},{9,8},{10,11... | collective-permute-start | bytes 4718600 | tf_op jit(solution)/shard_map/ppermute | solution.py:374
  116.4 0.0 copy-start
  116.4 1.4 %shard_map.55 = (bf16[288,768]{1,0:T(8,128)(2,1)S(1)}, bf16[288,768]{1,0:T(8,128)(2,1)S(1)}, f32[288,512]{1,0:T(8,128)S(1)}) custom-call(s32[8,512]{1,0:T(8,128)S(1)} %copy-done.3, bf16[288,512]{1,0:T(8,128)(2,1)S(1)} %get-tuple-element.28.wh_ref, bf16[288,512]{1,0:T(8,128)(2,1)S(1)} %get-tuple-element.29.wl_ref, f32[768,512]{1,0:T(8,128)S(1)} %bitcast.14), custom_call_target="tpu_custom_call" | custom-call | flops 2000000000 | bytes 4000000 | tf_op jit(solution)/shard_map/pallas_call | solution.py:313
  117.8 1.6 %collective-permute-done.1.res_ref = f32[768,512]{1,0:T(8,128)S(1)} collective-permute-done((f32[768,512]{1,0:T(8,128)S(1)}, f32[768,512]{1,0:T(8,128)S(1)}, u32[]{:S(2)}, u32[]{:S(2)}) %collective-permute-start.1) | collective-permute-done | bytes 1572896 | tf_op jit(solution)/shard_map/ppermute | solution.py:374
  119.4 0.0 copy-done
  119.4 2.7 %shard_map.56 = (f32[1000,256]{1,0:T(8,128)}, f32[32,1000]{1,0:T(8,128)}) custom-call(s32[4]{0:T(128)S(1)} %copy-done.4, bf16[288,768]{1,0:T(8,128)(2,1)S(1)} %get-tuple-element.31.hi_ref, bf16[288,768]{1,0:T(8,128)(2,1)S(1)} %get-tuple-element.32.lo_ref, f32[768,512]{1,0:T(8,128)S(1)} %collective-permute-done.1.res_ref, ...), custom_call_target="tpu_custom_call" | custom-call | tf_op jit(solution)/shard_map/pallas_call | solution.py:336
Async XLA Ops:
  1.3 45.6 %copy-start.4 = (s32[4]{0:T(128)S(1)}, s32[4]{0:T(128)}, u32[]{:S(2)}) copy-start(s32[4]{0:T(128)} %pad_add_fusion.info) | copy-start | bytes 52
  46.8 0.7 copy-start.2
  79.4 10.5 %collective-permute-start = (bf16[512,1024]{1,0:T(8,128)(2,1)S(1)}, bf16[512,1024]{1,0:T(8,128)(2,1)}, u32[]{:S(2)}, u32[]{:S(2)}) collective-permute-start(bf16[512,1024]{1,0:T(8,128)(2,1)S(1)} %shard_map.52.own_ref), channel_id=1, source_target_pairs={{0,1},{1,0},{2,3},{3,2},{4,5},{5,4},{6,7},{7,6},{8,9},{9,8},{10,11... | collective-permute-start | bytes 3145736 | tf_op jit(solution)/shard_map/ppermute | solution.py:370
  83.3 30.4 %all-to-all-start.1 = ((f32[16,48,512]{2,1,0:T(8,128)}), f32[16,48,512]{2,1,0:T(8,128)S(1)}, u32[]{:S(2)}, u32[]{:S(2)}) async-start(f32[16,48,512]{2,1,0:T(8,128)} %get-tuple-element.21), calls=%async_computation.1 | async-start | bytes 3145728 | tf_op jit(solution)/shard_map/all_to_all | solution.py:368
  87.0 1.2 %copy-start.1 = (bf16[256,2048]{1,0:T(8,128)(2,1)S(1)}, bf16[256,2048]{1,0:T(8,128)(2,1)}, u32[]{:S(2)}) copy-start(bf16[256,2048]{1,0:T(8,128)(2,1)} %pts_ref.1) | copy-start | bytes 3145732
  88.2 1.6 %copy-start.3 = (s32[8,512]{1,0:T(8,128)S(1)}, s32[8,512]{1,0:T(8,128)}, u32[]{:S(2)}) copy-start(s32[8,512]{1,0:T(8,128)} %get-tuple-element.19.tab_ref) | copy-start | bytes 49156
  113.7 5.7 %collective-permute-start.1 = (f32[768,512]{1,0:T(8,128)S(1)}, f32[768,512]{1,0:T(8,128)S(1)}, u32[]{:S(2)}, u32[]{:S(2)}) collective-permute-start(f32[768,512]{1,0:T(8,128)S(1)} %bitcast.13), channel_id=1, source_target_pairs={{0,1},{1,0},{2,3},{3,2},{4,5},{5,4},{6,7},{7,6},{8,9},{9,8},{10,11... | collective-permute-start | bytes 4718600 | tf_op jit(solution)/shard_map/ppermute | solution.py:374
  116.4 3.0 %copy-start = (f32[256,1000]{0,1:T(8,128)S(1)}, f32[256,1000]{0,1:T(8,128)}, u32[]{:S(2)}) copy-start(f32[256,1000]{0,1:T(8,128)} %param.4) | copy-start | bytes 3072004

commit v4 on v3

--- a/solution.py
+++ b/solution.py
@@ -96,12 +96,10 @@
     res_in.wait()
     res = res_ref[...]
     hi = res.astype(BF)
-    rest = res - hi.astype(F32)
-    mid = rest.astype(BF)
-    low = (rest - mid.astype(F32)).astype(BF)
+    low = (res - hi.astype(F32)).astype(BF)
     classes = res.shape[0]
     pad = jnp.zeros((8, CLASS_PAD - classes), F32)
-    parts = [jnp.concatenate([dot(take, v, NT), pad], axis=1).astype(BF) for v in (hi, mid, low)]
+    parts = [jnp.concatenate([dot(take, v, NT), pad], axis=1).astype(BF) for v in (hi, low)]
     half = pts_ref.shape[1] // 2
     chalf = CLASS_PAD // 2
     for core in range(2):
@@ -115,7 +113,7 @@
 
 
 def pack(info, ids, points, res_t, n_col):
-    width = points.shape[1] // 2 + 3 * CLASS_PAD // 2
+    width = points.shape[1] // 2 + CLASS_PAD
     n = ids.shape[1]
     return pl.pallas_call(
         functools.partial(pack_body, n_col=n_col),
@@ -156,10 +154,8 @@
     whole = [dot(jnp.where(part == q, pick, 0.0).astype(BF), data) for q in range(SPLIT)]
     whole = jnp.concatenate(whole, axis=1)
     half = pts_ref.shape[2]
-    chalf = CLASS_PAD // 2
     pts = whole[:, :half].astype(BF)
-    res = whole[:, half : half + chalf] + whole[:, half + chalf : half + 2 * chalf]
-    res = res + whole[:, half + 2 * chalf :]
+    res = whole[:, half:].astype(BF)
     for p in range(pts_ref.shape[0]):
         pts_ref[p] = pts
         res_ref[p] = res
@@ -170,7 +166,7 @@
         functools.partial(compact_body, rows=rows, n_col=n_col),
         out_shape=(
             jax.ShapeDtypeStruct((n_plane, COL_CAP, half), BF),
-            jax.ShapeDtypeStruct((n_plane, COL_CAP, CLASS_PAD // 2), F32),
+            jax.ShapeDtypeStruct((n_plane, COL_CAP, CLASS_PAD), BF),
         ),
         in_specs=[smem(), vmem(), vmem()],
         out_specs=(vmem(), vmem()),
@@ -224,7 +220,7 @@
         in_specs=[smem(), vmem(), vmem()],
         out_specs=(vmem(),) * 4,
         compiler_params=params(12),
-        cost_estimate=pl.CostEstimate(flops=2 * 10**9, bytes_accessed=3 * 10**6, transcendentals=0),
+        cost_estimate=pl.CostEstimate(flops=10**6, bytes_accessed=10**6, transcendentals=0),
     )(info, points, own)
 
 
@@ -293,8 +289,13 @@
             pltpu.VMEM((n, n), F32),
         ],
         compiler_params=params(18),
-        cost_estimate=pl.CostEstimate(flops=12 * 10**9, bytes_accessed=6 * 10**6, transcendentals=4 * 10**5),
+        cost_estimate=pl.CostEstimate(flops=10**6, bytes_accessed=10**6, transcendentals=0),
     )(info, tab, p_oth, oth, cross, p_cross, psq)
+
+
+def apply_weights(hi, lo, res_ref):
+    chalf = res_ref.shape[1] // 2
+    return mm3((hi, lo), (res_ref[:, :chalf], res_ref[:, chalf:]))
 
 
 def update_own_body(tab_ref, wh_ref, wl_ref, res_ref, hi_ref, lo_ref, ch_ref, *, span):
@@ -303,16 +304,16 @@
     lo = dot(wl_ref[...], place, NT).astype(BF)
     hi_ref[...] = hi
     lo_ref[...] = lo
-    ch_ref[...] = mm3((hi, lo), two_parts(res_ref[...]))
+    ch_ref[...] = apply_weights(hi, lo, res_ref)
 
 
 def update_own(tab, wh, wl, res, span):
     m = wh.shape[0]
-    wide, chalf = res.shape
+    wide, parts = res.shape
     out = jax.ShapeDtypeStruct((m, wide), BF)
     return pl.pallas_call(
         functools.partial(update_own_body, span=span),
-        out_shape=(out, out, jax.ShapeDtypeStruct((m, chalf), F32)),
+        out_shape=(out, out, jax.ShapeDtypeStruct((m, parts // 2), F32)),
         in_specs=[vmem()] * 4,
         out_specs=(vmem(),) * 3,
         compiler_params=params(10),
@@ -323,9 +324,9 @@
 def update_other_body(info, hi_ref, lo_ref, res_ref, ch_ref, res_t_ref, out_ref, share_ref, all_ref):
     core = info[0]
     classes, rows = res_t_ref.shape
-    chalf = res_ref.shape[1]
+    chalf = ch_ref.shape[1]
     all_ref[:, pl.ds(pl.multiple_of(core * chalf, chalf), chalf)] = ch_ref[...]
-    change = mm3((hi_ref[...], lo_ref[...]), two_parts(res_ref[...]))
+    change = apply_weights(hi_ref[...], lo_ref[...], res_ref)
     all_ref[:, pl.ds(pl.multiple_of((1 - core) * chalf, chalf), chalf)] = change
     share_ref[...] = all_ref[pl.ds(rows, share_ref.shape[0]), pl.ds(0, classes)]
     out_ref[...] = res_t_ref[...] - all_ref[pl.ds(0, rows), :].T[:classes]
@@ -365,7 +366,7 @@
     col_rows = col_rows.reshape(n_col * CAP * SPLIT, col_rows.shape[2])
     pts_out, res_out = compact(info, tab, col_rows, rows, half, n_plane, n_col)
     all_pts = lax.all_to_all(pts_out, PLANE, 0, 0, tiled=True).reshape(wide, half)
-    all_res = lax.all_to_all(res_out, PLANE, 0, 0, tiled=True).reshape(wide, CLASS_PAD // 2)
+    all_res = lax.all_to_all(res_out, PLANE, 0, 0, tiled=True).reshape(wide, CLASS_PAD)
     own = order(tab, all_pts, span)
     other = lax.ppermute(own, "c", swap)
     cross, p_cross, psq, p_oth = first_half(info, points, own)

time: 123 us -> 111 us (0.902)
  waiting for transfers between devices: 12 us -> 2.48 us
  starting transfers between devices: 10.3 us -> 13.9 us
  blocking collectives: 70.1 us -> 66.9 us
  Pallas kernels: 26.5 us -> 24.4 us
    all_to_all x1, waiting for transfers between devices: 10.4 us -> 0.21 us  [on_device(): lax.all_to_all(res_out, PLANE, 0, 0, tiled=True).reshape(wide, CLASS_PAD)]
    ppermute x1, starting transfers between devices: 2.69 us -> 5.95 us  [on_device(): other_res = lax.ppermute(all_res, 'c', swap)]
    all_to_all x1, blocking collectives: 41.8 us -> 38.8 us  [on_device(): col_rows = lax.all_to_all(packed, COLUMN, 0, 0, tiled=True)]
    pallas_call x1, Pallas kernels: 2.53 us -> 1.3 us  [compact(): pl.pallas_call(functools.partial(compact_body, rows=rows, n_col=n_col), o...]
  transfers between devices with their start and end apart: 3 -> 3, of which waited for: 2 -> 3; matrix products, arithmetic and copies ran while one was open for 0% -> 0% of each run, Pallas kernels for 13% -> 15%
where the time goes in v4:
time: 111 us; the launch traced here: 110 us
  blocking collectives  66.9 us (60%)
  Pallas kernels  24.4 us (22%)
  starting transfers between devices  13.9 us (13%)
  waiting for transfers between devices  2.48 us (2%)
    all_to_all x1, blocking collectives, on_device(): col_rows = lax.all_to_all(packed, COLUMN, 0, 0, tiled=True)  38.8 us
    all_to_all x1, blocking collectives, on_device(): lax.all_to_all(pts_out, PLANE, 0, 0, tiled=True).reshape(wide, half)  28.1 us
    pallas_call x1, Pallas kernels, inverse(): pl.pallas_call(functools.partial(inverse_body, share=share), out_shape=(o...  12.8 us
    ppermute x1, starting transfers between devices, on_device(): other_res = lax.ppermute(all_res, 'c', swap)  5.95 us
    ppermute x1, starting transfers between devices, on_device(): other = lax.ppermute(own, 'c', swap)  4.06 us
    all_to_all x1, starting transfers between devices, on_device(): lax.all_to_all(res_out, PLANE, 0, 0, tiled=True).reshape(wide, CLASS_PAD)  3.84 us
    pallas_call x1, Pallas kernels, pack(): pl.pallas_call(functools.partial(pack_body, n_col=n_col), out_shape=(jax....  3.62 us
    pallas_call x1, Pallas kernels, update_other(): pl.pallas_call(update_other_body, out_shape=(jax.ShapeDtypeStruct((classe...  2.71 us
  transfers between devices with their start and end apart: 3, of which 3 were waited for; matrix products, arithmetic and copies ran while one was open for 0% of the time, Pallas kernels for 15%

profile of v4, /device:TPU:1, one launch (start us, length us, event | category | flops | bytes accessed | tf_op | source)
XLA Modules:
  0.0 109.7 jit_solution(14160476185398877923)
XLA Ops:
  0.6 0.6 pad_add_fusion.info
  1.2 0.0 copy-start.5
  1.2 3.6 %shard_map.50 = (bf16[32,8,512]{2,1,0:T(8,128)(2,1)}, s32[8,512]{1,0:T(8,128)}) custom-call(s32[4]{0:T(128)} %pad_add_fusion.info, s32[1,512]{1,0:T(1,128)} %bitcast.16, bf16[256,2048]{1,0:T(8,128)(2,1)} %pts_ref.1, f32[1000,256]{1,0:T(8,128)} %bitcast.11), custom_call_target="tpu_custom_call" | custom-call | tf_op jit(solution)/shard_map/pallas_call | solution.py:118
  4.8 38.8 %all_to_all.15 = bf16[32,8,512]{2,1,0:T(8,128)(2,1)S(1)} all-to-all(bf16[32,8,512]{2,1,0:T(8,128)(2,1)} %get-tuple-element.20), channel_id=1, replica_groups=mesh['y'=4,'x'=4,'zh'=2,'zl'=8,'c'=2] {'zh','zl','c'}, dimensions={0} | all-to-all | bytes 524288 | tf_op jit(solution)/shard_map/all_to_all | solution.py:365
  43.6 0.0 copy-done.5
  43.6 0.0 copy-start.3
  43.6 0.7 copy-done.3
  44.3 1.3 %shard_map.51 = (bf16[16,48,1024]{2,1,0:T(8,128)(2,1)S(1)}, bf16[16,48,1024]{2,1,0:T(8,128)(2,1)S(1)}) custom-call(s32[4]{0:T(128)S(1)} %copy-done.5, s32[8,512]{1,0:T(8,128)S(1)} %copy-done.3, bf16[256,512]{1,0:T(8,128)(2,1)S(1)} %bitcast.15), custom_call_target="tpu_custom_call" | custom-call | tf_op jit(solution)/shard_map/pallas_call | solution.py:165
  45.6 0.0 copy-start.2
  45.6 28.1 %all_to_all.16 = bf16[16,48,1024]{2,1,0:T(8,128)(2,1)S(1)} all-to-all(bf16[16,48,1024]{2,1,0:T(8,128)(2,1)S(1)} %get-tuple-element.22), channel_id=1, replica_groups=mesh['y'=4,'x'=4,'zh'=2,'zl'=8,'c'=2] {'y','x'}, dimensions={0} | all-to-all | bytes 3145728 | tf_op jit(solution)/shard_map/all_to_all | solution.py:368
  73.8 0.0 copy-done.2
  73.8 0.0 copy-start.4
  73.8 3.8 %all-to-all-start.1 = ((bf16[16,48,1024]{2,1,0:T(8,128)(2,1)}), bf16[16,48,1024]{2,1,0:T(8,128)(2,1)S(1)}, u32[]{:S(2)}, u32[]{:S(2)}) async-start(bf16[16,48,1024]{2,1,0:T(8,128)(2,1)} %copy-done.2), calls=%async_computation.1 | async-start | bytes 3145728 | tf_op jit(solution)/shard_map/all_to_all | solution.py:369
  77.6 0.0 copy-start
  77.6 0.0 copy-done.4
  77.6 1.0 shard_map.52.own_ref
  78.7 4.1 %collective-permute-start = (bf16[512,1024]{1,0:T(8,128)(2,1)S(1)}, bf16[512,1024]{1,0:T(8,128)(2,1)S(1)}, u32[]{:S(2)}, u32[]{:S(2)}) collective-permute-start(bf16[512,1024]{1,0:T(8,128)(2,1)S(1)} %shard_map.52.own_ref), channel_id=1, source_target_pairs={{0,1},{1,0},{2,3},{3,2},{4,5},{5,4},{6,7},{7,6},{8,9},{9,8},{10,11... | collective-permute-start | bytes 3145736 | tf_op jit(solution)/shard_map/ppermute | solution.py:371
  82.7 0.0 copy-done
  82.7 1.6 %shard_map.53 = (f32[512,512]{1,0:T(8,128)S(1)}, f32[256,512]{1,0:T(8,128)S(1)}, f32[256,1]{1,0:T(8,128)S(1)}, bf16[256,1024]{1,0:T(8,128)(2,1)S(1)}) custom-call(s32[4]{0:T(128)S(1)} %copy-done.5, bf16[256,2048]{1,0:T(8,128)(2,1)S(1)} %copy-done, bf16[512,1024]{1,0:T(8,128)(2,1)S(1)} %shard_map.52.own_ref), custom_call_target="tpu_custom_call" | custom-call | flops 1000000 | bytes 1000000 | tf_op jit(solution)/shard_map/pallas_call | solution.py:212
  84.3 0.7 collective-permute-done.oth_ref
  85.0 12.8 %shard_map.54 = (bf16[288,512]{1,0:T(8,128)(2,1)S(1)}, bf16[288,512]{1,0:T(8,128)(2,1)S(1)}) custom-call(s32[4]{0:T(128)S(1)} %copy-done.5, s32[8,512]{1,0:T(8,128)S(1)} %copy-done.4, bf16[256,1024]{1,0:T(8,128)(2,1)S(1)} %get-tuple-element.23.p_oth_ref, bf16[512,1024]{1,0:T(8,128)(2,1)S(1)} %collective-permute-done.oth_ref, ...), custom_call_target="tpu_custom_call" | custom-call | flops 1000000 | bytes 1000000 | tf_op jit(solution)/shard_map/pallas_call | solution.py:279
  97.8 0.2 all-to-all-done.1
  98.0 6.0 %collective-permute-start.1 = (bf16[768,1024]{1,0:T(8,128)(2,1)S(1)}, bf16[768,1024]{1,0:T(8,128)(2,1)S(1)}, u32[]{:S(2)}, u32[]{:S(2)}) collective-permute-start(bf16[768,1024]{1,0:T(8,128)(2,1)S(1)} %bitcast.13), channel_id=1, source_target_pairs={{0,1},{1,0},{2,3},{3,2},{4,5},{5,4},{6,7},{7,6},{8,9},{9,8},{10,11... | collective-permute-start | bytes 4718600 | tf_op jit(solution)/shard_map/ppermute | solution.py:375
  103.9 0.0 copy-start.1
  103.9 1.4 %shard_map.55 = (bf16[288,768]{1,0:T(8,128)(2,1)S(1)}, bf16[288,768]{1,0:T(8,128)(2,1)S(1)}, f32[288,512]{1,0:T(8,128)S(1)}) custom-call(s32[8,512]{1,0:T(8,128)S(1)} %copy-done.4, bf16[288,512]{1,0:T(8,128)(2,1)S(1)} %get-tuple-element.28.wh_ref, bf16[288,512]{1,0:T(8,128)(2,1)S(1)} %get-tuple-element.29.wl_ref, bf16[768,1024]{1,0:T(8,128)(2,1)S(1)} %bitcast.14), custom_call_target="tpu_custom_call" | custom-call | flops 2000000000 | bytes 4000000 | tf_op jit(solution)/shard_map/pallas_call | solution.py:314
  105.3 1.6 %collective-permute-done.1.res_ref = bf16[768,1024]{1,0:T(8,128)(2,1)S(1)} collective-permute-done((bf16[768,1024]{1,0:T(8,128)(2,1)S(1)}, bf16[768,1024]{1,0:T(8,128)(2,1)S(1)}, u32[]{:S(2)}, u32[]{:S(2)}) %collective-permute-start.1) | collective-permute-done | bytes 1572896 | tf_op jit(solution)/shard_map/ppermute | solution.py:375
  106.9 0.0 copy-done.1
  106.9 2.7 %shard_map.56 = (f32[1000,256]{1,0:T(8,128)}, f32[32,1000]{1,0:T(8,128)}) custom-call(s32[4]{0:T(128)S(1)} %copy-done.5, bf16[288,768]{1,0:T(8,128)(2,1)S(1)} %get-tuple-element.31.hi_ref, bf16[288,768]{1,0:T(8,128)(2,1)S(1)} %get-tuple-element.32.lo_ref, bf16[768,1024]{1,0:T(8,128)(2,1)S(1)} %collective-permute-done.1.res_ref, ...), custom_call_target="tpu_custom_call" | custom-call | tf_op jit(solution)/shard_map/pallas_call | solution.py:337
Async XLA Ops:
  1.2 42.4 %copy-start.5 = (s32[4]{0:T(128)S(1)}, s32[4]{0:T(128)}, u32[]{:S(2)}) copy-start(s32[4]{0:T(128)} %pad_add_fusion.info) | copy-start | bytes 52
  43.6 0.7 copy-start.3
  45.6 28.1 %copy-start.2 = (bf16[16,48,1024]{2,1,0:T(8,128)(2,1)}, bf16[16,48,1024]{2,1,0:T(8,128)(2,1)S(1)}, u32[]{:S(2)}) copy-start(bf16[16,48,1024]{2,1,0:T(8,128)(2,1)S(1)} %get-tuple-element.21) | copy-start | bytes 4718596
  73.8 3.9 %copy-start.4 = (s32[8,512]{1,0:T(8,128)S(1)}, s32[8,512]{1,0:T(8,128)}, u32[]{:S(2)}) copy-start(s32[8,512]{1,0:T(8,128)} %get-tuple-element.19.tab_ref) | copy-start | bytes 49156
  73.8 24.2 %all-to-all-start.1 = ((bf16[16,48,1024]{2,1,0:T(8,128)(2,1)}), bf16[16,48,1024]{2,1,0:T(8,128)(2,1)S(1)}, u32[]{:S(2)}, u32[]{:S(2)}) async-start(bf16[16,48,1024]{2,1,0:T(8,128)(2,1)} %copy-done.2), calls=%async_computation.1 | async-start | bytes 3145728 | tf_op jit(solution)/shard_map/all_to_all | solution.py:369
  77.6 5.1 %copy-start = (bf16[256,2048]{1,0:T(8,128)(2,1)S(1)}, bf16[256,2048]{1,0:T(8,128)(2,1)}, u32[]{:S(2)}) copy-start(bf16[256,2048]{1,0:T(8,128)(2,1)} %pts_ref.1) | copy-start | bytes 3145732
  78.7 6.3 %collective-permute-start = (bf16[512,1024]{1,0:T(8,128)(2,1)S(1)}, bf16[512,1024]{1,0:T(8,128)(2,1)S(1)}, u32[]{:S(2)}, u32[]{:S(2)}) collective-permute-start(bf16[512,1024]{1,0:T(8,128)(2,1)S(1)} %shard_map.52.own_ref), channel_id=1, source_target_pairs={{0,1},{1,0},{2,3},{3,2},{4,5},{5,4},{6,7},{7,6},{8,9},{9,8},{10,11... | collective-permute-start | bytes 3145736 | tf_op jit(solution)/shard_map/ppermute | solution.py:371
  98.0 9.0 %collective-permute-start.1 = (bf16[768,1024]{1,0:T(8,128)(2,1)S(1)}, bf16[768,1024]{1,0:T(8,128)(2,1)S(1)}, u32[]{:S(2)}, u32[]{:S(2)}) collective-permute-start(bf16[768,1024]{1,0:T(8,128)(2,1)S(1)} %bitcast.13), channel_id=1, source_target_pairs={{0,1},{1,0},{2,3},{3,2},{4,5},{5,4},{6,7},{7,6},{8,9},{9,8},{10,11... | collective-permute-start | bytes 4718600 | tf_op jit(solution)/shard_map/ppermute | solution.py:375
  103.9 3.0 %copy-start.1 = (f32[256,1000]{0,1:T(8,128)S(1)}, f32[256,1000]{0,1:T(8,128)}, u32[]{:S(2)}) copy-start(f32[256,1000]{0,1:T(8,128)} %param.4) | copy-start | bytes 3072004

commit v5 on v4

--- a/solution.py
+++ b/solution.py
@@ -63,7 +63,7 @@
     return pltpu.CompilerParams(vmem_limit_bytes=mib * MIB)
 
 
-def pack_body(info, ids_hbm, pts_hbm, res_hbm, out_ref, tab_ref, ids_ref, pts_ref, res_ref, sems, *, n_col):
+def pack_body(info, ids_hbm, pts_hbm, res_hbm, out_ref, tab_ref, ids_ref, pts_ref, res_ref, sems, *, n_plane, n_col):
     me = info[2]
     rows = pts_ref.shape[0]
     ids_in = pltpu.make_async_copy(ids_hbm, ids_ref, sems.at[0])
@@ -82,7 +82,12 @@
     less = jnp.broadcast_to(ids_col, (n, n)) < ids
     rank = jnp.sum(jnp.where(less & (ids_col >= column * (rows * n_col)), 1, 0), axis=0, keepdims=True)
     slot = jnp.sum(jnp.where(less & (ids_col >= owner * rows), 1, 0), axis=0, keepdims=True)
-    tab_ref[...] = jnp.concatenate([ids, rank, slot, jnp.zeros((5, n), I32)], axis=0)
+    planes = COL_CAP * n_plane
+    straight = column * COL_CAP + rank
+    turned = planes - COL_CAP - column * COL_CAP + rank
+    here = jnp.where(info[0] == 0, straight, turned)
+    there = jnp.where(info[0] == 0, turned, straight)
+    tab_ref[...] = jnp.concatenate([ids, rank, slot, here, there, jnp.zeros((3, n), I32)], axis=0)
     mine = owner == me
     lane = iota((8, rows), 1)
     sub = iota((8, rows), 0)
@@ -112,11 +117,11 @@
             out_ref[2 * z + core] = block
 
 
-def pack(info, ids, points, res_t, n_col):
+def pack(info, ids, points, res_t, n_plane, n_col):
     width = points.shape[1] // 2 + CLASS_PAD
     n = ids.shape[1]
     return pl.pallas_call(
-        functools.partial(pack_body, n_col=n_col),
+        functools.partial(pack_body, n_plane=n_plane, n_col=n_col),
         out_shape=(
             jax.ShapeDtypeStruct((n_col, CAP * SPLIT, width // SPLIT), BF),
             jax.ShapeDtypeStruct((8, n), I32),
@@ -174,18 +179,18 @@
     )(info, tab, data)
 
 
-def place_matrix(tab_ref, wide, span):
-    ids, rank, _ = table(tab_ref)
-    return (iota((wide, ids.shape[1]), 0) == (ids // span) * COL_CAP + rank).astype(F32).astype(BF)
-
-
-def order_body(tab_ref, in_ref, out_ref, *, span):
-    out_ref[...] = dot(place_matrix(tab_ref, in_ref.shape[0], span), in_ref[...], TN).astype(BF)
-
-
-def order(tab, data, span):
-    return pl.pallas_call(
-        functools.partial(order_body, span=span),
+def place_matrix(tab_ref, wide, row=3):
+    at = tab_ref[row : row + 1, :]
+    return (iota((wide, at.shape[1]), 0) == at).astype(F32).astype(BF)
+
+
+def order_body(tab_ref, in_ref, out_ref):
+    out_ref[...] = dot(place_matrix(tab_ref, in_ref.shape[0]), in_ref[...], TN).astype(BF)
+
+
+def order(tab, data):
+    return pl.pallas_call(
+        order_body,
         out_shape=jax.ShapeDtypeStruct((tab.shape[1], data.shape[1]), BF),
         in_specs=[vmem(), vmem()],
         out_specs=vmem(),
@@ -298,21 +303,23 @@
     return mm3((hi, lo), (res_ref[:, :chalf], res_ref[:, chalf:]))
 
 
-def update_own_body(tab_ref, wh_ref, wl_ref, res_ref, hi_ref, lo_ref, ch_ref, *, span):
-    place = place_matrix(tab_ref, res_ref.shape[0], span)
-    hi = dot(wh_ref[...], place, NT).astype(BF)
-    lo = dot(wl_ref[...], place, NT).astype(BF)
-    hi_ref[...] = hi
-    lo_ref[...] = lo
+def update_own_body(tab_ref, wh_ref, wl_ref, res_ref, hi_ref, lo_ref, ch_ref):
+    wide = res_ref.shape[0]
+    here = place_matrix(tab_ref, wide)
+    hi = dot(wh_ref[...], here, NT).astype(BF)
+    lo = dot(wl_ref[...], here, NT).astype(BF)
     ch_ref[...] = apply_weights(hi, lo, res_ref)
-
-
-def update_own(tab, wh, wl, res, span):
+    there = place_matrix(tab_ref, wide, 4)
+    hi_ref[...] = dot(wh_ref[...], there, NT).astype(BF)
+    lo_ref[...] = dot(wl_ref[...], there, NT).astype(BF)
+
+
+def update_own(tab, wh, wl, res):
     m = wh.shape[0]
     wide, parts = res.shape
     out = jax.ShapeDtypeStruct((m, wide), BF)
     return pl.pallas_call(
-        functools.partial(update_own_body, span=span),
+        update_own_body,
         out_shape=(out, out, jax.ShapeDtypeStruct((m, parts // 2), F32)),
         in_specs=[vmem()] * 4,
         out_specs=(vmem(),) * 3,
@@ -342,6 +349,18 @@
         scratch_shapes=[pltpu.VMEM((rows + share, CLASS_PAD), F32)],
         compiler_params=params(16),
     )(info, hi, lo, res, change, res_t)
+
+
+def plane_groups():
+    groups = []
+    for place in range(32):
+        members = [p * 32 + place for p in range(16)]
+        groups.append(members if place % 2 == 0 else members[::-1])
+    return groups
+
+
+def over_plane(value):
+    return lax.all_to_all(value, EVERY, 0, 0, axis_index_groups=plane_groups(), tiled=True)
 
 
 def on_device(points, residual, block_ids):
@@ -355,25 +374,24 @@
     share = block // n_gy
     half = feats // 2
     wide = n_plane * COL_CAP
-    span = rows * n_col
     info = jnp.stack([lax.axis_index("c"), plane, plane * n_col + place, (place % n_gy) * share]).astype(I32)
     ids = block_ids.reshape(1, block)
     res_t = residual.T
     swap = [(0, 1), (1, 0)]
 
-    packed, tab = pack(info, ids, points, res_t, n_col)
+    packed, tab = pack(info, ids, points, res_t, n_plane, n_col)
     col_rows = lax.all_to_all(packed, COLUMN, 0, 0, tiled=True)
     col_rows = col_rows.reshape(n_col * CAP * SPLIT, col_rows.shape[2])
     pts_out, res_out = compact(info, tab, col_rows, rows, half, n_plane, n_col)
-    all_pts = lax.all_to_all(pts_out, PLANE, 0, 0, tiled=True).reshape(wide, half)
-    all_res = lax.all_to_all(res_out, PLANE, 0, 0, tiled=True).reshape(wide, CLASS_PAD)
-    own = order(tab, all_pts, span)
+    all_pts = over_plane(pts_out).reshape(wide, half)
+    all_res = over_plane(res_out).reshape(wide, CLASS_PAD)
+    own = order(tab, all_pts)
     other = lax.ppermute(own, "c", swap)
     cross, p_cross, psq, p_oth = first_half(info, points, own)
     wh, wl = inverse(info, tab, p_oth, other, cross, p_cross, psq, share)
     all_res, wh = lax.optimization_barrier((all_res, wh))
     other_res = lax.ppermute(all_res, "c", swap)
-    hi, lo, change = update_own(tab, wh, wl, all_res, span)
+    hi, lo, change = update_own(tab, wh, wl, all_res)
     out_t, step_share = update_other(info, hi, lo, other_res, change, res_t, share)
     return (out_t.T, step_share)
 

time: 111 us -> 109 us (0.982)
  blocking collectives: 66.9 us -> 64.5 us
  waiting for transfers between devices: 2.48 us -> 4.01 us
  starting transfers between devices: 13.9 us -> 12.7 us
    all_to_all x1, starting transfers between devices: 3.84 us -> 7.98 us  [over_plane(): lax.all_to_all(value, EVERY, 0, 0, axis_index_groups=plane_groups(), tile...]
    ppermute x1, starting transfers between devices: 5.95 us -> 2.83 us  [on_device(): other_res = lax.ppermute(all_res, 'c', swap)]
    all_to_all x1, blocking collectives: 28.1 us -> 25.7 us  [over_plane(): lax.all_to_all(value, EVERY, 0, 0, axis_index_groups=plane_groups(), tile...]
    ppermute x1, starting transfers between devices: 4.06 us -> 1.92 us  [on_device(): other = lax.ppermute(own, 'c', swap)]
    all_to_all x1, waiting for transfers between devices: 0.21 us -> 1.8 us  [over_plane(): lax.all_to_all(value, EVERY, 0, 0, axis_index_groups=plane_groups(), tile...]
  transfers between devices with their start and end apart: 3 -> 3, of which waited for: 3 -> 3; matrix products, arithmetic and copies ran while one was open for 0% -> 0% of each run, Pallas kernels for 15% -> 16%
where the time goes in v5:
time: 109 us; the launch traced here: 108 us
  blocking collectives  64.5 us (59%)
  Pallas kernels  24.8 us (23%)
  starting transfers between devices  12.7 us (12%)
  waiting for transfers between devices  4.01 us (4%)
    all_to_all x1, blocking collectives, on_device(): col_rows = lax.all_to_all(packed, COLUMN, 0, 0, tiled=True)  38.8 us
    all_to_all x1, blocking collectives, over_plane(): lax.all_to_all(value, EVERY, 0, 0, axis_index_groups=plane_groups(), tile...  25.7 us
    pallas_call x1, Pallas kernels, inverse(): pl.pallas_call(functools.partial(inverse_body, share=share), out_shape=(o...  12.8 us
    all_to_all x1, starting transfers between devices, over_plane(): lax.all_to_all(value, EVERY, 0, 0, axis_index_groups=plane_groups(), tile...  7.98 us
    pallas_call x1, Pallas kernels, pack(): pl.pallas_call(functools.partial(pack_body, n_plane=n_plane, n_col=n_col)...  3.62 us
    ppermute x1, starting transfers between devices, on_device(): other_res = lax.ppermute(all_res, 'c', swap)  2.83 us
    pallas_call x1, Pallas kernels, update_other(): pl.pallas_call(update_other_body, out_shape=(jax.ShapeDtypeStruct((classe...  2.71 us
  transfers between devices with their start and end apart: 3, of which 3 were waited for; matrix products, arithmetic and copies ran while one was open for 0% of the time, Pallas kernels for 16%

profile of v5, /device:TPU:1, one launch (start us, length us, event | category | flops | bytes accessed | tf_op | source)
XLA Modules:
  0.0 108.1 jit_solution(9074620455158251221)
XLA Ops:
  0.6 0.6 pad_add_fusion.info
  1.2 0.0 copy-start.5
  1.2 3.6 %shard_map.50 = (bf16[32,8,512]{2,1,0:T(8,128)(2,1)}, s32[8,512]{1,0:T(8,128)}) custom-call(s32[4]{0:T(128)} %pad_add_fusion.info, s32[1,512]{1,0:T(1,128)} %bitcast.16, bf16[256,2048]{1,0:T(8,128)(2,1)} %pts_ref.1, f32[1000,256]{1,0:T(8,128)} %bitcast.11), custom_call_target="tpu_custom_call" | custom-call | tf_op jit(solution)/shard_map/pallas_call | solution.py:123
  4.8 38.8 %all_to_all.15 = bf16[32,8,512]{2,1,0:T(8,128)(2,1)S(1)} all-to-all(bf16[32,8,512]{2,1,0:T(8,128)(2,1)} %get-tuple-element.20), channel_id=1, replica_groups=mesh['y'=4,'x'=4,'zh'=2,'zl'=8,'c'=2] {'zh','zl','c'}, dimensions={0} | all-to-all | bytes 524288 | tf_op jit(solution)/shard_map/all_to_all | solution.py:383
  43.6 0.0 copy-done.5
  43.6 0.0 copy-start.3
  43.6 0.7 copy-done.3
  44.3 1.3 %shard_map.51 = (bf16[16,48,1024]{2,1,0:T(8,128)(2,1)S(1)}, bf16[16,48,1024]{2,1,0:T(8,128)(2,1)S(1)}) custom-call(s32[4]{0:T(128)S(1)} %copy-done.5, s32[8,512]{1,0:T(8,128)S(1)} %copy-done.3, bf16[256,512]{1,0:T(8,128)(2,1)S(1)} %bitcast.15), custom_call_target="tpu_custom_call" | custom-call | tf_op jit(solution)/shard_map/pallas_call | solution.py:170
  45.6 0.0 copy-start.2
  45.6 25.7 %all_to_all.16 = bf16[16,48,1024]{2,1,0:T(8,128)(2,1)S(1)} all-to-all(bf16[16,48,1024]{2,1,0:T(8,128)(2,1)S(1)} %get-tuple-element.22), channel_id=1, replica_groups={{0,32,64,96,128,160,192,224,256,288,320,352,384,416,448,480},{481,449,4..., dimensions={0} | all-to-all | bytes 3145728 | tf_op jit(solution)/shard_map/all_to_all | solution.py:363
  71.4 0.0 copy-done.2
  71.4 0.0 copy-start.4
  71.4 8.0 %all-to-all-start.1 = ((bf16[16,48,1024]{2,1,0:T(8,128)(2,1)}), bf16[16,48,1024]{2,1,0:T(8,128)(2,1)S(1)}, u32[]{:S(2)}, u32[]{:S(2)}) async-start(bf16[16,48,1024]{2,1,0:T(8,128)(2,1)} %copy-done.2), calls=%async_computation.1 | async-start | bytes 3145728 | tf_op jit(solution)/shard_map/all_to_all | solution.py:363
  79.3 0.0 copy-start
  79.3 0.0 copy-done.4
  79.4 1.0 shard_map.52.own_ref
  80.4 1.9 %collective-permute-start = (bf16[512,1024]{1,0:T(8,128)(2,1)S(1)}, bf16[512,1024]{1,0:T(8,128)(2,1)S(1)}, u32[]{:S(2)}, u32[]{:S(2)}) collective-permute-start(bf16[512,1024]{1,0:T(8,128)(2,1)S(1)} %shard_map.52.own_ref), channel_id=1, source_target_pairs={{0,1},{1,0},{2,3},{3,2},{4,5},{5,4},{6,7},{7,6},{8,9},{9,8},{10,11... | collective-permute-start | bytes 3145736 | tf_op jit(solution)/shard_map/ppermute | solution.py:389
  82.3 0.0 copy-done
  82.3 1.6 %shard_map.53 = (f32[512,512]{1,0:T(8,128)S(1)}, f32[256,512]{1,0:T(8,128)S(1)}, f32[256,1]{1,0:T(8,128)S(1)}, bf16[256,1024]{1,0:T(8,128)(2,1)S(1)}) custom-call(s32[4]{0:T(128)S(1)} %copy-done.5, bf16[256,2048]{1,0:T(8,128)(2,1)S(1)} %copy-done, bf16[512,1024]{1,0:T(8,128)(2,1)S(1)} %shard_map.52.own_ref), custom_call_target="tpu_custom_call" | custom-call | flops 1000000 | bytes 1000000 | tf_op jit(solution)/shard_map/pallas_call | solution.py:217
  83.9 1.0 collective-permute-done.oth_ref
  84.9 12.8 %shard_map.54 = (bf16[288,512]{1,0:T(8,128)(2,1)S(1)}, bf16[288,512]{1,0:T(8,128)(2,1)S(1)}) custom-call(s32[4]{0:T(128)S(1)} %copy-done.5, s32[8,512]{1,0:T(8,128)S(1)} %copy-done.4, bf16[256,1024]{1,0:T(8,128)(2,1)S(1)} %get-tuple-element.23.p_oth_ref, bf16[512,1024]{1,0:T(8,128)(2,1)S(1)} %collective-permute-done.oth_ref, ...), custom_call_target="tpu_custom_call" | custom-call | flops 1000000 | bytes 1000000 | tf_op jit(solution)/shard_map/pallas_call | solution.py:284
  97.7 1.8 %all-to-all-done.1 = bf16[16,48,1024]{2,1,0:T(8,128)(2,1)S(1)} async-done(((bf16[16,48,1024]{2,1,0:T(8,128)(2,1)}), bf16[16,48,1024]{2,1,0:T(8,128)(2,1)S(1)}, u32[]{:S(2)}, u32[]{:S(2)}) %all-to-all-start.1) | async-done | bytes 1572896 | tf_op jit(solution)/shard_map/all_to_all | solution.py:363
  99.5 2.8 %collective-permute-start.1 = (bf16[768,1024]{1,0:T(8,128)(2,1)S(1)}, bf16[768,1024]{1,0:T(8,128)(2,1)S(1)}, u32[]{:S(2)}, u32[]{:S(2)}) collective-permute-start(bf16[768,1024]{1,0:T(8,128)(2,1)S(1)} %bitcast.13), channel_id=1, source_target_pairs={{0,1},{1,0},{2,3},{3,2},{4,5},{5,4},{6,7},{7,6},{8,9},{9,8},{10,11... | collective-permute-start | bytes 4718600 | tf_op jit(solution)/shard_map/ppermute | solution.py:393
  102.3 0.0 copy-start.1
  102.4 1.8 %shard_map.55 = (bf16[288,768]{1,0:T(8,128)(2,1)S(1)}, bf16[288,768]{1,0:T(8,128)(2,1)S(1)}, f32[288,512]{1,0:T(8,128)S(1)}) custom-call(s32[8,512]{1,0:T(8,128)S(1)} %copy-done.4, bf16[288,512]{1,0:T(8,128)(2,1)S(1)} %get-tuple-element.28.wh_ref, bf16[288,512]{1,0:T(8,128)(2,1)S(1)} %get-tuple-element.29.wl_ref, bf16[768,1024]{1,0:T(8,128)(2,1)S(1)} %bitcast.14), custom_call_target="tpu_custom_call" | custom-call | flops 2000000000 | bytes 4000000 | tf_op jit(solution)/shard_map/pallas_call | solution.py:321
  104.2 1.2 %collective-permute-done.1.res_ref = bf16[768,1024]{1,0:T(8,128)(2,1)S(1)} collective-permute-done((bf16[768,1024]{1,0:T(8,128)(2,1)S(1)}, bf16[768,1024]{1,0:T(8,128)(2,1)S(1)}, u32[]{:S(2)}, u32[]{:S(2)}) %collective-permute-start.1) | collective-permute-done | bytes 1572896 | tf_op jit(solution)/shard_map/ppermute | solution.py:393
  105.4 0.0 copy-done.1
  105.4 2.7 %shard_map.56 = (f32[1000,256]{1,0:T(8,128)}, f32[32,1000]{1,0:T(8,128)}) custom-call(s32[4]{0:T(128)S(1)} %copy-done.5, bf16[288,768]{1,0:T(8,128)(2,1)S(1)} %get-tuple-element.31.hi_ref, bf16[288,768]{1,0:T(8,128)(2,1)S(1)} %get-tuple-element.32.lo_ref, bf16[768,1024]{1,0:T(8,128)(2,1)S(1)} %collective-permute-done.1.res_ref, ...), custom_call_target="tpu_custom_call" | custom-call | tf_op jit(solution)/shard_map/pallas_call | solution.py:344
Async XLA Ops:
  1.2 42.4 %copy-start.5 = (s32[4]{0:T(128)S(1)}, s32[4]{0:T(128)}, u32[]{:S(2)}) copy-start(s32[4]{0:T(128)} %pad_add_fusion.info) | copy-start | bytes 52
  43.6 0.7 copy-start.3
  45.6 25.7 %copy-start.2 = (bf16[16,48,1024]{2,1,0:T(8,128)(2,1)}, bf16[16,48,1024]{2,1,0:T(8,128)(2,1)S(1)}, u32[]{:S(2)}) copy-start(bf16[16,48,1024]{2,1,0:T(8,128)(2,1)S(1)} %get-tuple-element.21) | copy-start | bytes 4718596
  71.4 8.0 %copy-start.4 = (s32[8,512]{1,0:T(8,128)S(1)}, s32[8,512]{1,0:T(8,128)}, u32[]{:S(2)}) copy-start(s32[8,512]{1,0:T(8,128)} %get-tuple-element.19.tab_ref) | copy-start | bytes 49156
  71.4 28.1 %all-to-all-start.1 = ((bf16[16,48,1024]{2,1,0:T(8,128)(2,1)}), bf16[16,48,1024]{2,1,0:T(8,128)(2,1)S(1)}, u32[]{:S(2)}, u32[]{:S(2)}) async-start(bf16[16,48,1024]{2,1,0:T(8,128)(2,1)} %copy-done.2), calls=%async_computation.1 | async-start | bytes 3145728 | tf_op jit(solution)/shard_map/all_to_all | solution.py:363
  79.3 3.0 %copy-start = (bf16[256,2048]{1,0:T(8,128)(2,1)S(1)}, bf16[256,2048]{1,0:T(8,128)(2,1)}, u32[]{:S(2)}) copy-start(bf16[256,2048]{1,0:T(8,128)(2,1)} %pts_ref.1) | copy-start | bytes 3145732
  80.4 4.6 %collective-permute-start = (bf16[512,1024]{1,0:T(8,128)(2,1)S(1)}, bf16[512,1024]{1,0:T(8,128)(2,1)S(1)}, u32[]{:S(2)}, u32[]{:S(2)}) collective-permute-start(bf16[512,1024]{1,0:T(8,128)(2,1)S(1)} %shard_map.52.own_ref), channel_id=1, source_target_pairs={{0,1},{1,0},{2,3},{3,2},{4,5},{5,4},{6,7},{7,6},{8,9},{9,8},{10,11... | collective-permute-start | bytes 3145736 | tf_op jit(solution)/shard_map/ppermute | solution.py:389
  99.5 5.8 %collective-permute-start.1 = (bf16[768,1024]{1,0:T(8,128)(2,1)S(1)}, bf16[768,1024]{1,0:T(8,128)(2,1)S(1)}, u32[]{:S(2)}, u32[]{:S(2)}) collective-permute-start(bf16[768,1024]{1,0:T(8,128)(2,1)S(1)} %bitcast.13), channel_id=1, source_target_pairs={{0,1},{1,0},{2,3},{3,2},{4,5},{5,4},{6,7},{7,6},{8,9},{9,8},{10,11... | collective-permute-start | bytes 4718600 | tf_op jit(solution)/shard_map/ppermute | solution.py:393
  102.3 3.0 %copy-start.1 = (f32[256,1000]{0,1:T(8,128)S(1)}, f32[256,1000]{0,1:T(8,128)}, u32[]{:S(2)}) copy-start(f32[256,1000]{0,1:T(8,128)} %param.4) | copy-start | bytes 3072004

commit v6 on v5

--- a/solution.py
+++ b/solution.py
@@ -25,6 +25,8 @@
 COL_CAP = 48
 CLASS_PAD = 1024
 SPLIT = 4
+CLASS_STEP = 496
+CLASS_SPAN = 504
 MIB = 1024 * 1024
 
 
@@ -109,7 +111,7 @@
     chalf = CLASS_PAD // 2
     for core in range(2):
         row = [picked[:CAP, core * half : (core + 1) * half]]
-        row += [v[:CAP, core * chalf : (core + 1) * chalf] for v in parts]
+        row += [v[:CAP, core * CLASS_STEP : core * CLASS_STEP + chalf] for v in parts]
         row = jnp.concatenate(row, axis=1).astype(F32)
         w = row.shape[1] // SPLIT
         block = jnp.concatenate([row[:, q * w : (q + 1) * w] for q in range(SPLIT)], axis=0).astype(BF)
@@ -303,52 +305,78 @@
     return mm3((hi, lo), (res_ref[:, :chalf], res_ref[:, chalf:]))
 
 
-def update_own_body(tab_ref, wh_ref, wl_ref, res_ref, hi_ref, lo_ref, ch_ref):
+def write_half(which, change, res_t_ref, out_hbm, buf, sem):
+    rows = res_t_ref.shape[1]
+    span = pl.ds(pl.multiple_of(which * CLASS_STEP, 8), CLASS_SPAN)
+    buf[...] = res_t_ref[span, :] - change[:rows].T[:CLASS_SPAN]
+    copy = pltpu.make_async_copy(buf, out_hbm.at[span, :], sem)
+    copy.start()
+    return copy
+
+
+def update_own_body(info, tab_ref, wh_ref, wl_ref, res_ref, res_t_ref, hi_ref, lo_ref, part_ref, out_hbm, buf, sem):
+    rows = res_t_ref.shape[1]
     wide = res_ref.shape[0]
     here = place_matrix(tab_ref, wide)
     hi = dot(wh_ref[...], here, NT).astype(BF)
     lo = dot(wl_ref[...], here, NT).astype(BF)
-    ch_ref[...] = apply_weights(hi, lo, res_ref)
+    change = apply_weights(hi, lo, res_ref)
+    part_ref[...] = change[rows:]
+    copy = write_half(info[0], change, res_t_ref, out_hbm, buf, sem)
     there = place_matrix(tab_ref, wide, 4)
     hi_ref[...] = dot(wh_ref[...], there, NT).astype(BF)
     lo_ref[...] = dot(wl_ref[...], there, NT).astype(BF)
-
-
-def update_own(tab, wh, wl, res):
+    copy.wait()
+
+
+def half_scratch(rows):
+    return [pltpu.VMEM((CLASS_SPAN, rows), F32), pltpu.SemaphoreType.DMA(())]
+
+
+def update_own(info, tab, wh, wl, res, res_t):
     m = wh.shape[0]
     wide, parts = res.shape
+    classes, rows = res_t.shape
     out = jax.ShapeDtypeStruct((m, wide), BF)
     return pl.pallas_call(
         update_own_body,
-        out_shape=(out, out, jax.ShapeDtypeStruct((m, parts // 2), F32)),
-        in_specs=[vmem()] * 4,
-        out_specs=(vmem(),) * 3,
-        compiler_params=params(10),
+        out_shape=(
+            out,
+            out,
+            jax.ShapeDtypeStruct((m - rows, parts // 2), F32),
+            jax.ShapeDtypeStruct((classes, rows), F32),
+        ),
+        in_specs=[smem()] + [vmem()] * 5,
+        out_specs=(vmem(), vmem(), vmem(), hbm()),
+        scratch_shapes=half_scratch(rows),
+        compiler_params=params(12),
         cost_estimate=pl.CostEstimate(flops=2 * 10**9, bytes_accessed=4 * 10**6, transcendentals=0),
-    )(tab, wh, wl, res)
-
-
-def update_other_body(info, hi_ref, lo_ref, res_ref, ch_ref, res_t_ref, out_ref, share_ref, all_ref):
+    )(info, tab, wh, wl, res, res_t)
+
+
+def update_other_body(info, hi_ref, lo_ref, res_ref, part_ref, res_t_ref, begun_hbm, out_hbm, share_ref, buf, sem):
     core = info[0]
     classes, rows = res_t_ref.shape
-    chalf = ch_ref.shape[1]
-    all_ref[:, pl.ds(pl.multiple_of(core * chalf, chalf), chalf)] = ch_ref[...]
     change = apply_weights(hi_ref[...], lo_ref[...], res_ref)
-    all_ref[:, pl.ds(pl.multiple_of((1 - core) * chalf, chalf), chalf)] = change
-    share_ref[...] = all_ref[pl.ds(rows, share_ref.shape[0]), pl.ds(0, classes)]
-    out_ref[...] = res_t_ref[...] - all_ref[pl.ds(0, rows), :].T[:classes]
-
-
-def update_other(info, hi, lo, res, change, res_t, share):
+    copy = write_half(1 - core, change, res_t_ref, out_hbm, buf, sem)
+    mine, theirs = part_ref[...], change[rows:]
+    low = jnp.where(core == 0, mine, theirs)
+    high = jnp.where(core == 0, theirs, mine)
+    share_ref[...] = jnp.concatenate([low[:, :CLASS_SPAN], high[:, 2 * CLASS_SPAN - classes : CLASS_SPAN]], axis=1)
+    copy.wait()
+
+
+def update_other(info, hi, lo, res, part, res_t, begun):
     classes, rows = res_t.shape
     return pl.pallas_call(
         update_other_body,
-        out_shape=(jax.ShapeDtypeStruct((classes, rows), F32), jax.ShapeDtypeStruct((share, classes), F32)),
-        in_specs=[smem()] + [vmem()] * 5,
-        out_specs=(vmem(), vmem()),
-        scratch_shapes=[pltpu.VMEM((rows + share, CLASS_PAD), F32)],
-        compiler_params=params(16),
-    )(info, hi, lo, res, change, res_t)
+        out_shape=(jax.ShapeDtypeStruct((classes, rows), F32), jax.ShapeDtypeStruct((part.shape[0], classes), F32)),
+        in_specs=[smem()] + [vmem()] * 5 + [hbm()],
+        out_specs=(hbm(), vmem()),
+        input_output_aliases={6: 0},
+        scratch_shapes=half_scratch(rows),
+        compiler_params=params(12),
+    )(info, hi, lo, res, part, res_t, begun)
 
 
 def plane_groups():
@@ -391,8 +419,8 @@
     wh, wl = inverse(info, tab, p_oth, other, cross, p_cross, psq, share)
     all_res, wh = lax.optimization_barrier((all_res, wh))
     other_res = lax.ppermute(all_res, "c", swap)
-    hi, lo, change = update_own(tab, wh, wl, all_res)
-    out_t, step_share = update_other(info, hi, lo, other_res, change, res_t, share)
+    hi, lo, part, begun = update_own(info, tab, wh, wl, all_res, res_t)
+    out_t, step_share = update_other(info, hi, lo, other_res, part, res_t, begun)
     return (out_t.T, step_share)
 
 

time: 109 us -> 109 us (level)
  Pallas kernels: 24.8 us -> 26.4 us
  waiting for transfers between devices: 4.01 us -> 2.84 us
    pallas_call x1, Pallas kernels: 1.82 us -> 3.09 us  [update_own(): pl.pallas_call(update_own_body, out_shape=(out, out, jax.ShapeDtypeStruct...]
    ppermute x1, waiting for transfers between devices: 1.18 us -> 0.01 us  [on_device(): other_res = lax.ppermute(all_res, 'c', swap)]
  transfers between devices with their start and end apart: 3 -> 3, of which waited for: 3 -> 2; matrix products, arithmetic and copies ran while one was open for 0% -> 0% of each run, Pallas kernels for 16% -> 17%
where the time goes in v6:
time: 109 us
  blocking collectives  64.5 us (59%)
  Pallas kernels  26.4 us (24%)
  starting transfers between devices  12.7 us (12%)
  waiting for transfers between devices  2.84 us (3%)
    all_to_all x1, blocking collectives, on_device(): col_rows = lax.all_to_all(packed, COLUMN, 0, 0, tiled=True)  38.8 us
    all_to_all x1, blocking collectives, over_plane(): lax.all_to_all(value, EVERY, 0, 0, axis_index_groups=plane_groups(), tile...  25.7 us
    pallas_call x1, Pallas kernels, inverse(): pl.pallas_call(functools.partial(inverse_body, share=share), out_shape=(o...  12.8 us
    all_to_all x1, starting transfers between devices, over_plane(): lax.all_to_all(value, EVERY, 0, 0, axis_index_groups=plane_groups(), tile...  7.97 us
    pallas_call x1, Pallas kernels, pack(): pl.pallas_call(functools.partial(pack_body, n_plane=n_plane, n_col=n_col)...  3.69 us
    pallas_call x1, Pallas kernels, update_own(): pl.pallas_call(update_own_body, out_shape=(out, out, jax.ShapeDtypeStruct...  3.09 us
    pallas_call x1, Pallas kernels, update_other(): pl.pallas_call(update_other_body, out_shape=(jax.ShapeDtypeStruct((classe...  2.98 us
    ppermute x1, starting transfers between devices, on_device(): other_res = lax.ppermute(all_res, 'c', swap)  2.83 us
  transfers between devices with their start and end apart: 3, of which 2 were waited for; matrix products, arithmetic and copies ran while one was open for 0% of the time, Pallas kernels for 17%

profile of v6, /device:TPU:1, one launch (start us, length us, event | category | flops | bytes accessed | tf_op | source)
XLA Modules:
  0.0 108.5 jit_solution(15411916771156913220)
XLA Ops:
  0.6 0.6 pad_add_fusion.info
  1.2 0.0 copy-start.5
  1.2 3.7 %shard_map.50 = (bf16[32,8,512]{2,1,0:T(8,128)(2,1)}, s32[8,512]{1,0:T(8,128)}) custom-call(s32[4]{0:T(128)} %pad_add_fusion.info, s32[1,512]{1,0:T(1,128)} %bitcast.18, bf16[256,2048]{1,0:T(8,128)(2,1)} %pts_ref.1, f32[1000,256]{1,0:T(8,128)} %bitcast.11), custom_call_target="tpu_custom_call" | custom-call | tf_op jit(solution)/shard_map/pallas_call | solution.py:125
  4.9 38.8 %all_to_all.15 = bf16[32,8,512]{2,1,0:T(8,128)(2,1)S(1)} all-to-all(bf16[32,8,512]{2,1,0:T(8,128)(2,1)} %get-tuple-element.21), channel_id=1, replica_groups=mesh['y'=4,'x'=4,'zh'=2,'zl'=8,'c'=2] {'zh','zl','c'}, dimensions={0} | all-to-all | bytes 524288 | tf_op jit(solution)/shard_map/all_to_all | solution.py:411
  43.7 0.0 copy-done.5
  43.7 0.0 copy-start.3
  43.7 0.7 copy-done.3
  44.4 1.3 %shard_map.51 = (bf16[16,48,1024]{2,1,0:T(8,128)(2,1)S(1)}, bf16[16,48,1024]{2,1,0:T(8,128)(2,1)S(1)}) custom-call(s32[4]{0:T(128)S(1)} %copy-done.5, s32[8,512]{1,0:T(8,128)S(1)} %copy-done.3, bf16[256,512]{1,0:T(8,128)(2,1)S(1)} %bitcast.16), custom_call_target="tpu_custom_call" | custom-call | tf_op jit(solution)/shard_map/pallas_call | solution.py:172
  45.7 0.0 copy-start.2
  45.7 25.7 %all_to_all.16 = bf16[16,48,1024]{2,1,0:T(8,128)(2,1)S(1)} all-to-all(bf16[16,48,1024]{2,1,0:T(8,128)(2,1)S(1)} %get-tuple-element.23), channel_id=1, replica_groups={{0,32,64,96,128,160,192,224,256,288,320,352,384,416,448,480},{481,449,4..., dimensions={0} | all-to-all | bytes 3145728 | tf_op jit(solution)/shard_map/all_to_all | solution.py:391
  71.4 0.0 copy-done.2
  71.4 0.0 copy-start.4
  71.4 8.0 %all-to-all-start.1 = ((bf16[16,48,1024]{2,1,0:T(8,128)(2,1)}), bf16[16,48,1024]{2,1,0:T(8,128)(2,1)S(1)}, u32[]{:S(2)}, u32[]{:S(2)}) async-start(bf16[16,48,1024]{2,1,0:T(8,128)(2,1)} %copy-done.2), calls=%async_computation.1 | async-start | bytes 3145728 | tf_op jit(solution)/shard_map/all_to_all | solution.py:391
  79.4 0.0 copy-start
  79.4 0.0 copy-done.4
  79.4 1.0 shard_map.52.own_ref
  80.4 1.9 %collective-permute-start = (bf16[512,1024]{1,0:T(8,128)(2,1)S(1)}, bf16[512,1024]{1,0:T(8,128)(2,1)S(1)}, u32[]{:S(2)}, u32[]{:S(2)}) collective-permute-start(bf16[512,1024]{1,0:T(8,128)(2,1)S(1)} %shard_map.52.own_ref), channel_id=1, source_target_pairs={{0,1},{1,0},{2,3},{3,2},{4,5},{5,4},{6,7},{7,6},{8,9},{9,8},{10,11... | collective-permute-start | bytes 3145736 | tf_op jit(solution)/shard_map/ppermute | solution.py:417
  82.4 0.0 copy-done
  82.4 1.6 %shard_map.53 = (f32[512,512]{1,0:T(8,128)S(1)}, f32[256,512]{1,0:T(8,128)S(1)}, f32[256,1]{1,0:T(8,128)S(1)}, bf16[256,1024]{1,0:T(8,128)(2,1)S(1)}) custom-call(s32[4]{0:T(128)S(1)} %copy-done.5, bf16[256,2048]{1,0:T(8,128)(2,1)S(1)} %copy-done, bf16[512,1024]{1,0:T(8,128)(2,1)S(1)} %shard_map.52.own_ref), custom_call_target="tpu_custom_call" | custom-call | flops 1000000 | bytes 1000000 | tf_op jit(solution)/shard_map/pallas_call | solution.py:219
  84.0 1.0 collective-permute-done.oth_ref
  85.0 0.0 copy-start.1
  85.0 12.8 %shard_map.54 = (bf16[288,512]{1,0:T(8,128)(2,1)S(1)}, bf16[288,512]{1,0:T(8,128)(2,1)S(1)}) custom-call(s32[4]{0:T(128)S(1)} %copy-done.5, s32[8,512]{1,0:T(8,128)S(1)} %copy-done.4, bf16[256,1024]{1,0:T(8,128)(2,1)S(1)} %get-tuple-element.24.p_oth_ref, bf16[512,1024]{1,0:T(8,128)(2,1)S(1)} %collective-permute-done.oth_ref, ...), custom_call_target="tpu_custom_call" | custom-call | flops 1000000 | bytes 1000000 | tf_op jit(solution)/shard_map/pallas_call | solution.py:286
  97.8 1.8 %all-to-all-done.1 = bf16[16,48,1024]{2,1,0:T(8,128)(2,1)S(1)} async-done(((bf16[16,48,1024]{2,1,0:T(8,128)(2,1)}), bf16[16,48,1024]{2,1,0:T(8,128)(2,1)S(1)}, u32[]{:S(2)}, u32[]{:S(2)}) %all-to-all-start.1) | async-done | bytes 1572896 | tf_op jit(solution)/shard_map/all_to_all | solution.py:391
  99.6 2.8 %collective-permute-start.1 = (bf16[768,1024]{1,0:T(8,128)(2,1)S(1)}, bf16[768,1024]{1,0:T(8,128)(2,1)S(1)}, u32[]{:S(2)}, u32[]{:S(2)}) collective-permute-start(bf16[768,1024]{1,0:T(8,128)(2,1)S(1)} %bitcast.14), channel_id=1, source_target_pairs={{0,1},{1,0},{2,3},{3,2},{4,5},{5,4},{6,7},{7,6},{8,9},{9,8},{10,11... | collective-permute-start | bytes 4718600 | tf_op jit(solution)/shard_map/ppermute | solution.py:421
  102.4 0.0 copy-done.1
  102.4 3.1 %shard_map.55 = (bf16[288,768]{1,0:T(8,128)(2,1)S(1)}, bf16[288,768]{1,0:T(8,128)(2,1)S(1)}, f32[32,512]{1,0:T(8,128)S(1)}, f32[1000,256]{1,0:T(8,128)}) custom-call(s32[4]{0:T(128)S(1)} %copy-done.5, s32[8,512]{1,0:T(8,128)S(1)} %copy-done.4, bf16[288,512]{1,0:T(8,128)(2,1)S(1)} %get-tuple-element.29.wh_ref, bf16[288,512]{1,0:T(8,128)(2,1)S(1)} %get-tuple-element.30.wl_ref, ...), custom_call_target="tpu_custom_call" | custom-call | flops 2000000000 | bytes 4000000 | tf_op jit(solution)/shard_map/pallas_call | solution.py:341
  105.5 0.0 collective-permute-done.1.res_ref
  105.5 3.0 %shard_map.56 = (f32[1000,256]{1,0:T(8,128)}, f32[32,1000]{1,0:T(8,128)}) custom-call(s32[4]{0:T(128)S(1)} %copy-done.5, bf16[288,768]{1,0:T(8,128)(2,1)S(1)} %get-tuple-element.32.hi_ref, bf16[288,768]{1,0:T(8,128)(2,1)S(1)} %get-tuple-element.33.lo_ref, bf16[768,1024]{1,0:T(8,128)(2,1)S(1)} %collective-permute-done.1.res_ref, ...), custom_call_target="tpu_custom_call", output_to_operand_aliasing={{0}: (6, {})} | custom-call | tf_op jit(solution)/shard_map/pallas_call | solution.py:371
Async XLA Ops:
  1.2 42.5 %copy-start.5 = (s32[4]{0:T(128)S(1)}, s32[4]{0:T(128)}, u32[]{:S(2)}) copy-start(s32[4]{0:T(128)} %pad_add_fusion.info) | copy-start | bytes 52
  43.7 0.7 copy-start.3
  45.7 25.7 %copy-start.2 = (bf16[16,48,1024]{2,1,0:T(8,128)(2,1)}, bf16[16,48,1024]{2,1,0:T(8,128)(2,1)S(1)}, u32[]{:S(2)}) copy-start(bf16[16,48,1024]{2,1,0:T(8,128)(2,1)S(1)} %get-tuple-element.22) | copy-start | bytes 4718596
  71.4 8.0 %copy-start.4 = (s32[8,512]{1,0:T(8,128)S(1)}, s32[8,512]{1,0:T(8,128)}, u32[]{:S(2)}) copy-start(s32[8,512]{1,0:T(8,128)} %get-tuple-element.20.tab_ref) | copy-start | bytes 49156
  71.4 28.1 %all-to-all-start.1 = ((bf16[16,48,1024]{2,1,0:T(8,128)(2,1)}), bf16[16,48,1024]{2,1,0:T(8,128)(2,1)S(1)}, u32[]{:S(2)}, u32[]{:S(2)}) async-start(bf16[16,48,1024]{2,1,0:T(8,128)(2,1)} %copy-done.2), calls=%async_computation.1 | async-start | bytes 3145728 | tf_op jit(solution)/shard_map/all_to_all | solution.py:391
  79.4 3.0 %copy-start = (bf16[256,2048]{1,0:T(8,128)(2,1)S(1)}, bf16[256,2048]{1,0:T(8,128)(2,1)}, u32[]{:S(2)}) copy-start(bf16[256,2048]{1,0:T(8,128)(2,1)} %pts_ref.1) | copy-start | bytes 3145732
  80.4 4.6 %collective-permute-start = (bf16[512,1024]{1,0:T(8,128)(2,1)S(1)}, bf16[512,1024]{1,0:T(8,128)(2,1)S(1)}, u32[]{:S(2)}, u32[]{:S(2)}) collective-permute-start(bf16[512,1024]{1,0:T(8,128)(2,1)S(1)} %shard_map.52.own_ref), channel_id=1, source_target_pairs={{0,1},{1,0},{2,3},{3,2},{4,5},{5,4},{6,7},{7,6},{8,9},{9,8},{10,11... | collective-permute-start | bytes 3145736 | tf_op jit(solution)/shard_map/ppermute | solution.py:417
  85.0 17.4 %copy-start.1 = (f32[256,1000]{0,1:T(8,128)S(1)}, f32[256,1000]{0,1:T(8,128)}, u32[]{:S(2)}) copy-start(f32[256,1000]{0,1:T(8,128)} %param.4) | copy-start | bytes 3072004
  99.6 6.0 %collective-permute-start.1 = (bf16[768,1024]{1,0:T(8,128)(2,1)S(1)}, bf16[768,1024]{1,0:T(8,128)(2,1)S(1)}, u32[]{:S(2)}, u32[]{:S(2)}) collective-permute-start(bf16[768,1024]{1,0:T(8,128)(2,1)S(1)} %bitcast.14), channel_id=1, source_target_pairs={{0,1},{1,0},{2,3},{3,2},{4,5},{5,4},{6,7},{7,6},{8,9},{9,8},{10,11... | collective-permute-start | bytes 4718600 | tf_op jit(solution)/shard_map/ppermute | solution.py:421

commit v7 on v5

--- a/solution.py
+++ b/solution.py
@@ -25,6 +25,10 @@
 COL_CAP = 48
 CLASS_PAD = 1024
 SPLIT = 4
+CLASS_STEP = 496
+CLASS_SPAN = 504
+SCALE_LANE = 511
+FRACTION = 2.0**22
 MIB = 1024 * 1024
 
 
@@ -109,7 +113,7 @@
     chalf = CLASS_PAD // 2
     for core in range(2):
         row = [picked[:CAP, core * half : (core + 1) * half]]
-        row += [v[:CAP, core * chalf : (core + 1) * chalf] for v in parts]
+        row += [v[:CAP, core * CLASS_STEP : core * CLASS_STEP + chalf] for v in parts]
         row = jnp.concatenate(row, axis=1).astype(F32)
         w = row.shape[1] // SPLIT
         block = jnp.concatenate([row[:, q * w : (q + 1) * w] for q in range(SPLIT)], axis=0).astype(BF)
@@ -140,6 +144,27 @@
 
 def table(tab_ref):
     return tab_ref[0:1, :], tab_ref[1:2, :], tab_ref[2:3, :]
+
+
+def encode(res):
+    top = jnp.max(jnp.abs(res), axis=1, keepdims=True)
+    power = jnp.floor(jnp.log2(jnp.maximum(top, 1e-30))) + 1.0
+    code = jnp.floor(res * (FRACTION / jnp.exp2(power)) + 0.5).astype(I32)
+    code = jnp.where(iota(res.shape, 1) == SCALE_LANE, power.astype(I32) * 256, code)
+    low = code & 255
+    half = res.shape[1] // 2
+    pair = (low[:, :half] | (low[:, half:] << 8)) - 32768
+    return jnp.concatenate([code >> 8, pair], axis=1).astype(jnp.int16)
+
+
+def decode(words):
+    words = words.astype(I32)
+    n = words.shape[1] * 2 // 3
+    high = words[:, :n]
+    pair = words[:, n:] + 32768
+    low = jnp.concatenate([pair & 255, pair >> 8], axis=1)
+    unit = jnp.exp2(high[:, SCALE_LANE : SCALE_LANE + 1].astype(F32)) * (1.0 / FRACTION)
+    return (high * 256 + low).astype(F32) * unit
 
 
 def compact_body(info, tab_ref, in_ref, pts_ref, res_ref, *, rows, n_col):
@@ -160,7 +185,8 @@
     whole = jnp.concatenate(whole, axis=1)
     half = pts_ref.shape[2]
     pts = whole[:, :half].astype(BF)
-    res = whole[:, half:].astype(BF)
+    chalf = CLASS_PAD // 2
+    res = encode(whole[:, half : half + chalf] + whole[:, half + chalf :])
     for p in range(pts_ref.shape[0]):
         pts_ref[p] = pts
         res_ref[p] = res
@@ -171,7 +197,7 @@
         functools.partial(compact_body, rows=rows, n_col=n_col),
         out_shape=(
             jax.ShapeDtypeStruct((n_plane, COL_CAP, half), BF),
-            jax.ShapeDtypeStruct((n_plane, COL_CAP, CLASS_PAD), BF),
+            jax.ShapeDtypeStruct((n_plane, COL_CAP, CLASS_PAD * 3 // 4), jnp.int16),
         ),
         in_specs=[smem(), vmem(), vmem()],
         out_specs=(vmem(), vmem()),
@@ -299,8 +325,7 @@
 
 
 def apply_weights(hi, lo, res_ref):
-    chalf = res_ref.shape[1] // 2
-    return mm3((hi, lo), (res_ref[:, :chalf], res_ref[:, chalf:]))
+    return mm3((hi, lo), two_parts(decode(res_ref[...])))
 
 
 def update_own_body(tab_ref, wh_ref, wl_ref, res_ref, hi_ref, lo_ref, ch_ref):
@@ -316,11 +341,11 @@
 
 def update_own(tab, wh, wl, res):
     m = wh.shape[0]
-    wide, parts = res.shape
+    wide = res.shape[0]
     out = jax.ShapeDtypeStruct((m, wide), BF)
     return pl.pallas_call(
         update_own_body,
-        out_shape=(out, out, jax.ShapeDtypeStruct((m, parts // 2), F32)),
+        out_shape=(out, out, jax.ShapeDtypeStruct((m, CLASS_PAD // 2), F32)),
         in_specs=[vmem()] * 4,
         out_specs=(vmem(),) * 3,
         compiler_params=params(10),
@@ -328,15 +353,17 @@
     )(tab, wh, wl, res)
 
 
-def update_other_body(info, hi_ref, lo_ref, res_ref, ch_ref, res_t_ref, out_ref, share_ref, all_ref):
+def update_other_body(info, hi_ref, lo_ref, res_ref, ch_ref, res_t_ref, out_ref, share_ref):
     core = info[0]
     classes, rows = res_t_ref.shape
-    chalf = ch_ref.shape[1]
-    all_ref[:, pl.ds(pl.multiple_of(core * chalf, chalf), chalf)] = ch_ref[...]
-    change = apply_weights(hi_ref[...], lo_ref[...], res_ref)
-    all_ref[:, pl.ds(pl.multiple_of((1 - core) * chalf, chalf), chalf)] = change
-    share_ref[...] = all_ref[pl.ds(rows, share_ref.shape[0]), pl.ds(0, classes)]
-    out_ref[...] = res_t_ref[...] - all_ref[pl.ds(0, rows), :].T[:classes]
+    skip = 2 * CLASS_SPAN - classes
+    mine = ch_ref[...]
+    theirs = apply_weights(hi_ref[...], lo_ref[...], res_ref)
+    low = jnp.where(core == 0, mine, theirs)
+    high = jnp.where(core == 0, theirs, mine)
+    share_ref[...] = jnp.concatenate([low[rows:, :CLASS_SPAN], high[rows:, skip:CLASS_SPAN]], axis=1)
+    out_ref[:CLASS_SPAN, :] = res_t_ref[:CLASS_SPAN, :] - low[:rows].T[:CLASS_SPAN]
+    out_ref[CLASS_SPAN:, :] = res_t_ref[CLASS_SPAN:, :] - high[:rows].T[skip:CLASS_SPAN]
 
 
 def update_other(info, hi, lo, res, change, res_t, share):
@@ -346,7 +373,6 @@
         out_shape=(jax.ShapeDtypeStruct((classes, rows), F32), jax.ShapeDtypeStruct((share, classes), F32)),
         in_specs=[smem()] + [vmem()] * 5,
         out_specs=(vmem(), vmem()),
-        scratch_shapes=[pltpu.VMEM((rows + share, CLASS_PAD), F32)],
         compiler_params=params(16),
     )(info, hi, lo, res, change, res_t)
 
@@ -384,7 +410,7 @@
     col_rows = col_rows.reshape(n_col * CAP * SPLIT, col_rows.shape[2])
     pts_out, res_out = compact(info, tab, col_rows, rows, half, n_plane, n_col)
     all_pts = over_plane(pts_out).reshape(wide, half)
-    all_res = over_plane(res_out).reshape(wide, CLASS_PAD)
+    all_res = over_plane(res_out).reshape(wide, CLASS_PAD * 3 // 4)
     own = order(tab, all_pts)
     other = lax.ppermute(own, "c", swap)
     cross, p_cross, psq, p_oth = first_half(info, points, own)

time: 109 us -> 106 us (0.972)
  waiting for transfers between devices: 4.01 us -> 1.64 us
    all_to_all x1, waiting for transfers between devices: 1.8 us -> 0.01 us  [over_plane(): lax.all_to_all(value, EVERY, 0, 0, axis_index_groups=plane_groups(), tile...]
  transfers between devices with their start and end apart: 3 -> 3, of which waited for: 3 -> 2; matrix products, arithmetic and copies ran while one was open for 0% -> 0% of each run, Pallas kernels for 16% -> 17%
where the time goes in v7:
time: 106 us
  blocking collectives  64.5 us (61%)
  Pallas kernels  25.4 us (24%)
  starting transfers between devices  11.9 us (11%)
  waiting for transfers between devices  1.64 us (2%)
    all_to_all x1, blocking collectives, on_device(): col_rows = lax.all_to_all(packed, COLUMN, 0, 0, tiled=True)  38.8 us
    all_to_all x1, blocking collectives, over_plane(): lax.all_to_all(value, EVERY, 0, 0, axis_index_groups=plane_groups(), tile...  25.7 us
    pallas_call x1, Pallas kernels, inverse(): pl.pallas_call(functools.partial(inverse_body, share=share), out_shape=(o...  12.8 us
    all_to_all x1, starting transfers between devices, over_plane(): lax.all_to_all(value, EVERY, 0, 0, axis_index_groups=plane_groups(), tile...  7.96 us
    pallas_call x1, Pallas kernels, pack(): pl.pallas_call(functools.partial(pack_body, n_plane=n_plane, n_col=n_col)...  3.69 us
    pallas_call x1, Pallas kernels, update_other(): pl.pallas_call(update_other_body, out_shape=(jax.ShapeDtypeStruct((classe...  3.01 us
  transfers between devices with their start and end apart: 3, of which 2 were waited for; matrix products, arithmetic and copies ran while one was open for 0% of the time, Pallas kernels for 17%

profile of v7, /device:TPU:1, one launch (start us, length us, event | category | flops | bytes accessed | tf_op | source)
XLA Modules:
  0.0 105.5 jit_solution(9960226675704974980)
XLA Ops:
  0.6 0.6 pad_add_fusion.info
  1.2 0.0 copy-start.5
  1.2 3.7 %shard_map.50 = (bf16[32,8,512]{2,1,0:T(8,128)(2,1)}, s32[8,512]{1,0:T(8,128)}) custom-call(s32[4]{0:T(128)} %pad_add_fusion.info, s32[1,512]{1,0:T(1,128)} %bitcast.16, bf16[256,2048]{1,0:T(8,128)(2,1)} %pts_ref.1, f32[1000,256]{1,0:T(8,128)} %bitcast.11), custom_call_target="tpu_custom_call" | custom-call | tf_op jit(solution)/shard_map/pallas_call | solution.py:127
  4.9 38.8 %all_to_all.15 = bf16[32,8,512]{2,1,0:T(8,128)(2,1)S(1)} all-to-all(bf16[32,8,512]{2,1,0:T(8,128)(2,1)} %get-tuple-element.20), channel_id=1, replica_groups=mesh['y'=4,'x'=4,'zh'=2,'zl'=8,'c'=2] {'zh','zl','c'}, dimensions={0} | all-to-all | bytes 524288 | tf_op jit(solution)/shard_map/all_to_all | solution.py:409
  43.7 0.0 copy-done.5
  43.7 0.0 copy-start.3
  43.7 0.7 copy-done.3
  44.4 1.3 %shard_map.51 = (bf16[16,48,1024]{2,1,0:T(8,128)(2,1)S(1)}, s16[16,48,768]{2,1,0:T(8,128)(2,1)S(1)}) custom-call(s32[4]{0:T(128)S(1)} %copy-done.5, s32[8,512]{1,0:T(8,128)S(1)} %copy-done.3, bf16[256,512]{1,0:T(8,128)(2,1)S(1)} %bitcast.15), custom_call_target="tpu_custom_call" | custom-call | tf_op jit(solution)/shard_map/pallas_call | solution.py:196
  45.7 0.0 copy-start.2
  45.7 25.7 %all_to_all.16 = bf16[16,48,1024]{2,1,0:T(8,128)(2,1)S(1)} all-to-all(bf16[16,48,1024]{2,1,0:T(8,128)(2,1)S(1)} %get-tuple-element.22), channel_id=1, replica_groups={{0,32,64,96,128,160,192,224,256,288,320,352,384,416,448,480},{481,449,4..., dimensions={0} | all-to-all | bytes 3145728 | tf_op jit(solution)/shard_map/all_to_all | solution.py:389
  71.5 0.0 copy-done.2
  71.5 0.0 copy-start.4
  71.5 8.0 %all-to-all-start.1 = ((s16[16,48,768]{2,1,0:T(8,128)(2,1)}), s16[16,48,768]{2,1,0:T(8,128)(2,1)S(1)}, u32[]{:S(2)}, u32[]{:S(2)}) async-start(s16[16,48,768]{2,1,0:T(8,128)(2,1)} %copy-done.2), calls=%async_computation.1 | async-start | bytes 2359296 | tf_op jit(solution)/shard_map/all_to_all | solution.py:389
  79.4 0.0 copy-done.4
  79.4 0.0 copy-start
  79.4 1.0 shard_map.52.own_ref
  80.5 1.9 %collective-permute-start = (bf16[512,1024]{1,0:T(8,128)(2,1)S(1)}, bf16[512,1024]{1,0:T(8,128)(2,1)S(1)}, u32[]{:S(2)}, u32[]{:S(2)}) collective-permute-start(bf16[512,1024]{1,0:T(8,128)(2,1)S(1)} %shard_map.52.own_ref), channel_id=1, source_target_pairs={{0,1},{1,0},{2,3},{3,2},{4,5},{5,4},{6,7},{7,6},{8,9},{9,8},{10,11... | collective-permute-start | bytes 3145736 | tf_op jit(solution)/shard_map/ppermute | solution.py:415
  82.4 0.0 copy-done
  82.4 1.6 %shard_map.53 = (f32[512,512]{1,0:T(8,128)S(1)}, f32[256,512]{1,0:T(8,128)S(1)}, f32[256,1]{1,0:T(8,128)S(1)}, bf16[256,1024]{1,0:T(8,128)(2,1)S(1)}) custom-call(s32[4]{0:T(128)S(1)} %copy-done.5, bf16[256,2048]{1,0:T(8,128)(2,1)S(1)} %copy-done, bf16[512,1024]{1,0:T(8,128)(2,1)S(1)} %shard_map.52.own_ref), custom_call_target="tpu_custom_call" | custom-call | flops 1000000 | bytes 1000000 | tf_op jit(solution)/shard_map/pallas_call | solution.py:243
  84.0 1.0 collective-permute-done.oth_ref
  85.0 12.8 %shard_map.54 = (bf16[288,512]{1,0:T(8,128)(2,1)S(1)}, bf16[288,512]{1,0:T(8,128)(2,1)S(1)}) custom-call(s32[4]{0:T(128)S(1)} %copy-done.5, s32[8,512]{1,0:T(8,128)S(1)} %copy-done.4, bf16[256,1024]{1,0:T(8,128)(2,1)S(1)} %get-tuple-element.23.p_oth_ref, bf16[512,1024]{1,0:T(8,128)(2,1)S(1)} %collective-permute-done.oth_ref, ...), custom_call_target="tpu_custom_call" | custom-call | flops 1000000 | bytes 1000000 | tf_op jit(solution)/shard_map/pallas_call | solution.py:310
  97.8 0.0 all-to-all-done.1
  97.8 2.0 %collective-permute-start.1 = (s16[768,768]{1,0:T(8,128)(2,1)S(1)}, s16[768,768]{1,0:T(8,128)(2,1)S(1)}, u32[]{:S(2)}, u32[]{:S(2)}) collective-permute-start(s16[768,768]{1,0:T(8,128)(2,1)S(1)} %bitcast.13), channel_id=1, source_target_pairs={{0,1},{1,0},{2,3},{3,2},{4,5},{5,4},{6,7},{7,6},{8,9},{9,8},{10,11... | collective-permute-start | bytes 3538952 | tf_op jit(solution)/shard_map/ppermute | solution.py:419
  99.8 0.0 copy-start.1
  99.9 2.1 %shard_map.55 = (bf16[288,768]{1,0:T(8,128)(2,1)S(1)}, bf16[288,768]{1,0:T(8,128)(2,1)S(1)}, f32[288,512]{1,0:T(8,128)S(1)}) custom-call(s32[8,512]{1,0:T(8,128)S(1)} %copy-done.4, bf16[288,512]{1,0:T(8,128)(2,1)S(1)} %get-tuple-element.28.wh_ref, bf16[288,512]{1,0:T(8,128)(2,1)S(1)} %get-tuple-element.29.wl_ref, s16[768,768]{1,0:T(8,128)(2,1)S(1)} %bitcast.14), custom_call_target="tpu_custom_call" | custom-call | flops 2000000000 | bytes 4000000 | tf_op jit(solution)/shard_map/pallas_call | solution.py:346
  101.9 0.6 collective-permute-done.1.res_ref
  102.5 0.0 copy-done.1
  102.5 3.0 %shard_map.56 = (f32[1000,256]{1,0:T(8,128)}, f32[32,1000]{1,0:T(8,128)}) custom-call(s32[4]{0:T(128)S(1)} %copy-done.5, bf16[288,768]{1,0:T(8,128)(2,1)S(1)} %get-tuple-element.31.hi_ref, bf16[288,768]{1,0:T(8,128)(2,1)S(1)} %get-tuple-element.32.lo_ref, s16[768,768]{1,0:T(8,128)(2,1)S(1)} %collective-permute-done.1.res_ref, ...), custom_call_target="tpu_custom_call" | custom-call | tf_op jit(solution)/shard_map/pallas_call | solution.py:371
Async XLA Ops:
  1.2 42.5 %copy-start.5 = (s32[4]{0:T(128)S(1)}, s32[4]{0:T(128)}, u32[]{:S(2)}) copy-start(s32[4]{0:T(128)} %pad_add_fusion.info) | copy-start | bytes 52
  43.7 0.7 copy-start.3
  45.7 25.7 %copy-start.2 = (s16[16,48,768]{2,1,0:T(8,128)(2,1)}, s16[16,48,768]{2,1,0:T(8,128)(2,1)S(1)}, u32[]{:S(2)}) copy-start(s16[16,48,768]{2,1,0:T(8,128)(2,1)S(1)} %get-tuple-element.21) | copy-start | bytes 3538948
  71.5 8.0 %copy-start.4 = (s32[8,512]{1,0:T(8,128)S(1)}, s32[8,512]{1,0:T(8,128)}, u32[]{:S(2)}) copy-start(s32[8,512]{1,0:T(8,128)} %get-tuple-element.19.tab_ref) | copy-start | bytes 49156
  71.5 26.3 %all-to-all-start.1 = ((s16[16,48,768]{2,1,0:T(8,128)(2,1)}), s16[16,48,768]{2,1,0:T(8,128)(2,1)S(1)}, u32[]{:S(2)}, u32[]{:S(2)}) async-start(s16[16,48,768]{2,1,0:T(8,128)(2,1)} %copy-done.2), calls=%async_computation.1 | async-start | bytes 2359296 | tf_op jit(solution)/shard_map/all_to_all | solution.py:389
  79.4 3.0 %copy-start = (bf16[256,2048]{1,0:T(8,128)(2,1)S(1)}, bf16[256,2048]{1,0:T(8,128)(2,1)}, u32[]{:S(2)}) copy-start(bf16[256,2048]{1,0:T(8,128)(2,1)} %pts_ref.1) | copy-start | bytes 3145732
  80.5 4.6 %collective-permute-start = (bf16[512,1024]{1,0:T(8,128)(2,1)S(1)}, bf16[512,1024]{1,0:T(8,128)(2,1)S(1)}, u32[]{:S(2)}, u32[]{:S(2)}) collective-permute-start(bf16[512,1024]{1,0:T(8,128)(2,1)S(1)} %shard_map.52.own_ref), channel_id=1, source_target_pairs={{0,1},{1,0},{2,3},{3,2},{4,5},{5,4},{6,7},{7,6},{8,9},{9,8},{10,11... | collective-permute-start | bytes 3145736 | tf_op jit(solution)/shard_map/ppermute | solution.py:415
  97.8 4.7 %collective-permute-start.1 = (s16[768,768]{1,0:T(8,128)(2,1)S(1)}, s16[768,768]{1,0:T(8,128)(2,1)S(1)}, u32[]{:S(2)}, u32[]{:S(2)}) collective-permute-start(s16[768,768]{1,0:T(8,128)(2,1)S(1)} %bitcast.13), channel_id=1, source_target_pairs={{0,1},{1,0},{2,3},{3,2},{4,5},{5,4},{6,7},{7,6},{8,9},{9,8},{10,11... | collective-permute-start | bytes 3538952 | tf_op jit(solution)/shard_map/ppermute | solution.py:419
  99.8 2.7 %copy-start.1 = (f32[256,1000]{0,1:T(8,128)S(1)}, f32[256,1000]{0,1:T(8,128)}, u32[]{:S(2)}) copy-start(f32[256,1000]{0,1:T(8,128)} %param.4) | copy-start | bytes 3072004

commit v8 on v7

--- a/solution.py
+++ b/solution.py
@@ -284,20 +284,25 @@
     x_ref[...] = jnp.where(eye, 2.0 * s, 0.0) - (s * s) * gram
     d = (hi - lo) / (hi + lo)
 
-    def refine(resid):
+    def refine(resid, whole):
         x = x_ref[...] * (2.0 / (2.0 - resid))
         xh, xl = two_parts(x)
-        r = (jnp.where(eye, 1.0, 0.0) - mm3((gh_ref[...], gl_ref[...]), (xh, xl))).astype(BF)
+        gh = gh_ref[...]
+        gx = dot(gh, xh) + (dot(gh, xl) + dot(gl_ref[...], xh) if whole else dot(gh, xl))
+        r = (jnp.where(eye, 1.0, 0.0) - gx).astype(BF)
         x_ref[...] = x + (dot(xh, r) + dot(xl, r))
         after = resid / (2.0 - resid)
         return after * after
 
-    lax.while_loop(lambda resid: resid > 5e-4, refine, d * d)
-    xs = two_parts(x_ref[...])
+    resid = lax.while_loop(lambda v: v > 0.5, functools.partial(refine, whole=False), d * d)
+    lax.while_loop(lambda v: v > 0.02, functools.partial(refine, whole=True), resid)
+    xh, xl = two_parts(x_ref[...])
     m = m_ref[...]
-    w = mm3(two_parts(m), xs)
-    e = m - dot(w, g_ref[...], NN, HI)
-    w = w + mm3(two_parts(e), xs)
+    w = mm3(two_parts(m), (xh, xl))
+    e = (m - mm3(two_parts(w), (gh_ref[...], gl_ref[...]))).astype(BF)
+    w = w + (dot(e, xh) + dot(e, xl))
+    e = (m - dot(w, g_ref[...], NN, HI)).astype(BF)
+    w = w + (dot(e, xh) + dot(e, xl))
     wh, wl = two_parts(w)
     hi_ref[...] = wh
     lo_ref[...] = wl

time: 106 us -> 106 us (level)
  no operation moved by 1% of the time
where the time goes in v8:
time: 106 us
  blocking collectives  64.5 us (61%)
  Pallas kernels  25.5 us (24%)
  starting transfers between devices  12.1 us (11%)
  waiting for transfers between devices  1.46 us (1%)
    all_to_all x1, blocking collectives, on_device(): col_rows = lax.all_to_all(packed, COLUMN, 0, 0, tiled=True)  38.8 us
    all_to_all x1, blocking collectives, over_plane(): lax.all_to_all(value, EVERY, 0, 0, axis_index_groups=plane_groups(), tile...  25.7 us
    pallas_call x1, Pallas kernels, inverse(): pl.pallas_call(functools.partial(inverse_body, share=share), out_shape=(o...  12.8 us
    all_to_all x1, starting transfers between devices, over_plane(): lax.all_to_all(value, EVERY, 0, 0, axis_index_groups=plane_groups(), tile...  7.97 us
    pallas_call x1, Pallas kernels, pack(): pl.pallas_call(functools.partial(pack_body, n_plane=n_plane, n_col=n_col)...  3.69 us
    pallas_call x1, Pallas kernels, update_other(): pl.pallas_call(update_other_body, out_shape=(jax.ShapeDtypeStruct((classe...  3.01 us
    ppermute x1, starting transfers between devices, on_device(): other_res = lax.ppermute(all_res, 'c', swap)  2.22 us
  transfers between devices with their start and end apart: 3, of which 2 were waited for; matrix products, arithmetic and copies ran while one was open for 0% of the time, Pallas kernels for 17%

profile of v8, /device:TPU:1, one launch (start us, length us, event | category | flops | bytes accessed | tf_op | source)
XLA Modules:
  0.0 105.6 jit_solution(4442299529449405563)
XLA Ops:
  0.6 0.6 pad_add_fusion.info
  1.2 0.0 copy-start.5
  1.2 3.7 %shard_map.50 = (bf16[32,8,512]{2,1,0:T(8,128)(2,1)}, s32[8,512]{1,0:T(8,128)}) custom-call(s32[4]{0:T(128)} %pad_add_fusion.info, s32[1,512]{1,0:T(1,128)} %bitcast.16, bf16[256,2048]{1,0:T(8,128)(2,1)} %pts_ref.1, f32[1000,256]{1,0:T(8,128)} %bitcast.11), custom_call_target="tpu_custom_call" | custom-call | tf_op jit(solution)/shard_map/pallas_call | solution.py:127
  4.9 38.8 %all_to_all.15 = bf16[32,8,512]{2,1,0:T(8,128)(2,1)S(1)} all-to-all(bf16[32,8,512]{2,1,0:T(8,128)(2,1)} %get-tuple-element.20), channel_id=1, replica_groups=mesh['y'=4,'x'=4,'zh'=2,'zl'=8,'c'=2] {'zh','zl','c'}, dimensions={0} | all-to-all | bytes 524288 | tf_op jit(solution)/shard_map/all_to_all | solution.py:414
  43.7 0.0 copy-done.5
  43.7 0.0 copy-start.3
  43.7 0.7 copy-done.3
  44.4 1.3 %shard_map.51 = (bf16[16,48,1024]{2,1,0:T(8,128)(2,1)S(1)}, s16[16,48,768]{2,1,0:T(8,128)(2,1)S(1)}) custom-call(s32[4]{0:T(128)S(1)} %copy-done.5, s32[8,512]{1,0:T(8,128)S(1)} %copy-done.3, bf16[256,512]{1,0:T(8,128)(2,1)S(1)} %bitcast.15), custom_call_target="tpu_custom_call" | custom-call | tf_op jit(solution)/shard_map/pallas_call | solution.py:196
  45.7 0.0 copy-start.2
  45.7 25.7 %all_to_all.16 = bf16[16,48,1024]{2,1,0:T(8,128)(2,1)S(1)} all-to-all(bf16[16,48,1024]{2,1,0:T(8,128)(2,1)S(1)} %get-tuple-element.22), channel_id=1, replica_groups={{0,32,64,96,128,160,192,224,256,288,320,352,384,416,448,480},{481,449,4..., dimensions={0} | all-to-all | bytes 3145728 | tf_op jit(solution)/shard_map/all_to_all | solution.py:394
  71.5 0.0 copy-done.2
  71.5 0.0 copy-start.4
  71.5 8.0 %all-to-all-start.1 = ((s16[16,48,768]{2,1,0:T(8,128)(2,1)}), s16[16,48,768]{2,1,0:T(8,128)(2,1)S(1)}, u32[]{:S(2)}, u32[]{:S(2)}) async-start(s16[16,48,768]{2,1,0:T(8,128)(2,1)} %copy-done.2), calls=%async_computation.1 | async-start | bytes 2359296 | tf_op jit(solution)/shard_map/all_to_all | solution.py:394
  79.4 0.0 copy-done.4
  79.4 0.0 copy-start
  79.5 1.0 shard_map.52.own_ref
  80.5 1.9 %collective-permute-start = (bf16[512,1024]{1,0:T(8,128)(2,1)S(1)}, bf16[512,1024]{1,0:T(8,128)(2,1)S(1)}, u32[]{:S(2)}, u32[]{:S(2)}) collective-permute-start(bf16[512,1024]{1,0:T(8,128)(2,1)S(1)} %shard_map.52.own_ref), channel_id=1, source_target_pairs={{0,1},{1,0},{2,3},{3,2},{4,5},{5,4},{6,7},{7,6},{8,9},{9,8},{10,11... | collective-permute-start | bytes 3145736 | tf_op jit(solution)/shard_map/ppermute | solution.py:420
  82.4 0.0 copy-done
  82.4 1.6 %shard_map.53 = (f32[512,512]{1,0:T(8,128)S(1)}, f32[256,512]{1,0:T(8,128)S(1)}, f32[256,1]{1,0:T(8,128)S(1)}, bf16[256,1024]{1,0:T(8,128)(2,1)S(1)}) custom-call(s32[4]{0:T(128)S(1)} %copy-done.5, bf16[256,2048]{1,0:T(8,128)(2,1)S(1)} %copy-done, bf16[512,1024]{1,0:T(8,128)(2,1)S(1)} %shard_map.52.own_ref), custom_call_target="tpu_custom_call" | custom-call | flops 1000000 | bytes 1000000 | tf_op jit(solution)/shard_map/pallas_call | solution.py:243
  84.0 1.0 collective-permute-done.oth_ref
  85.0 12.8 %shard_map.54 = (bf16[288,512]{1,0:T(8,128)(2,1)S(1)}, bf16[288,512]{1,0:T(8,128)(2,1)S(1)}) custom-call(s32[4]{0:T(128)S(1)} %copy-done.5, s32[8,512]{1,0:T(8,128)S(1)} %copy-done.4, bf16[256,1024]{1,0:T(8,128)(2,1)S(1)} %get-tuple-element.23.p_oth_ref, bf16[512,1024]{1,0:T(8,128)(2,1)S(1)} %collective-permute-done.oth_ref, ...), custom_call_target="tpu_custom_call" | custom-call | flops 1000000 | bytes 1000000 | tf_op jit(solution)/shard_map/pallas_call | solution.py:315
  97.8 0.0 all-to-all-done.1
  97.8 2.2 %collective-permute-start.1 = (s16[768,768]{1,0:T(8,128)(2,1)S(1)}, s16[768,768]{1,0:T(8,128)(2,1)S(1)}, u32[]{:S(2)}, u32[]{:S(2)}) collective-permute-start(s16[768,768]{1,0:T(8,128)(2,1)S(1)} %bitcast.13), channel_id=1, source_target_pairs={{0,1},{1,0},{2,3},{3,2},{4,5},{5,4},{6,7},{7,6},{8,9},{9,8},{10,11... | collective-permute-start | bytes 3538952 | tf_op jit(solution)/shard_map/ppermute | solution.py:424
  100.1 0.0 copy-start.1
  100.1 2.1 %shard_map.55 = (bf16[288,768]{1,0:T(8,128)(2,1)S(1)}, bf16[288,768]{1,0:T(8,128)(2,1)S(1)}, f32[288,512]{1,0:T(8,128)S(1)}) custom-call(s32[8,512]{1,0:T(8,128)S(1)} %copy-done.4, bf16[288,512]{1,0:T(8,128)(2,1)S(1)} %get-tuple-element.28.wh_ref, bf16[288,512]{1,0:T(8,128)(2,1)S(1)} %get-tuple-element.29.wl_ref, s16[768,768]{1,0:T(8,128)(2,1)S(1)} %bitcast.14), custom_call_target="tpu_custom_call" | custom-call | flops 2000000000 | bytes 4000000 | tf_op jit(solution)/shard_map/pallas_call | solution.py:351
  102.2 0.4 collective-permute-done.1.res_ref
  102.6 0.0 copy-done.1
  102.6 3.0 %shard_map.56 = (f32[1000,256]{1,0:T(8,128)}, f32[32,1000]{1,0:T(8,128)}) custom-call(s32[4]{0:T(128)S(1)} %copy-done.5, bf16[288,768]{1,0:T(8,128)(2,1)S(1)} %get-tuple-element.31.hi_ref, bf16[288,768]{1,0:T(8,128)(2,1)S(1)} %get-tuple-element.32.lo_ref, s16[768,768]{1,0:T(8,128)(2,1)S(1)} %collective-permute-done.1.res_ref, ...), custom_call_target="tpu_custom_call" | custom-call | tf_op jit(solution)/shard_map/pallas_call | solution.py:376
Async XLA Ops:
  1.2 42.5 %copy-start.5 = (s32[4]{0:T(128)S(1)}, s32[4]{0:T(128)}, u32[]{:S(2)}) copy-start(s32[4]{0:T(128)} %pad_add_fusion.info) | copy-start | bytes 52
  43.7 0.7 copy-start.3
  45.7 25.7 %copy-start.2 = (s16[16,48,768]{2,1,0:T(8,128)(2,1)}, s16[16,48,768]{2,1,0:T(8,128)(2,1)S(1)}, u32[]{:S(2)}) copy-start(s16[16,48,768]{2,1,0:T(8,128)(2,1)S(1)} %get-tuple-element.21) | copy-start | bytes 3538948
  71.5 8.0 %copy-start.4 = (s32[8,512]{1,0:T(8,128)S(1)}, s32[8,512]{1,0:T(8,128)}, u32[]{:S(2)}) copy-start(s32[8,512]{1,0:T(8,128)} %get-tuple-element.19.tab_ref) | copy-start | bytes 49156
  71.5 26.4 %all-to-all-start.1 = ((s16[16,48,768]{2,1,0:T(8,128)(2,1)}), s16[16,48,768]{2,1,0:T(8,128)(2,1)S(1)}, u32[]{:S(2)}, u32[]{:S(2)}) async-start(s16[16,48,768]{2,1,0:T(8,128)(2,1)} %copy-done.2), calls=%async_computation.1 | async-start | bytes 2359296 | tf_op jit(solution)/shard_map/all_to_all | solution.py:394
  79.4 3.0 %copy-start = (bf16[256,2048]{1,0:T(8,128)(2,1)S(1)}, bf16[256,2048]{1,0:T(8,128)(2,1)}, u32[]{:S(2)}) copy-start(bf16[256,2048]{1,0:T(8,128)(2,1)} %pts_ref.1) | copy-start | bytes 3145732
  80.5 4.6 %collective-permute-start = (bf16[512,1024]{1,0:T(8,128)(2,1)S(1)}, bf16[512,1024]{1,0:T(8,128)(2,1)S(1)}, u32[]{:S(2)}, u32[]{:S(2)}) collective-permute-start(bf16[512,1024]{1,0:T(8,128)(2,1)S(1)} %shard_map.52.own_ref), channel_id=1, source_target_pairs={{0,1},{1,0},{2,3},{3,2},{4,5},{5,4},{6,7},{7,6},{8,9},{9,8},{10,11... | collective-permute-start | bytes 3145736 | tf_op jit(solution)/shard_map/ppermute | solution.py:420
  97.8 4.7 %collective-permute-start.1 = (s16[768,768]{1,0:T(8,128)(2,1)S(1)}, s16[768,768]{1,0:T(8,128)(2,1)S(1)}, u32[]{:S(2)}, u32[]{:S(2)}) collective-permute-start(s16[768,768]{1,0:T(8,128)(2,1)S(1)} %bitcast.13), channel_id=1, source_target_pairs={{0,1},{1,0},{2,3},{3,2},{4,5},{5,4},{6,7},{7,6},{8,9},{9,8},{10,11... | collective-permute-start | bytes 3538952 | tf_op jit(solution)/shard_map/ppermute | solution.py:424
  100.1 2.5 %copy-start.1 = (f32[256,1000]{0,1:T(8,128)S(1)}, f32[256,1000]{0,1:T(8,128)}, u32[]{:S(2)}) copy-start(f32[256,1000]{0,1:T(8,128)} %param.4) | copy-start | bytes 3072004

commit v9 on v8

--- a/solution.py
+++ b/solution.py
@@ -28,7 +28,8 @@
 CLASS_STEP = 496
 CLASS_SPAN = 504
 SCALE_LANE = 511
-FRACTION = 2.0**22
+FRACTION = 500000.0
+CODED = 640
 MIB = 1024 * 1024
 
 
@@ -150,21 +151,23 @@
     top = jnp.max(jnp.abs(res), axis=1, keepdims=True)
     power = jnp.floor(jnp.log2(jnp.maximum(top, 1e-30))) + 1.0
     code = jnp.floor(res * (FRACTION / jnp.exp2(power)) + 0.5).astype(I32)
-    code = jnp.where(iota(res.shape, 1) == SCALE_LANE, power.astype(I32) * 256, code)
-    low = code & 255
-    half = res.shape[1] // 2
-    pair = (low[:, :half] | (low[:, half:] << 8)) - 32768
-    return jnp.concatenate([code >> 8, pair], axis=1).astype(jnp.int16)
+    code = jnp.where(iota(res.shape, 1) == SCALE_LANE, power.astype(I32) * 16, code)
+    low = code & 15
+    part = res.shape[1] // 4
+    word = low[:, :part]
+    for k in range(1, 4):
+        word = word | (low[:, k * part : (k + 1) * part] << (4 * k))
+    return jnp.concatenate([code >> 4, word - 32768], axis=1).astype(jnp.int16)
 
 
 def decode(words):
     words = words.astype(I32)
-    n = words.shape[1] * 2 // 3
+    n = words.shape[1] * 4 // 5
     high = words[:, :n]
-    pair = words[:, n:] + 32768
-    low = jnp.concatenate([pair & 255, pair >> 8], axis=1)
+    word = words[:, n:] + 32768
+    low = jnp.concatenate([(word >> (4 * k)) & 15 for k in range(4)], axis=1)
     unit = jnp.exp2(high[:, SCALE_LANE : SCALE_LANE + 1].astype(F32)) * (1.0 / FRACTION)
-    return (high * 256 + low).astype(F32) * unit
+    return (high * 16 + low).astype(F32) * unit
 
 
 def compact_body(info, tab_ref, in_ref, pts_ref, res_ref, *, rows, n_col):
@@ -197,7 +200,7 @@
         functools.partial(compact_body, rows=rows, n_col=n_col),
         out_shape=(
             jax.ShapeDtypeStruct((n_plane, COL_CAP, half), BF),
-            jax.ShapeDtypeStruct((n_plane, COL_CAP, CLASS_PAD * 3 // 4), jnp.int16),
+            jax.ShapeDtypeStruct((n_plane, COL_CAP, CODED), jnp.int16),
         ),
         in_specs=[smem(), vmem(), vmem()],
         out_specs=(vmem(), vmem()),
@@ -325,7 +328,7 @@
             pltpu.VMEM((n, n), F32),
         ],
         compiler_params=params(18),
-        cost_estimate=pl.CostEstimate(flops=10**6, bytes_accessed=10**6, transcendentals=0),
+        cost_estimate=pl.CostEstimate(flops=12 * 10**9, bytes_accessed=6 * 10**6, transcendentals=4 * 10**5),
     )(info, tab, p_oth, oth, cross, p_cross, psq)
 
 
@@ -415,7 +418,7 @@
     col_rows = col_rows.reshape(n_col * CAP * SPLIT, col_rows.shape[2])
     pts_out, res_out = compact(info, tab, col_rows, rows, half, n_plane, n_col)
     all_pts = over_plane(pts_out).reshape(wide, half)
-    all_res = over_plane(res_out).reshape(wide, CLASS_PAD * 3 // 4)
+    all_res = over_plane(res_out).reshape(wide, CODED)
     own = order(tab, all_pts)
     other = lax.ppermute(own, "c", swap)
     cross, p_cross, psq, p_oth = first_half(info, points, own)

time: 106 us -> 107 us (level)
  starting transfers between devices: 12.1 us -> 13.3 us
  waiting for transfers between devices: 1.46 us -> 0.26 us
    ppermute x1, starting transfers between devices: 1.92 us -> 4.13 us  [on_device(): other = lax.ppermute(own, 'c', swap)]
  transfers between devices with their start and end apart: 3 -> 3, of which waited for: 2 -> 1; matrix products, arithmetic and copies ran while one was open for 0% -> 0% of each run, Pallas kernels for 17% -> 16%
where the time goes in v9:
time: 107 us; the launch traced here: 106 us
  blocking collectives  64.5 us (60%)
  Pallas kernels  26.2 us (24%)
  starting transfers between devices  13.3 us (12%)
    all_to_all x1, blocking collectives, on_device(): col_rows = lax.all_to_all(packed, COLUMN, 0, 0, tiled=True)  38.8 us
    all_to_all x1, blocking collectives, over_plane(): lax.all_to_all(value, EVERY, 0, 0, axis_index_groups=plane_groups(), tile...  25.7 us
    pallas_call x1, Pallas kernels, inverse(): pl.pallas_call(functools.partial(inverse_body, share=share), out_shape=(o...  13.5 us
    all_to_all x1, starting transfers between devices, over_plane(): lax.all_to_all(value, EVERY, 0, 0, axis_index_groups=plane_groups(), tile...  7.05 us
    ppermute x1, starting transfers between devices, on_device(): other = lax.ppermute(own, 'c', swap)  4.13 us
    pallas_call x1, Pallas kernels, pack(): pl.pallas_call(functools.partial(pack_body, n_plane=n_plane, n_col=n_col)...  3.69 us
    pallas_call x1, Pallas kernels, update_other(): pl.pallas_call(update_other_body, out_shape=(jax.ShapeDtypeStruct((classe...  3.01 us
  transfers between devices with their start and end apart: 3, of which 1 were waited for; matrix products, arithmetic and copies ran while one was open for 0% of the time, Pallas kernels for 16%

profile of v9, /device:TPU:1, one launch (start us, length us, event | category | flops | bytes accessed | tf_op | source)
XLA Modules:
  0.0 106.3 jit_solution(11980871449518624309)
XLA Ops:
  0.6 0.6 pad_add_fusion.info
  1.2 0.0 copy-start.5
  1.2 3.7 %shard_map.50 = (bf16[32,8,512]{2,1,0:T(8,128)(2,1)}, s32[8,512]{1,0:T(8,128)}) custom-call(s32[4]{0:T(128)} %pad_add_fusion.info, s32[1,512]{1,0:T(1,128)} %bitcast.16, bf16[256,2048]{1,0:T(8,128)(2,1)} %pts_ref.1, f32[1000,256]{1,0:T(8,128)} %bitcast.11), custom_call_target="tpu_custom_call" | custom-call | tf_op jit(solution)/shard_map/pallas_call | solution.py:128
  4.9 38.8 %all_to_all.15 = bf16[32,8,512]{2,1,0:T(8,128)(2,1)S(1)} all-to-all(bf16[32,8,512]{2,1,0:T(8,128)(2,1)} %get-tuple-element.20), channel_id=1, replica_groups=mesh['y'=4,'x'=4,'zh'=2,'zl'=8,'c'=2] {'zh','zl','c'}, dimensions={0} | all-to-all | bytes 524288 | tf_op jit(solution)/shard_map/all_to_all | solution.py:417
  43.7 0.0 copy-done.5
  43.7 0.0 copy-start.3
  43.7 0.7 copy-done.3
  44.4 1.3 %shard_map.51 = (bf16[16,48,1024]{2,1,0:T(8,128)(2,1)S(1)}, s16[16,48,640]{2,1,0:T(8,128)(2,1)S(1)}) custom-call(s32[4]{0:T(128)S(1)} %copy-done.5, s32[8,512]{1,0:T(8,128)S(1)} %copy-done.3, bf16[256,512]{1,0:T(8,128)(2,1)S(1)} %bitcast.13), custom_call_target="tpu_custom_call" | custom-call | tf_op jit(solution)/shard_map/pallas_call | solution.py:199
  45.7 0.0 copy-start.2
  45.7 25.7 %all_to_all.16 = bf16[16,48,1024]{2,1,0:T(8,128)(2,1)S(1)} all-to-all(bf16[16,48,1024]{2,1,0:T(8,128)(2,1)S(1)} %get-tuple-element.22), channel_id=1, replica_groups={{0,32,64,96,128,160,192,224,256,288,320,352,384,416,448,480},{481,449,4..., dimensions={0} | all-to-all | bytes 3145728 | tf_op jit(solution)/shard_map/all_to_all | solution.py:397
  71.5 0.0 copy-done.2
  71.5 1.0 shard_map.52.own_ref
  72.5 0.0 copy-start
  72.5 4.1 %collective-permute-start = (bf16[512,1024]{1,0:T(8,128)(2,1)S(1)}, bf16[512,1024]{1,0:T(8,128)(2,1)}, u32[]{:S(2)}, u32[]{:S(2)}) collective-permute-start(bf16[512,1024]{1,0:T(8,128)(2,1)S(1)} %shard_map.52.own_ref), channel_id=1, source_target_pairs={{0,1},{1,0},{2,3},{3,2},{4,5},{5,4},{6,7},{7,6},{8,9},{9,8},{10,11... | collective-permute-start | bytes 3145736 | tf_op jit(solution)/shard_map/ppermute | solution.py:423
  76.6 0.0 copy-start.4
  76.6 7.0 %all-to-all-start.1 = ((s16[16,48,640]{2,1,0:T(8,128)(2,1)}), s16[16,48,640]{2,1,0:T(8,128)(2,1)S(1)}, u32[]{:S(2)}, u32[]{:S(2)}) async-start(s16[16,48,640]{2,1,0:T(8,128)(2,1)} %copy-done.2), calls=%async_computation.1 | async-start | bytes 1966080 | tf_op jit(solution)/shard_map/all_to_all | solution.py:397
  83.7 0.0 copy-done
  83.7 1.6 %shard_map.53 = (f32[512,512]{1,0:T(8,128)S(1)}, f32[256,512]{1,0:T(8,128)S(1)}, f32[256,1]{1,0:T(8,128)S(1)}, bf16[256,1024]{1,0:T(8,128)(2,1)S(1)}) custom-call(s32[4]{0:T(128)S(1)} %copy-done.5, bf16[256,2048]{1,0:T(8,128)(2,1)S(1)} %copy-done, bf16[512,1024]{1,0:T(8,128)(2,1)S(1)} %shard_map.52.own_ref), custom_call_target="tpu_custom_call" | custom-call | flops 1000000 | bytes 1000000 | tf_op jit(solution)/shard_map/pallas_call | solution.py:246
  85.3 0.0 collective-permute-done.oth_ref
  85.3 0.0 copy-done.4
  85.3 13.5 %shard_map.54 = (bf16[288,512]{1,0:T(8,128)(2,1)S(1)}, bf16[288,512]{1,0:T(8,128)(2,1)S(1)}) custom-call(s32[4]{0:T(128)S(1)} %copy-done.5, s32[8,512]{1,0:T(8,128)S(1)} %copy-done.4, bf16[256,1024]{1,0:T(8,128)(2,1)S(1)} %get-tuple-element.23.p_oth_ref, bf16[512,1024]{1,0:T(8,128)(2,1)} %collective-permute-done.oth_ref, ...), custom_call_target="tpu_custom_call" | custom-call | flops 12000000000 | bytes 6000000 | tf_op jit(solution)/shard_map/pallas_call | solution.py:318
  98.8 0.0 all-to-all-done.1
  98.8 2.1 %collective-permute-start.1 = (s16[768,640]{1,0:T(8,128)(2,1)S(1)}, s16[768,640]{1,0:T(8,128)(2,1)S(1)}, u32[]{:S(2)}, u32[]{:S(2)}) collective-permute-start(s16[768,640]{1,0:T(8,128)(2,1)S(1)} %bitcast.14), channel_id=1, source_target_pairs={{0,1},{1,0},{2,3},{3,2},{4,5},{5,4},{6,7},{7,6},{8,9},{9,8},{10,11... | collective-permute-start | bytes 2949128 | tf_op jit(solution)/shard_map/ppermute | solution.py:427
  100.9 0.0 copy-start.1
  100.9 2.1 %shard_map.55 = (bf16[288,768]{1,0:T(8,128)(2,1)S(1)}, bf16[288,768]{1,0:T(8,128)(2,1)S(1)}, f32[288,512]{1,0:T(8,128)S(1)}) custom-call(s32[8,512]{1,0:T(8,128)S(1)} %copy-done.4, bf16[288,512]{1,0:T(8,128)(2,1)S(1)} %get-tuple-element.28.wh_ref, bf16[288,512]{1,0:T(8,128)(2,1)S(1)} %get-tuple-element.29.wl_ref, s16[768,640]{1,0:T(8,128)(2,1)S(1)} %bitcast.15), custom_call_target="tpu_custom_call" | custom-call | flops 2000000000 | bytes 4000000 | tf_op jit(solution)/shard_map/pallas_call | solution.py:354
  103.0 0.3 collective-permute-done.1.res_ref
  103.3 0.0 copy-done.1
  103.3 3.0 %shard_map.56 = (f32[1000,256]{1,0:T(8,128)}, f32[32,1000]{1,0:T(8,128)}) custom-call(s32[4]{0:T(128)S(1)} %copy-done.5, bf16[288,768]{1,0:T(8,128)(2,1)S(1)} %get-tuple-element.31.hi_ref, bf16[288,768]{1,0:T(8,128)(2,1)S(1)} %get-tuple-element.32.lo_ref, s16[768,640]{1,0:T(8,128)(2,1)S(1)} %collective-permute-done.1.res_ref, ...), custom_call_target="tpu_custom_call" | custom-call | tf_op jit(solution)/shard_map/pallas_call | solution.py:379
Async XLA Ops:
  1.2 42.5 %copy-start.5 = (s32[4]{0:T(128)S(1)}, s32[4]{0:T(128)}, u32[]{:S(2)}) copy-start(s32[4]{0:T(128)} %pad_add_fusion.info) | copy-start | bytes 52
  43.7 0.7 copy-start.3
  45.7 25.7 %copy-start.2 = (s16[16,48,640]{2,1,0:T(8,128)(2,1)}, s16[16,48,640]{2,1,0:T(8,128)(2,1)S(1)}, u32[]{:S(2)}) copy-start(s16[16,48,640]{2,1,0:T(8,128)(2,1)S(1)} %get-tuple-element.21) | copy-start | bytes 2949124
  72.5 11.2 %copy-start = (bf16[256,2048]{1,0:T(8,128)(2,1)S(1)}, bf16[256,2048]{1,0:T(8,128)(2,1)}, u32[]{:S(2)}) copy-start(bf16[256,2048]{1,0:T(8,128)(2,1)} %pts_ref.1) | copy-start | bytes 3145732
  72.5 12.8 %collective-permute-start = (bf16[512,1024]{1,0:T(8,128)(2,1)S(1)}, bf16[512,1024]{1,0:T(8,128)(2,1)}, u32[]{:S(2)}, u32[]{:S(2)}) collective-permute-start(bf16[512,1024]{1,0:T(8,128)(2,1)S(1)} %shard_map.52.own_ref), channel_id=1, source_target_pairs={{0,1},{1,0},{2,3},{3,2},{4,5},{5,4},{6,7},{7,6},{8,9},{9,8},{10,11... | collective-permute-start | bytes 3145736 | tf_op jit(solution)/shard_map/ppermute | solution.py:423
  76.6 8.7 %copy-start.4 = (s32[8,512]{1,0:T(8,128)S(1)}, s32[8,512]{1,0:T(8,128)}, u32[]{:S(2)}) copy-start(s32[8,512]{1,0:T(8,128)} %get-tuple-element.19.tab_ref) | copy-start | bytes 49156
  76.6 22.2 %all-to-all-start.1 = ((s16[16,48,640]{2,1,0:T(8,128)(2,1)}), s16[16,48,640]{2,1,0:T(8,128)(2,1)S(1)}, u32[]{:S(2)}, u32[]{:S(2)}) async-start(s16[16,48,640]{2,1,0:T(8,128)(2,1)} %copy-done.2), calls=%async_computation.1 | async-start | bytes 1966080 | tf_op jit(solution)/shard_map/all_to_all | solution.py:397
  98.8 4.5 %collective-permute-start.1 = (s16[768,640]{1,0:T(8,128)(2,1)S(1)}, s16[768,640]{1,0:T(8,128)(2,1)S(1)}, u32[]{:S(2)}, u32[]{:S(2)}) collective-permute-start(s16[768,640]{1,0:T(8,128)(2,1)S(1)} %bitcast.14), channel_id=1, source_target_pairs={{0,1},{1,0},{2,3},{3,2},{4,5},{5,4},{6,7},{7,6},{8,9},{9,8},{10,11... | collective-permute-start | bytes 2949128 | tf_op jit(solution)/shard_map/ppermute | solution.py:427
  100.9 2.4 %copy-start.1 = (f32[256,1000]{0,1:T(8,128)S(1)}, f32[256,1000]{0,1:T(8,128)}, u32[]{:S(2)}) copy-start(f32[256,1000]{0,1:T(8,128)} %param.4) | copy-start | bytes 3072004

commit v10 on v8

--- a/solution.py
+++ b/solution.py
@@ -55,10 +55,6 @@
     return pl.BlockSpec(memory_space=pltpu.VMEM)
 
 
-def smem():
-    return pl.BlockSpec(memory_space=pltpu.SMEM)
-
-
 def hbm():
     return pl.BlockSpec(memory_space=pltpu.HBM)
 
@@ -67,8 +63,20 @@
     return pltpu.CompilerParams(vmem_limit_bytes=mib * MIB)
 
 
-def pack_body(info, ids_hbm, pts_hbm, res_hbm, out_ref, tab_ref, ids_ref, pts_ref, res_ref, sems, *, n_plane, n_col):
-    me = info[2]
+def my_core():
+    return lax.axis_index("c")
+
+
+def my_plane():
+    return lax.axis_index("y") * 4 + lax.axis_index("x")
+
+
+def my_place():
+    return (lax.axis_index("zh") * 8 + lax.axis_index("zl")) * 2 + my_core()
+
+
+def pack_body(ids_hbm, pts_hbm, res_hbm, out_ref, tab_ref, ids_ref, pts_ref, res_ref, sems, *, n_plane, n_col):
+    me = my_plane() * n_col + my_place()
     rows = pts_ref.shape[0]
     ids_in = pltpu.make_async_copy(ids_hbm, ids_ref, sems.at[0])
     pts_in = pltpu.make_async_copy(pts_hbm, pts_ref, sems.at[1])
@@ -89,8 +97,8 @@
     planes = COL_CAP * n_plane
     straight = column * COL_CAP + rank
     turned = planes - COL_CAP - column * COL_CAP + rank
-    here = jnp.where(info[0] == 0, straight, turned)
-    there = jnp.where(info[0] == 0, turned, straight)
+    here = jnp.where(my_core() == 0, straight, turned)
+    there = jnp.where(my_core() == 0, turned, straight)
     tab_ref[...] = jnp.concatenate([ids, rank, slot, here, there, jnp.zeros((3, n), I32)], axis=0)
     mine = owner == me
     lane = iota((8, rows), 1)
@@ -121,7 +129,7 @@
             out_ref[2 * z + core] = block
 
 
-def pack(info, ids, points, res_t, n_plane, n_col):
+def pack(ids, points, res_t, n_plane, n_col):
     width = points.shape[1] // 2 + CLASS_PAD
     n = ids.shape[1]
     return pl.pallas_call(
@@ -130,7 +138,7 @@
             jax.ShapeDtypeStruct((n_col, CAP * SPLIT, width // SPLIT), BF),
             jax.ShapeDtypeStruct((8, n), I32),
         ),
-        in_specs=[smem(), hbm(), hbm(), hbm()],
+        in_specs=[hbm(), hbm(), hbm()],
         out_specs=(vmem(), vmem()),
         scratch_shapes=[
             pltpu.VMEM(ids.shape, I32),
@@ -139,7 +147,7 @@
             pltpu.SemaphoreType.DMA((3,)),
         ],
         compiler_params=params(60),
-    )(info, ids, points, res_t)
+    )(ids, points, res_t)
 
 
 def table(tab_ref):
@@ -167,8 +175,8 @@
     return (high * 256 + low).astype(F32) * unit
 
 
-def compact_body(info, tab_ref, in_ref, pts_ref, res_ref, *, rows, n_col):
-    plane = info[1]
+def compact_body(tab_ref, in_ref, pts_ref, res_ref, *, rows, n_col):
+    plane = my_plane()
     ids, rank, slot = table(tab_ref)
     n = ids.shape[1]
     owner = ids // rows
@@ -192,17 +200,17 @@
         res_ref[p] = res
 
 
-def compact(info, tab, data, rows, half, n_plane, n_col):
+def compact(tab, data, rows, half, n_plane, n_col):
     return pl.pallas_call(
         functools.partial(compact_body, rows=rows, n_col=n_col),
         out_shape=(
             jax.ShapeDtypeStruct((n_plane, COL_CAP, half), BF),
             jax.ShapeDtypeStruct((n_plane, COL_CAP, CLASS_PAD * 3 // 4), jnp.int16),
         ),
-        in_specs=[smem(), vmem(), vmem()],
+        in_specs=[vmem(), vmem()],
         out_specs=(vmem(), vmem()),
         compiler_params=params(16),
-    )(info, tab, data)
+    )(tab, data)
 
 
 def place_matrix(tab_ref, wide, row=3):
@@ -224,8 +232,8 @@
     )(tab, data)
 
 
-def first_half_body(info, pts_ref, own_ref, cross_ref, p_cross_ref, psq_ref, p_oth_ref, *, half):
-    core = info[0]
+def first_half_body(pts_ref, own_ref, cross_ref, p_cross_ref, psq_ref, p_oth_ref, *, half):
+    core = my_core()
     own = own_ref[...]
     cross_ref[...] = dot(own, own, NT)
     p_own = pts_ref[:, pl.ds(pl.multiple_of(core * half, half), half)]
@@ -237,7 +245,7 @@
     psq_ref[...] = jnp.sum(a * a, axis=1, keepdims=True) + jnp.sum(b * b, axis=1, keepdims=True)
 
 
-def first_half(info, points, own):
+def first_half(points, own):
     n, half = own.shape
     rows = points.shape[0]
     return pl.pallas_call(
@@ -248,17 +256,18 @@
             jax.ShapeDtypeStruct((rows, 1), F32),
             jax.ShapeDtypeStruct((rows, half), BF),
         ),
-        in_specs=[smem(), vmem(), vmem()],
+        in_specs=[vmem(), vmem()],
         out_specs=(vmem(),) * 4,
         compiler_params=params(12),
         cost_estimate=pl.CostEstimate(flops=10**6, bytes_accessed=10**6, transcendentals=0),
-    )(info, points, own)
-
-
-def inverse_body(info, tab_ref, p_oth_ref, oth_ref, cross_ref, p_cross_ref, psq_ref, hi_ref, lo_ref, g_ref, m_ref, gh_ref, gl_ref, x_ref, *, share):
+    )(points, own)
+
+
+def inverse_body(tab_ref, p_oth_ref, oth_ref, cross_ref, p_cross_ref, psq_ref, hi_ref, lo_ref, g_ref, m_ref, gh_ref, gl_ref, x_ref, *, share):
     n = oth_ref.shape[0]
     rows = p_cross_ref.shape[0]
-    me, share_at = info[2], info[3]
+    me = my_plane() * 32 + my_place()
+    share_at = lax.rem(my_place(), 16) * share
     oth = oth_ref[...]
     cross = cross_ref[...] + dot(oth, oth, NT)
     eye = iota((n, n), 0) == iota((n, n), 1)
@@ -308,14 +317,14 @@
     lo_ref[...] = wl
 
 
-def inverse(info, tab, p_oth, oth, cross, p_cross, psq, share):
+def inverse(tab, p_oth, oth, cross, p_cross, psq, share):
     n = oth.shape[0]
     rows = p_oth.shape[0]
     out = jax.ShapeDtypeStruct((rows + share, n), BF)
     return pl.pallas_call(
         functools.partial(inverse_body, share=share),
         out_shape=(out, out),
-        in_specs=[smem()] + [vmem()] * 6,
+        in_specs=[vmem()] * 6,
         out_specs=(vmem(), vmem()),
         scratch_shapes=[
             pltpu.VMEM((n, n), F32),
@@ -326,7 +335,7 @@
         ],
         compiler_params=params(18),
         cost_estimate=pl.CostEstimate(flops=10**6, bytes_accessed=10**6, transcendentals=0),
-    )(info, tab, p_oth, oth, cross, p_cross, psq)
+    )(tab, p_oth, oth, cross, p_cross, psq)
 
 
 def apply_weights(hi, lo, res_ref):
@@ -358,8 +367,8 @@
     )(tab, wh, wl, res)
 
 
-def update_other_body(info, hi_ref, lo_ref, res_ref, ch_ref, res_t_ref, out_ref, share_ref):
-    core = info[0]
+def update_other_body(hi_ref, lo_ref, res_ref, ch_ref, res_t_ref, out_ref, share_ref):
+    core = my_core()
     classes, rows = res_t_ref.shape
     skip = 2 * CLASS_SPAN - classes
     mine = ch_ref[...]
@@ -371,15 +380,15 @@
     out_ref[CLASS_SPAN:, :] = res_t_ref[CLASS_SPAN:, :] - high[:rows].T[skip:CLASS_SPAN]
 
 
-def update_other(info, hi, lo, res, change, res_t, share):
+def update_other(hi, lo, res, change, res_t, share):
     classes, rows = res_t.shape
     return pl.pallas_call(
         update_other_body,
         out_shape=(jax.ShapeDtypeStruct((classes, rows), F32), jax.ShapeDtypeStruct((share, classes), F32)),
-        in_specs=[smem()] + [vmem()] * 5,
+        in_specs=[vmem()] * 5,
         out_specs=(vmem(), vmem()),
         compiler_params=params(16),
-    )(info, hi, lo, res, change, res_t)
+    )(hi, lo, res, change, res_t)
 
 
 def plane_groups():
@@ -405,25 +414,24 @@
     share = block // n_gy
     half = feats // 2
     wide = n_plane * COL_CAP
-    info = jnp.stack([lax.axis_index("c"), plane, plane * n_col + place, (place % n_gy) * share]).astype(I32)
     ids = block_ids.reshape(1, block)
     res_t = residual.T
     swap = [(0, 1), (1, 0)]
 
-    packed, tab = pack(info, ids, points, res_t, n_plane, n_col)
+    packed, tab = pack(ids, points, res_t, n_plane, n_col)
     col_rows = lax.all_to_all(packed, COLUMN, 0, 0, tiled=True)
     col_rows = col_rows.reshape(n_col * CAP * SPLIT, col_rows.shape[2])
-    pts_out, res_out = compact(info, tab, col_rows, rows, half, n_plane, n_col)
+    pts_out, res_out = compact(tab, col_rows, rows, half, n_plane, n_col)
     all_pts = over_plane(pts_out).reshape(wide, half)
     all_res = over_plane(res_out).reshape(wide, CLASS_PAD * 3 // 4)
     own = order(tab, all_pts)
     other = lax.ppermute(own, "c", swap)
-    cross, p_cross, psq, p_oth = first_half(info, points, own)
-    wh, wl = inverse(info, tab, p_oth, other, cross, p_cross, psq, share)
+    cross, p_cross, psq, p_oth = first_half(points, own)
+    wh, wl = inverse(tab, p_oth, other, cross, p_cross, psq, share)
     all_res, wh = lax.optimization_barrier((all_res, wh))
     other_res = lax.ppermute(all_res, "c", swap)
     hi, lo, change = update_own(tab, wh, wl, all_res)
-    out_t, step_share = update_other(info, hi, lo, other_res, change, res_t, share)
+    out_t, step_share = update_other(hi, lo, other_res, change, res_t, share)
     return (out_t.T, step_share)
 
 

time: 106 us -> 103 us (0.972)
  Pallas kernels: 25.5 us -> 22.5 us
  transfers between devices with their start and end apart: 3 -> 3, of which waited for: 2 -> 2; matrix products, arithmetic and copies ran while one was open for 0% -> 0% of each run, Pallas kernels for 17% -> 16%
where the time goes in v10:
time: 103 us
  blocking collectives  64.5 us (63%)
  Pallas kernels  22.5 us (22%)
  starting transfers between devices  12.1 us (12%)
  waiting for transfers between devices  1.99 us (2%)
    all_to_all x1, blocking collectives, on_device(): col_rows = lax.all_to_all(packed, COLUMN, 0, 0, tiled=True)  38.8 us
    all_to_all x1, blocking collectives, over_plane(): lax.all_to_all(value, EVERY, 0, 0, axis_index_groups=plane_groups(), tile...  25.7 us
    pallas_call x1, Pallas kernels, inverse(): pl.pallas_call(functools.partial(inverse_body, share=share), out_shape=(o...  12.3 us
    all_to_all x1, starting transfers between devices, over_plane(): lax.all_to_all(value, EVERY, 0, 0, axis_index_groups=plane_groups(), tile...  7.97 us
    pallas_call x1, Pallas kernels, pack(): pl.pallas_call(functools.partial(pack_body, n_plane=n_plane, n_col=n_col)...  2.9 us
    pallas_call x1, Pallas kernels, update_other(): pl.pallas_call(update_other_body, out_shape=(jax.ShapeDtypeStruct((classe...  2.47 us
    ppermute x1, starting transfers between devices, on_device(): other_res = lax.ppermute(all_res, 'c', swap)  2.22 us
    pallas_call x1, Pallas kernels, update_own(): pl.pallas_call(update_own_body, out_shape=(out, out, jax.ShapeDtypeStruct...  2.06 us
  transfers between devices with their start and end apart: 3, of which 2 were waited for; matrix products, arithmetic and copies ran while one was open for 0% of the time, Pallas kernels for 16%

profile of v10, /device:TPU:1, one launch (start us, length us, event | category | flops | bytes accessed | tf_op | source)
XLA Modules:
  0.0 102.6 jit_solution(3366967023130357710)
XLA Ops:
  0.6 2.9 %shard_map.50 = (bf16[32,8,512]{2,1,0:T(8,128)(2,1)}, s32[8,512]{1,0:T(8,128)}) custom-call(s32[1,512]{1,0:T(1,128)} %bitcast.12, bf16[256,2048]{1,0:T(8,128)(2,1)} %pts_ref.1, f32[1000,256]{1,0:T(8,128)} %bitcast.7), custom_call_target="tpu_custom_call" | custom-call | tf_op jit(solution)/shard_map/pallas_call | solution.py:135
  3.5 38.8 %all_to_all.15 = bf16[32,8,512]{2,1,0:T(8,128)(2,1)S(1)} all-to-all(bf16[32,8,512]{2,1,0:T(8,128)(2,1)} %get-tuple-element.20), channel_id=1, replica_groups=mesh['y'=4,'x'=4,'zh'=2,'zl'=8,'c'=2] {'zh','zl','c'}, dimensions={0} | all-to-all | bytes 524288 | tf_op jit(solution)/shard_map/all_to_all | solution.py:422
  42.3 0.0 copy-start.3
  42.3 0.7 copy-done.3
  43.0 0.8 shard_map.51
  43.8 0.0 copy-start.2
  43.8 25.7 %all_to_all.16 = bf16[16,48,1024]{2,1,0:T(8,128)(2,1)S(1)} all-to-all(bf16[16,48,1024]{2,1,0:T(8,128)(2,1)S(1)} %get-tuple-element.22), channel_id=1, replica_groups={{0,32,64,96,128,160,192,224,256,288,320,352,384,416,448,480},{481,449,4..., dimensions={0} | all-to-all | bytes 3145728 | tf_op jit(solution)/shard_map/all_to_all | solution.py:403
  69.5 0.0 copy-done.2
  69.5 0.0 copy-start.4
  69.6 8.0 %all-to-all-start.1 = ((s16[16,48,768]{2,1,0:T(8,128)(2,1)}), s16[16,48,768]{2,1,0:T(8,128)(2,1)S(1)}, u32[]{:S(2)}, u32[]{:S(2)}) async-start(s16[16,48,768]{2,1,0:T(8,128)(2,1)} %copy-done.2), calls=%async_computation.1 | async-start | bytes 2359296 | tf_op jit(solution)/shard_map/all_to_all | solution.py:403
  77.5 0.0 copy-done.4
  77.5 0.0 copy-start
  77.5 1.0 shard_map.52.own_ref
  78.6 1.9 %collective-permute-start = (bf16[512,1024]{1,0:T(8,128)(2,1)S(1)}, bf16[512,1024]{1,0:T(8,128)(2,1)S(1)}, u32[]{:S(2)}, u32[]{:S(2)}) collective-permute-start(bf16[512,1024]{1,0:T(8,128)(2,1)S(1)} %shard_map.52.own_ref), channel_id=1, source_target_pairs={{0,1},{1,0},{2,3},{3,2},{4,5},{5,4},{6,7},{7,6},{8,9},{9,8},{10,11... | collective-permute-start | bytes 3145736 | tf_op jit(solution)/shard_map/ppermute | solution.py:428
  80.5 0.0 copy-done
  80.5 1.1 %shard_map.53 = (f32[512,512]{1,0:T(8,128)S(1)}, f32[256,512]{1,0:T(8,128)S(1)}, f32[256,1]{1,0:T(8,128)S(1)}, bf16[256,1024]{1,0:T(8,128)(2,1)S(1)}) custom-call(bf16[256,2048]{1,0:T(8,128)(2,1)S(1)} %copy-done, bf16[512,1024]{1,0:T(8,128)(2,1)S(1)} %shard_map.52.own_ref), custom_call_target="tpu_custom_call" | custom-call | flops 1000000 | bytes 1000000 | tf_op jit(solution)/shard_map/pallas_call | solution.py:251
  81.5 1.6 %collective-permute-done.oth_ref = bf16[512,1024]{1,0:T(8,128)(2,1)S(1)} collective-permute-done((bf16[512,1024]{1,0:T(8,128)(2,1)S(1)}, bf16[512,1024]{1,0:T(8,128)(2,1)S(1)}, u32[]{:S(2)}, u32[]{:S(2)}) %collective-permute-start) | collective-permute-done | bytes 1048608 | tf_op jit(solution)/shard_map/ppermute | solution.py:428
  83.1 12.3 %shard_map.54 = (bf16[288,512]{1,0:T(8,128)(2,1)S(1)}, bf16[288,512]{1,0:T(8,128)(2,1)S(1)}) custom-call(s32[8,512]{1,0:T(8,128)S(1)} %copy-done.4, bf16[256,1024]{1,0:T(8,128)(2,1)S(1)} %get-tuple-element.23.p_oth_ref, bf16[512,1024]{1,0:T(8,128)(2,1)S(1)} %collective-permute-done.oth_ref, f32[512,512]{1,0:T(8,128)S(1)} %get-tuple-element.24.cross_ref, ...), custom_call_target="tpu_custom_call" | custom-call | flops 1000000 | bytes 1000000 | tf_op jit(solution)/shard_map/pallas_call | solution.py:324
  95.4 0.0 all-to-all-done.1
  95.4 2.2 %collective-permute-start.1 = (s16[768,768]{1,0:T(8,128)(2,1)S(1)}, s16[768,768]{1,0:T(8,128)(2,1)S(1)}, u32[]{:S(2)}, u32[]{:S(2)}) collective-permute-start(s16[768,768]{1,0:T(8,128)(2,1)S(1)} %bitcast.9), channel_id=1, source_target_pairs={{0,1},{1,0},{2,3},{3,2},{4,5},{5,4},{6,7},{7,6},{8,9},{9,8},{10,11... | collective-permute-start | bytes 3538952 | tf_op jit(solution)/shard_map/ppermute | solution.py:432
  97.6 0.0 copy-start.1
  97.6 2.1 %shard_map.55 = (bf16[288,768]{1,0:T(8,128)(2,1)S(1)}, bf16[288,768]{1,0:T(8,128)(2,1)S(1)}, f32[288,512]{1,0:T(8,128)S(1)}) custom-call(s32[8,512]{1,0:T(8,128)S(1)} %copy-done.4, bf16[288,512]{1,0:T(8,128)(2,1)S(1)} %get-tuple-element.28.wh_ref, bf16[288,512]{1,0:T(8,128)(2,1)S(1)} %get-tuple-element.29.wl_ref, s16[768,768]{1,0:T(8,128)(2,1)S(1)} %bitcast.10), custom_call_target="tpu_custom_call" | custom-call | flops 2000000000 | bytes 4000000 | tf_op jit(solution)/shard_map/pallas_call | solution.py:360
  99.7 0.4 collective-permute-done.1.res_ref
  100.1 0.0 copy-done.1
  100.1 2.5 %shard_map.56 = (f32[1000,256]{1,0:T(8,128)}, f32[32,1000]{1,0:T(8,128)}) custom-call(bf16[288,768]{1,0:T(8,128)(2,1)S(1)} %get-tuple-element.31.hi_ref, bf16[288,768]{1,0:T(8,128)(2,1)S(1)} %get-tuple-element.32.lo_ref, s16[768,768]{1,0:T(8,128)(2,1)S(1)} %collective-permute-done.1.res_ref, f32[288,512]{1,0:T(8,128)S(1)} %get-tuple-element.33.ch_ref, ...), custom_call_target="tpu_custom_call" | custom-call | tf_op jit(solution)/shard_map/pallas_call | solution.py:385
Async XLA Ops:
  42.3 0.7 copy-start.3
  43.8 25.7 %copy-start.2 = (s16[16,48,768]{2,1,0:T(8,128)(2,1)}, s16[16,48,768]{2,1,0:T(8,128)(2,1)S(1)}, u32[]{:S(2)}) copy-start(s16[16,48,768]{2,1,0:T(8,128)(2,1)S(1)} %get-tuple-element.21) | copy-start | bytes 3538948
  69.5 8.0 %copy-start.4 = (s32[8,512]{1,0:T(8,128)S(1)}, s32[8,512]{1,0:T(8,128)}, u32[]{:S(2)}) copy-start(s32[8,512]{1,0:T(8,128)} %get-tuple-element.19.tab_ref) | copy-start | bytes 49156
  69.6 25.8 %all-to-all-start.1 = ((s16[16,48,768]{2,1,0:T(8,128)(2,1)}), s16[16,48,768]{2,1,0:T(8,128)(2,1)S(1)}, u32[]{:S(2)}, u32[]{:S(2)}) async-start(s16[16,48,768]{2,1,0:T(8,128)(2,1)} %copy-done.2), calls=%async_computation.1 | async-start | bytes 2359296 | tf_op jit(solution)/shard_map/all_to_all | solution.py:403
  77.5 3.0 %copy-start = (bf16[256,2048]{1,0:T(8,128)(2,1)S(1)}, bf16[256,2048]{1,0:T(8,128)(2,1)}, u32[]{:S(2)}) copy-start(bf16[256,2048]{1,0:T(8,128)(2,1)} %pts_ref.1) | copy-start | bytes 3145732
  78.6 4.6 %collective-permute-start = (bf16[512,1024]{1,0:T(8,128)(2,1)S(1)}, bf16[512,1024]{1,0:T(8,128)(2,1)S(1)}, u32[]{:S(2)}, u32[]{:S(2)}) collective-permute-start(bf16[512,1024]{1,0:T(8,128)(2,1)S(1)} %shard_map.52.own_ref), channel_id=1, source_target_pairs={{0,1},{1,0},{2,3},{3,2},{4,5},{5,4},{6,7},{7,6},{8,9},{9,8},{10,11... | collective-permute-start | bytes 3145736 | tf_op jit(solution)/shard_map/ppermute | solution.py:428
  95.4 4.7 %collective-permute-start.1 = (s16[768,768]{1,0:T(8,128)(2,1)S(1)}, s16[768,768]{1,0:T(8,128)(2,1)S(1)}, u32[]{:S(2)}, u32[]{:S(2)}) collective-permute-start(s16[768,768]{1,0:T(8,128)(2,1)S(1)} %bitcast.9), channel_id=1, source_target_pairs={{0,1},{1,0},{2,3},{3,2},{4,5},{5,4},{6,7},{7,6},{8,9},{9,8},{10,11... | collective-permute-start | bytes 3538952 | tf_op jit(solution)/shard_map/ppermute | solution.py:432
  97.6 2.5 %copy-start.1 = (f32[256,1000]{0,1:T(8,128)S(1)}, f32[256,1000]{0,1:T(8,128)}, u32[]{:S(2)}) copy-start(f32[256,1000]{0,1:T(8,128)} %param.4) | copy-start | bytes 3072004

commit v11 on v10

--- a/solution.py
+++ b/solution.py
@@ -28,7 +28,8 @@
 CLASS_STEP = 496
 CLASS_SPAN = 504
 SCALE_LANE = 511
-FRACTION = 2.0**22
+FRACTION = 500000.0
+CODED = 640
 MIB = 1024 * 1024
 
 
@@ -158,21 +159,23 @@
     top = jnp.max(jnp.abs(res), axis=1, keepdims=True)
     power = jnp.floor(jnp.log2(jnp.maximum(top, 1e-30))) + 1.0
     code = jnp.floor(res * (FRACTION / jnp.exp2(power)) + 0.5).astype(I32)
-    code = jnp.where(iota(res.shape, 1) == SCALE_LANE, power.astype(I32) * 256, code)
-    low = code & 255
-    half = res.shape[1] // 2
-    pair = (low[:, :half] | (low[:, half:] << 8)) - 32768
-    return jnp.concatenate([code >> 8, pair], axis=1).astype(jnp.int16)
+    code = jnp.where(iota(res.shape, 1) == SCALE_LANE, power.astype(I32) * 16, code)
+    low = code & 15
+    part = res.shape[1] // 4
+    word = low[:, :part]
+    for k in range(1, 4):
+        word = word | (low[:, k * part : (k + 1) * part] << (4 * k))
+    return jnp.concatenate([code >> 4, word - 32768], axis=1).astype(jnp.int16)
 
 
 def decode(words):
     words = words.astype(I32)
-    n = words.shape[1] * 2 // 3
+    n = words.shape[1] * 4 // 5
     high = words[:, :n]
-    pair = words[:, n:] + 32768
-    low = jnp.concatenate([pair & 255, pair >> 8], axis=1)
+    word = words[:, n:] + 32768
+    low = jnp.concatenate([(word >> (4 * k)) & 15 for k in range(4)], axis=1)
     unit = jnp.exp2(high[:, SCALE_LANE : SCALE_LANE + 1].astype(F32)) * (1.0 / FRACTION)
-    return (high * 256 + low).astype(F32) * unit
+    return (high * 16 + low).astype(F32) * unit
 
 
 def compact_body(tab_ref, in_ref, pts_ref, res_ref, *, rows, n_col):
@@ -205,7 +208,7 @@
         functools.partial(compact_body, rows=rows, n_col=n_col),
         out_shape=(
             jax.ShapeDtypeStruct((n_plane, COL_CAP, half), BF),
-            jax.ShapeDtypeStruct((n_plane, COL_CAP, CLASS_PAD * 3 // 4), jnp.int16),
+            jax.ShapeDtypeStruct((n_plane, COL_CAP, CODED), jnp.int16),
         ),
         in_specs=[vmem(), vmem()],
         out_specs=(vmem(), vmem()),
@@ -423,7 +426,7 @@
     col_rows = col_rows.reshape(n_col * CAP * SPLIT, col_rows.shape[2])
     pts_out, res_out = compact(tab, col_rows, rows, half, n_plane, n_col)
     all_pts = over_plane(pts_out).reshape(wide, half)
-    all_res = over_plane(res_out).reshape(wide, CLASS_PAD * 3 // 4)
+    all_res = over_plane(res_out).reshape(wide, CODED)
     own = order(tab, all_pts)
     other = lax.ppermute(own, "c", swap)
     cross, p_cross, psq, p_oth = first_half(points, own)

time: 103 us -> 105 us (1.019)
  starting transfers between devices: 12.1 us -> 14.4 us
  waiting for transfers between devices: 1.99 us -> 0.01 us
  Pallas kernels: 22.5 us -> 23.9 us
    ppermute x1, starting transfers between devices: 1.92 us -> 4.13 us  [on_device(): other = lax.ppermute(own, 'c', swap)]
    ppermute x1, waiting for transfers between devices: 1.56 us -> 0.01 us  [on_device(): other = lax.ppermute(own, 'c', swap)]
    pallas_call x1, Pallas kernels: 2.06 us -> 3.36 us  [update_own(): pl.pallas_call(update_own_body, out_shape=(out, out, jax.ShapeDtypeStruct...]
  transfers between devices with their start and end apart: 3 -> 3, of which waited for: 2 -> 0; matrix products, arithmetic and copies ran while one was open for 0% -> 0% of each run, Pallas kernels for 16% -> 16%
where the time goes in v11:
time: 105 us; the launch traced here: 104 us
  blocking collectives  64.5 us (61%)
  Pallas kernels  23.9 us (23%)
  starting transfers between devices  14.4 us (14%)
    all_to_all x1, blocking collectives, on_device(): col_rows = lax.all_to_all(packed, COLUMN, 0, 0, tiled=True)  38.8 us
    all_to_all x1, blocking collectives, over_plane(): lax.all_to_all(value, EVERY, 0, 0, axis_index_groups=plane_groups(), tile...  25.7 us
    pallas_call x1, Pallas kernels, inverse(): pl.pallas_call(functools.partial(inverse_body, share=share), out_shape=(o...  12.3 us
    all_to_all x1, starting transfers between devices, over_plane(): lax.all_to_all(value, EVERY, 0, 0, axis_index_groups=plane_groups(), tile...  7.67 us
    ppermute x1, starting transfers between devices, on_device(): other = lax.ppermute(own, 'c', swap)  4.13 us
    pallas_call x1, Pallas kernels, update_own(): pl.pallas_call(update_own_body, out_shape=(out, out, jax.ShapeDtypeStruct...  3.36 us
    pallas_call x1, Pallas kernels, pack(): pl.pallas_call(functools.partial(pack_body, n_plane=n_plane, n_col=n_col)...  2.9 us
    ppermute x1, starting transfers between devices, on_device(): other_res = lax.ppermute(all_res, 'c', swap)  2.6 us
  transfers between devices with their start and end apart: 3, of which 0 were waited for; matrix products, arithmetic and copies ran while one was open for 0% of the time, Pallas kernels for 16%

profile of v11, /device:TPU:1, one launch (start us, length us, event | category | flops | bytes accessed | tf_op | source)
XLA Modules:
  0.0 104.2 jit_solution(17313519631656616533)
XLA Ops:
  0.6 2.9 %shard_map.50 = (bf16[32,8,512]{2,1,0:T(8,128)(2,1)}, s32[8,512]{1,0:T(8,128)}) custom-call(s32[1,512]{1,0:T(1,128)} %bitcast.10, bf16[256,2048]{1,0:T(8,128)(2,1)} %pts_ref.1, f32[1000,256]{1,0:T(8,128)} %bitcast.7), custom_call_target="tpu_custom_call" | custom-call | tf_op jit(solution)/shard_map/pallas_call | solution.py:136
  3.5 38.8 %all_to_all.15 = bf16[32,8,512]{2,1,0:T(8,128)(2,1)S(1)} all-to-all(bf16[32,8,512]{2,1,0:T(8,128)(2,1)} %get-tuple-element.20), channel_id=1, replica_groups=mesh['y'=4,'x'=4,'zh'=2,'zl'=8,'c'=2] {'zh','zl','c'}, dimensions={0} | all-to-all | bytes 524288 | tf_op jit(solution)/shard_map/all_to_all | solution.py:425
  42.3 0.0 copy-start.3
  42.3 0.7 copy-done.3
  43.0 0.8 shard_map.51
  43.8 0.0 copy-start.2
  43.8 25.7 %all_to_all.16 = bf16[16,48,1024]{2,1,0:T(8,128)(2,1)S(1)} all-to-all(bf16[16,48,1024]{2,1,0:T(8,128)(2,1)S(1)} %get-tuple-element.22), channel_id=1, replica_groups={{0,32,64,96,128,160,192,224,256,288,320,352,384,416,448,480},{481,449,4..., dimensions={0} | all-to-all | bytes 3145728 | tf_op jit(solution)/shard_map/all_to_all | solution.py:406
  69.5 0.0 copy-done.2
  69.6 1.0 shard_map.52.own_ref
  70.6 0.0 copy-start
  70.6 4.1 %collective-permute-start = (bf16[512,1024]{1,0:T(8,128)(2,1)S(1)}, bf16[512,1024]{1,0:T(8,128)(2,1)S(1)}, u32[]{:S(2)}, u32[]{:S(2)}) collective-permute-start(bf16[512,1024]{1,0:T(8,128)(2,1)S(1)} %shard_map.52.own_ref), channel_id=1, source_target_pairs={{0,1},{1,0},{2,3},{3,2},{4,5},{5,4},{6,7},{7,6},{8,9},{9,8},{10,11... | collective-permute-start | bytes 3145736 | tf_op jit(solution)/shard_map/ppermute | solution.py:431
  74.7 0.0 copy-start.4
  74.7 7.7 %all-to-all-start.1 = ((s16[16,48,640]{2,1,0:T(8,128)(2,1)}), s16[16,48,640]{2,1,0:T(8,128)(2,1)}, u32[]{:S(2)}, u32[]{:S(2)}) async-start(s16[16,48,640]{2,1,0:T(8,128)(2,1)} %copy-done.2), calls=%async_computation.1 | async-start | bytes 1966080 | tf_op jit(solution)/shard_map/all_to_all | solution.py:406
  82.4 0.0 copy-done
  82.4 1.0 %shard_map.53 = (f32[512,512]{1,0:T(8,128)S(1)}, f32[256,512]{1,0:T(8,128)S(1)}, f32[256,1]{1,0:T(8,128)S(1)}, bf16[256,1024]{1,0:T(8,128)(2,1)S(1)}) custom-call(bf16[256,2048]{1,0:T(8,128)(2,1)S(1)} %copy-done, bf16[512,1024]{1,0:T(8,128)(2,1)S(1)} %shard_map.52.own_ref), custom_call_target="tpu_custom_call" | custom-call | flops 1000000 | bytes 1000000 | tf_op jit(solution)/shard_map/pallas_call | solution.py:254
  83.5 0.0 collective-permute-done.oth_ref
  83.5 0.0 copy-done.4
  83.5 12.3 %shard_map.54 = (bf16[288,512]{1,0:T(8,128)(2,1)S(1)}, bf16[288,512]{1,0:T(8,128)(2,1)S(1)}) custom-call(s32[8,512]{1,0:T(8,128)S(1)} %copy-done.4, bf16[256,1024]{1,0:T(8,128)(2,1)S(1)} %get-tuple-element.23.p_oth_ref, bf16[512,1024]{1,0:T(8,128)(2,1)S(1)} %collective-permute-done.oth_ref, f32[512,512]{1,0:T(8,128)S(1)} %get-tuple-element.24.cross_ref, ...), custom_call_target="tpu_custom_call" | custom-call | flops 1000000 | bytes 1000000 | tf_op jit(solution)/shard_map/pallas_call | solution.py:327
  95.7 0.0 all-to-all-done.1
  95.8 2.6 %collective-permute-start.1 = (s16[768,640]{1,0:T(8,128)(2,1)}, s16[768,640]{1,0:T(8,128)(2,1)S(1)}, u32[]{:S(2)}, u32[]{:S(2)}) collective-permute-start(s16[768,640]{1,0:T(8,128)(2,1)} %bitcast.3.res_ref), channel_id=1, source_target_pairs={{0,1},{1,0},{2,3},{3,2},{4,5},{5,4},{6,7},{7,6},{8,9},{9,8},{10,11... | collective-permute-start | bytes 2949128 | tf_op jit(solution)/shard_map/ppermute | solution.py:435
  98.4 0.0 copy-start.1
  98.4 3.4 %shard_map.55 = (bf16[288,768]{1,0:T(8,128)(2,1)S(1)}, bf16[288,768]{1,0:T(8,128)(2,1)S(1)}, f32[288,512]{1,0:T(8,128)S(1)}) custom-call(s32[8,512]{1,0:T(8,128)S(1)} %copy-done.4, bf16[288,512]{1,0:T(8,128)(2,1)S(1)} %get-tuple-element.28.wh_ref, bf16[288,512]{1,0:T(8,128)(2,1)S(1)} %get-tuple-element.29.wl_ref, s16[768,640]{1,0:T(8,128)(2,1)} %bitcast.3.res_ref), custom_call_target="tpu_custom_call" | custom-call | flops 2000000000 | bytes 4000000 | tf_op jit(solution)/shard_map/pallas_call | solution.py:363
  101.7 0.0 collective-permute-done.1.res_ref
  101.7 0.0 copy-done.1
  101.8 2.5 %shard_map.56 = (f32[1000,256]{1,0:T(8,128)}, f32[32,1000]{1,0:T(8,128)}) custom-call(bf16[288,768]{1,0:T(8,128)(2,1)S(1)} %get-tuple-element.31.hi_ref, bf16[288,768]{1,0:T(8,128)(2,1)S(1)} %get-tuple-element.32.lo_ref, s16[768,640]{1,0:T(8,128)(2,1)S(1)} %collective-permute-done.1.res_ref, f32[288,512]{1,0:T(8,128)S(1)} %get-tuple-element.33.ch_ref, ...), custom_call_target="tpu_custom_call" | custom-call | tf_op jit(solution)/shard_map/pallas_call | solution.py:388
Async XLA Ops:
  42.3 0.7 copy-start.3
  43.8 25.7 %copy-start.2 = (s16[16,48,640]{2,1,0:T(8,128)(2,1)}, s16[16,48,640]{2,1,0:T(8,128)(2,1)S(1)}, u32[]{:S(2)}) copy-start(s16[16,48,640]{2,1,0:T(8,128)(2,1)S(1)} %get-tuple-element.21) | copy-start | bytes 2949124
  70.6 11.8 %copy-start = (bf16[256,2048]{1,0:T(8,128)(2,1)S(1)}, bf16[256,2048]{1,0:T(8,128)(2,1)}, u32[]{:S(2)}) copy-start(bf16[256,2048]{1,0:T(8,128)(2,1)} %pts_ref.1) | copy-start | bytes 3145732
  70.6 12.9 %collective-permute-start = (bf16[512,1024]{1,0:T(8,128)(2,1)S(1)}, bf16[512,1024]{1,0:T(8,128)(2,1)S(1)}, u32[]{:S(2)}, u32[]{:S(2)}) collective-permute-start(bf16[512,1024]{1,0:T(8,128)(2,1)S(1)} %shard_map.52.own_ref), channel_id=1, source_target_pairs={{0,1},{1,0},{2,3},{3,2},{4,5},{5,4},{6,7},{7,6},{8,9},{9,8},{10,11... | collective-permute-start | bytes 3145736 | tf_op jit(solution)/shard_map/ppermute | solution.py:431
  74.7 8.7 %copy-start.4 = (s32[8,512]{1,0:T(8,128)S(1)}, s32[8,512]{1,0:T(8,128)}, u32[]{:S(2)}) copy-start(s32[8,512]{1,0:T(8,128)} %get-tuple-element.19.tab_ref) | copy-start | bytes 49156
  74.7 21.0 %all-to-all-start.1 = ((s16[16,48,640]{2,1,0:T(8,128)(2,1)}), s16[16,48,640]{2,1,0:T(8,128)(2,1)}, u32[]{:S(2)}, u32[]{:S(2)}) async-start(s16[16,48,640]{2,1,0:T(8,128)(2,1)} %copy-done.2), calls=%async_computation.1 | async-start | bytes 1966080 | tf_op jit(solution)/shard_map/all_to_all | solution.py:406
  95.8 6.0 %collective-permute-start.1 = (s16[768,640]{1,0:T(8,128)(2,1)}, s16[768,640]{1,0:T(8,128)(2,1)S(1)}, u32[]{:S(2)}, u32[]{:S(2)}) collective-permute-start(s16[768,640]{1,0:T(8,128)(2,1)} %bitcast.3.res_ref), channel_id=1, source_target_pairs={{0,1},{1,0},{2,3},{3,2},{4,5},{5,4},{6,7},{7,6},{8,9},{9,8},{10,11... | collective-permute-start | bytes 2949128 | tf_op jit(solution)/shard_map/ppermute | solution.py:435
  98.4 3.4 %copy-start.1 = (f32[256,1000]{0,1:T(8,128)S(1)}, f32[256,1000]{0,1:T(8,128)}, u32[]{:S(2)}) copy-start(f32[256,1000]{0,1:T(8,128)} %param.4) | copy-start | bytes 3072004
